TPU v7x, 32 devices: a whole 2x2x4 slice. The times are simulated.
32 devices in a mesh: dp: 8 (over y, x, core), tensor: 4 (over z).
Axes of the slice: x: 2, y: 2, z: 4, core: 2. Of those that a mesh axis runs over, the one named last changes fastest.
Arguments:
- in_streams: bfloat16 [4, 4096, 2048], P(None, ('dp', 'tensor')), may hold values from -6 to 6
- stored: bfloat16 [8, 4096, 2048], P(None, ('dp', 'tensor')), may hold values from -6 to 6
- cotangent: bfloat16 [4, 4096, 2048], P(None, ('dp', 'tensor')), may hold values from -8 to 8
- in_weights: float32 [2048, 14336], P('dp', 'tensor'), may hold values from -0.176776695 to 0.176776695
- in_moment: float32 [2048, 14336], P('dp', 'tensor'), may hold values from -9.387309e-05 to 9.387309e-05
- in_second: float32 [2048, 14336], P('dp', 'tensor'), may hold values from 1.0435448e-09 to 4.1741792e-09
- in_average: float32 [2048, 14336], P('dp', 'tensor'), may hold values from -0.125 to 0.125
- out_weights: float32 [2048, 10240], P('dp', 'tensor'), may hold values from -0.70710678 to 0.70710678
- out_moment: float32 [2048, 10240], P('dp', 'tensor'), may hold values from -9.387309e-05 to 9.387309e-05
- output_second_moment: float32 [2048, 10240], P('dp', 'tensor'), may hold values from 1.0435448e-09 to 4.1741792e-09
- out_average: float32 [2048, 10240], P('dp', 'tensor'), may hold values from -0.125 to 0.125
- small_params: float32 [50, 2048], replicated, may hold values from -2 to 2
- small_moment: float32 [50, 2048], replicated, may hold values from -0.001552825 to 0.001552825
- small_second: float32 [50, 2048], replicated, may hold values from 9.391903e-09 to 1.1421784e-06
- small_average: float32 [50, 2048], replicated, may hold values from -3 to 3
- mix_weights: float32 [37, 36], replicated, may hold values from -1 to 1
- mix_moment: float32 [37, 36], replicated, may hold values from -0.001552825 to 0.001552825
- mix_second: float32 [37, 36], replicated, may hold values from 2.855446e-07 to 1.1421783e-06
- mix_average: float32 [37, 36], replicated, may hold values from -1 to 1
Outputs:
- out_streams: bfloat16 [4, 4096, 2048], P(None, ('dp', 'tensor'))
- grad_streams: bfloat16 [4, 4096, 2048], P(None, ('dp', 'tensor'))
- grad_stored: bfloat16 [8, 4096, 2048], P(None, ('dp', 'tensor'))
- grad_norm: float32 [], replicated
- in_updated: float32 [2048, 14336], P('dp', 'tensor')
- in_moment_new: float32 [2048, 14336], P('dp', 'tensor')
- in_second_new: float32 [2048, 14336], P('dp', 'tensor')
- in_average_new: float32 [2048, 14336], P('dp', 'tensor')
- in_copy: bfloat16 [2048, 14336], P('dp', 'tensor')
- out_updated: float32 [2048, 10240], P('dp', 'tensor')
- out_moment_new: float32 [2048, 10240], P('dp', 'tensor')
- out_second_new: float32 [2048, 10240], P('dp', 'tensor')
- out_average_new: float32 [2048, 10240], P('dp', 'tensor')
- out_copy: bfloat16 [2048, 10240], P('dp', 'tensor')
- small_updated: float32 [50, 2048], replicated
- small_moment_new: float32 [50, 2048], replicated
- small_second_new: float32 [50, 2048], replicated
- small_average_new: float32 [50, 2048], replicated
- mix_updated: float32 [37, 36], replicated
- mix_moment_new: float32 [37, 36], replicated
- mix_second_new: float32 [37, 36], replicated
- mix_average_new: float32 [37, 36], replicated
All inputs are finite; a program needn't handle non-finite values.
Results may differ from a plain program's by a relative error of at most 0.024.
Values may be sent and summed in bfloat16 or wider, within the bound.
A program may use at most 320 MiB of HBM per device.

v0:
```python
import jax
import jax.numpy as jnp
from jax import lax
from jax.sharding import PartitionSpec as P

D = 2048
HEADS = 16
HD = 128
ROT = 32
FF = 8192
STREAMS = 4
LAYER = 8
STEP = 10
LAYERS = 9
MIXH = 36


norm_eps = 1e-05
mix_eps = 1e-06
beta_first = 0.9
beta_second = 0.95
adam_eps = 1e-08
decay_rate = 0.01
learn_rate = 0.03
small_rate = 0.2
clip_norm = 1.0
average_keep = 0.5
masked_score = -1e30
highest_precision = lax.Precision.HIGHEST
bfloat = jnp.bfloat16
single = jnp.float32


def rope_tables(length):
    half_rot = ROT // 2
    exponent = jnp.arange(half_rot, dtype=jnp.float32) * (2.0 / ROT)
    inverse = 1.0 / 10000.0**exponent
    angles = jnp.arange(length, dtype=jnp.float32)[:, None] * inverse[None, :]
    angles = jnp.concatenate([angles, angles], axis=1)
    return (jnp.cos(angles), jnp.sin(angles))


def rotate(values, cosine_table, sine_table):
    half_rot = ROT // 2
    leading = values[..., :ROT]
    turned = jnp.concatenate([-leading[..., half_rot:], leading[..., :half_rot]], axis=-1)
    leading = leading * cosine_table[:, None, :] + turned * sine_table[:, None, :]
    return jnp.concatenate([leading, values[..., ROT:]], axis=-1)


def rotate_back(gradients, cosine_table, sine_table):
    half_rot = ROT // 2
    leading = gradients[..., :ROT]
    spun_part = leading * sine_table[:, None, :]
    turned = jnp.concatenate([spun_part[..., half_rot:], -spun_part[..., :half_rot]], axis=-1)
    leading = leading * cosine_table[:, None, :] + turned
    return jnp.concatenate([leading, gradients[..., ROT:]], axis=-1)


def gelu_value(values):
    return jax.nn.gelu(values, approximate=False)


def gelu_slope(values):
    normal_cdf = 0.5 * (1.0 + lax.erf(values * 0.7071067811865476))
    return normal_cdf + values * jnp.exp(-0.5 * values * values) * 0.3989422804014327


def contract_last(left_side, right_side):
    return lax.dot_general(
        left_side,
        right_side,
        (((left_side.ndim - 1,), (right_side.ndim - 1,)), ((), ())),
        preferred_element_type=single,
    )


def contract_first(left_side, right_side):
    return lax.dot_general(
        left_side, right_side, (((0,), (0,)), ((), ())), preferred_element_type=single
    )


def causal_mask(first_row, block_rows, length):
    places = first_row + jnp.arange(block_rows, dtype=jnp.int32)
    return jnp.arange(length, dtype=jnp.int32)[None, :] <= places[:, None]


def adamw_step(weight, moment, second, average, gradient, factor, rate):
    clipped = gradient * factor
    moment = beta_first * moment + (1.0 - beta_first) * clipped
    second = beta_second * second + (1.0 - beta_second) * clipped * clipped
    step_ratio = (
        moment
        / (1.0 - beta_first**STEP)
        / (jnp.sqrt(second / (1.0 - beta_second**STEP)) + adam_eps)
    )
    weight = weight - rate * (step_ratio + decay_rate * weight)
    average = average_keep * average + (1.0 - average_keep) * weight
    return (weight, moment, second, average)


def shards(
    in_streams,
    stored,
    cotangent,
    in_weights,
    in_moment,
    in_second,
    in_average,
    out_weights,
    out_moment,
    output_second_moment,
    out_average,
    small_params,
    small_moment,
    small_second,
    small_average,
    mix_weights,
    mix_moment,
    mix_second,
    mix_average,
):
    groups = lax.axis_size("tensor")
    group_index = lax.axis_index("tensor")
    heads_group = HEADS // groups
    units_group = FF // groups
    attn_width = heads_group * 3 * HD
    proj_width = heads_group * HD
    own_rows = in_streams.shape[1]
    length = own_rows * groups
    up_rows = FF // D
    block_rows = min(512, length)
    block_count = length // block_rows
    score_scale = HD ** (-0.5)
    shard_rows = D // lax.axis_size("dp")
    full_in, full_out = (
        lax.all_gather(in_weights.astype(bfloat), "dp", axis=0, tiled=True),
        lax.all_gather(out_weights.astype(bfloat), "dp", axis=0, tiled=True),
    )
    gain_mix = small_params[4]
    bias_heads = lax.dynamic_slice_in_dim(
        small_params[5:8].reshape(3, HEADS, HD), group_index * heads_group, heads_group, 1
    )
    bias_units = lax.dynamic_slice_in_dim(
        small_params[10 : 10 + up_rows].reshape(FF), group_index * units_group, units_group, 0
    )
    mix_low = small_params[10 + up_rows :].astype(bfloat)
    flow_rows = in_streams.astype(single)
    centred = flow_rows - jnp.mean(flow_rows, axis=-1, keepdims=True)
    inverse = lax.rsqrt(jnp.mean(centred * centred, axis=-1, keepdims=True) + norm_eps)
    unit_flows = centred * inverse
    gain_all = jnp.stack([small_params[0], small_params[0], small_params[0], small_params[2]])[
        :, None, :
    ]
    shift_all = jnp.stack([small_params[1], small_params[1], small_params[1], small_params[3]])[
        :, None, :
    ]
    normed_own = (unit_flows * gain_all + shift_all).astype(bfloat)
    normed = lax.all_gather(normed_own, "tensor", axis=1, tiled=True)
    attn_weights = full_in[:, :attn_width].reshape(D, heads_group, 3, HD)
    up_weights = full_in[:, attn_width:]
    cosine_table, sine_table = rope_tables(length)

    def project(part_index):
        return (
            jnp.einsum(
                "ld,dhe->lhe",
                normed[part_index],
                attn_weights[:, :, part_index, :],
                preferred_element_type=single,
            )
            + bias_heads[part_index][None]
        )

    queries = rotate(project(0), cosine_table, sine_table).astype(bfloat)
    key_heads = rotate(project(1), cosine_table, sine_table).astype(bfloat)
    value_heads = project(2).astype(bfloat)
    up_pre = jnp.dot(normed[3], up_weights, preferred_element_type=single) + bias_units
    hidden = gelu_value(up_pre).astype(bfloat)

    def forward_block(block_index):
        first_row = block_index * block_rows
        scores = (
            jnp.einsum("qhe,khe->hqk", queries, key_heads, preferred_element_type=single)
            * score_scale
        )
        scores = jnp.where(causal_mask(first_row, block_rows, length)[None], scores, masked_score)
        row_top = jnp.max(scores, axis=-1, keepdims=True)
        raised = jnp.exp(scores - row_top)
        row_sum = jnp.sum(raised, axis=-1, keepdims=True)
        weights_low = (raised / row_sum).astype(bfloat)
        mixed_heads = jnp.einsum(
            "hqk,khe->qhe", weights_low, value_heads, preferred_element_type=single
        )
        return (mixed_heads, (row_top + jnp.log(row_sum))[..., 0])

    attended, log_sums = lax.map(forward_block, jnp.arange(block_count, dtype=jnp.int32))
    attended = attended.reshape(length, heads_group, HD).astype(bfloat)
    joined = jnp.concatenate([attended.reshape(length, proj_width), hidden], axis=1)
    partial_value = contract_last(joined, full_out)
    summed = lax.psum(partial_value.astype(jnp.bfloat16), "tensor").astype(jnp.float32)
    branch = lax.dynamic_slice_in_dim(summed, group_index * own_rows, own_rows, 0)
    newest = flow_rows[3] + branch + small_params[8] + small_params[9]
    inv_rms = lax.rsqrt(jnp.mean(newest * newest, axis=-1, keepdims=True) + mix_eps)
    mix_normed = (newest * inv_rms * gain_mix).astype(bfloat)
    mix_pre = contract_last(mix_normed, mix_low)
    mixing_activation = gelu_value(mix_pre)
    mixing_weights = (
        jnp.dot(mixing_activation, mix_weights[:MIXH], precision=highest_precision)
        + mix_weights[MIXH]
    )
    mixing_weights = mixing_weights.reshape(own_rows, STREAMS, LAYERS)
    composed = mixing_weights[:, :, LAYER].T[:, :, None] * newest[None]
    for layer_index in range(LAYER):
        composed = (
            composed
            + mixing_weights[:, :, layer_index].T[:, :, None]
            * stored[layer_index].astype(single)[None]
        )
    out_streams = composed.astype(bfloat)
    back_flows = cotangent.astype(single)
    d_stored = jnp.einsum("srd,jrd->rsj", cotangent, stored, preferred_element_type=single)
    d_newest_col = jnp.einsum("srd,rd->rs", back_flows, newest, precision=highest_precision)
    d_mixing = jnp.concatenate([d_stored, d_newest_col[:, :, None]], axis=2).reshape(own_rows, MIXH)
    spread_gradient = jnp.einsum(
        "rsj,srd->jrd", mixing_weights, back_flows, precision=highest_precision
    )
    grad_stored = spread_gradient[:LAYER].astype(bfloat)
    d_act = jnp.dot(d_mixing, mix_weights[:MIXH].T, precision=highest_precision)
    grad_mix_out = jnp.dot(mixing_activation.T, d_mixing, precision=highest_precision)
    grad_mix_bias = jnp.sum(d_mixing, axis=0)
    d_mix_pre = (d_act * gelu_slope(mix_pre)).astype(bfloat)
    grad_mix_in = contract_first(d_mix_pre, mix_normed)
    d_mix_normed = jnp.dot(d_mix_pre, mix_low, preferred_element_type=single)
    scaled_back = d_mix_normed * gain_mix
    grad_gain_mix = jnp.sum(d_mix_normed * newest * inv_rms, axis=0)
    d_newest = (
        spread_gradient[LAYER]
        + inv_rms * scaled_back
        - newest * inv_rms**3 * jnp.mean(scaled_back * newest, axis=-1, keepdims=True)
    )
    grad_bias_out = jnp.sum(d_newest, axis=0)
    branch_grads = lax.all_gather(d_newest.astype(bfloat), "tensor", axis=0, tiled=True)
    d_joined = jnp.dot(branch_grads, full_out, preferred_element_type=single)
    d_attended = d_joined[:, :proj_width].reshape(length, heads_group, HD).astype(bfloat)
    d_up = (d_joined[:, proj_width:] * gelu_slope(up_pre)).astype(bfloat)

    def backward_block(carried, block_index):
        key_sum, value_sum = carried
        first_row = block_index * block_rows
        scores = (
            jnp.einsum("qhe,khe->hqk", queries, key_heads, preferred_element_type=single)
            * score_scale
        )
        scores = jnp.where(causal_mask(first_row, block_rows, length)[None], scores, masked_score)
        chances = jnp.exp(scores - log_sums[block_index][..., None])
        chances_low = chances.astype(bfloat)
        d_chances = jnp.einsum(
            "qhe,khe->hqk", d_attended, value_heads, preferred_element_type=single
        )
        centre = jnp.sum(d_chances * chances, axis=-1, keepdims=True)
        d_scores = (chances * (d_chances - centre)).astype(bfloat)
        d_picked = (
            jnp.einsum("hqk,khe->qhe", d_scores, key_heads, preferred_element_type=single)
            * score_scale
        )
        key_sum = (
            key_sum
            + jnp.einsum("hqk,qhe->khe", d_scores, queries, preferred_element_type=single)
            * score_scale
        )
        value_sum = value_sum + jnp.einsum(
            "hqk,qhe->khe", chances_low, d_attended, preferred_element_type=single
        )
        return ((key_sum, value_sum), d_picked)

    zero_heads = jnp.zeros((length, heads_group, HD), single)
    (d_key_heads, value_head_gradient), d_queries = lax.scan(
        backward_block, (zero_heads, zero_heads), jnp.arange(block_count, dtype=jnp.int32)
    )
    d_queries = d_queries.reshape(length, heads_group, HD)
    d_pre_q = rotate_back(d_queries, cosine_table, sine_table).astype(bfloat)
    d_pre_k = rotate_back(d_key_heads, cosine_table, sine_table).astype(bfloat)
    d_pre_v = value_head_gradient.astype(bfloat)
    d_pres = jnp.stack([d_pre_q, d_pre_k, d_pre_v], axis=2)
    bias_grads = jnp.sum(d_pres, axis=0, dtype=single)
    unit_grads = jnp.sum(d_up, axis=0, dtype=single)
    d_norm_parts = [
        jnp.einsum(
            "lhe,dhe->ld",
            d_pres[:, :, part_index],
            attn_weights[:, :, part_index, :],
            preferred_element_type=single,
        )
        for part_index in range(3)
    ]
    d_norm_parts.append(contract_last(d_up, up_weights))
    d_normed = jnp.stack(d_norm_parts)
    d_sum = lax.psum(d_normed.astype(jnp.bfloat16), "tensor").astype(jnp.float32)
    d_own = lax.dynamic_slice_in_dim(d_sum, group_index * own_rows, own_rows, 1)
    d_unit = d_own * gain_all
    d_flows = inverse * (
        d_unit
        - jnp.mean(d_unit, axis=-1, keepdims=True)
        - unit_flows * jnp.mean(d_unit * unit_flows, axis=-1, keepdims=True)
    )
    grad_streams = jnp.concatenate([d_flows[:3], (d_flows[3] + d_newest)[None]], axis=0).astype(
        bfloat
    )
    gain_grads = jnp.sum(d_own * unit_flows, axis=1)
    shift_grads = jnp.sum(d_own, axis=1)
    head_rows = lax.dynamic_update_slice_in_dim(
        jnp.zeros((HEADS, 3, HD), single), bias_grads, group_index * heads_group, 0
    )
    head_rows = jnp.transpose(head_rows, (1, 0, 2)).reshape(3, D)
    unit_full = lax.dynamic_update_slice_in_dim(
        jnp.zeros((FF,), single), unit_grads, group_index * units_group, 0
    )
    small_grad = jnp.concatenate(
        [
            jnp.stack(
                [
                    gain_grads[0] + gain_grads[1] + gain_grads[2],
                    shift_grads[0] + shift_grads[1] + shift_grads[2],
                    gain_grads[3],
                    shift_grads[3],
                    grad_gain_mix,
                ]
            ),
            head_rows,
            jnp.stack([grad_bias_out, grad_bias_out]),
            unit_full.reshape(up_rows, D),
            grad_mix_in,
        ],
        axis=0,
    )
    mix_grad = jnp.concatenate([grad_mix_out, grad_mix_bias[None]], axis=0)
    small_parameter_total, mix_total = lax.psum((small_grad, mix_grad), ("dp", "tensor"))
    attn_part = jnp.einsum(
        "pld,lhpe->dhpe", normed[:3], d_pres, preferred_element_type=single
    ).reshape(lax.axis_size("dp") * shard_rows, attn_width)
    up_part = contract_first(normed[3], d_up)
    weight_grads = lax.psum_scatter(
        jnp.concatenate(
            [jnp.concatenate([attn_part, up_part], axis=1), contract_first(branch_grads, joined)],
            axis=1,
        ).astype(jnp.bfloat16),
        "dp",
        scatter_dimension=0,
        tiled=True,
    ).astype(jnp.float32)
    grad_in = weight_grads[:, : attn_width + units_group]
    grad_out = weight_grads[:, attn_width + units_group :]
    big_square = jnp.sum(grad_in * grad_in) + jnp.sum(grad_out * grad_out)
    big_total = lax.psum(big_square, ("dp", "tensor"))
    grad_norm = jnp.sqrt(
        big_total
        + jnp.sum(small_parameter_total * small_parameter_total)
        + jnp.sum(mix_total * mix_total)
    )
    factor = clip_norm / jnp.maximum(grad_norm, clip_norm)
    in_new = adamw_step(in_weights, in_moment, in_second, in_average, grad_in, factor, learn_rate)
    out_new = adamw_step(
        out_weights, out_moment, output_second_moment, out_average, grad_out, factor, learn_rate
    )
    small_new = adamw_step(
        small_params,
        small_moment,
        small_second,
        small_average,
        small_parameter_total,
        factor,
        small_rate,
    )
    mix_new = adamw_step(
        mix_weights, mix_moment, mix_second, mix_average, mix_total, factor, small_rate
    )
    return (
        out_streams,
        grad_streams,
        grad_stored,
        grad_norm,
        in_new[0],
        in_new[1],
        in_new[2],
        in_new[3],
        in_new[0].astype(bfloat),
        out_new[0],
        out_new[1],
        out_new[2],
        out_new[3],
        out_new[0].astype(bfloat),
        small_new[0],
        small_new[1],
        small_new[2],
        small_new[3],
        mix_new[0],
        mix_new[1],
        mix_new[2],
        mix_new[3],
    )


def solution(mesh):
    in_specs = (
        P(None, ("dp", "tensor"), None),
        P(None, ("dp", "tensor"), None),
        P(None, ("dp", "tensor"), None),
        P("dp", "tensor"),
        P("dp", "tensor"),
        P("dp", "tensor"),
        P("dp", "tensor"),
        P("dp", "tensor"),
        P("dp", "tensor"),
        P("dp", "tensor"),
        P("dp", "tensor"),
        P(),
        P(),
        P(),
        P(),
        P(),
        P(),
        P(),
        P(),
    )
    out_specs = (
        P(None, ("dp", "tensor"), None),
        P(None, ("dp", "tensor"), None),
        P(None, ("dp", "tensor"), None),
        P(),
        P("dp", "tensor"),
        P("dp", "tensor"),
        P("dp", "tensor"),
        P("dp", "tensor"),
        P("dp", "tensor"),
        P("dp", "tensor"),
        P("dp", "tensor"),
        P("dp", "tensor"),
        P("dp", "tensor"),
        P("dp", "tensor"),
        P(),
        P(),
        P(),
        P(),
        P(),
        P(),
        P(),
        P(),
    )
    return jax.shard_map(shards, mesh=mesh, in_specs=in_specs, out_specs=out_specs, check_vma=False)
```

profile of v0, /device:TPU:0, one launch (start us, length us, event | category | flops | bytes accessed | tf_op | source)
XLA Modules:
  0.0 1219.2 jit_solution(5732050449572549305)
XLA Ops:
  24.0 74.4 %all-gather.7.cloned.1.call-done = bf16[2048,3584]{0,1:T(8,128)(2,1)} async-done(((bf16[256,3584]{0,1:T(8,128)(2,1)}), bf16[2048,3584]{0,1:T(8,128)(2,1)}) %all-gather.7.cloned.1.call-update) | async-done | bytes 14680080 | tf_op jit(solution)/shard_map/all_gather | solution.py:138
  106.7 143.5 %all-gather.5.cloned.1.call-done = bf16[4,512,2048]{2,1,0:T(8,128)(2,1)} async-done(((bf16[4,128,2048]{2,1,0:T(8,128)(2,1)}), bf16[4,512,2048]{2,1,0:T(8,128)(2,1)}) %all-gather.5.cloned.1.call-update) | async-done | bytes 8388624 | tf_op jit(solution)/shard_map/all_gather | solution.py:160
  264.9 17.2 %fusion.13 = (bf16[512,2048]{1,0:T(8,128)(2,1)}, f32[512,2048]{1,0:T(8,128)}) fusion(f32[2048]{0:T(1024)} %dynamic_slice.20, bf16[2048,3584]{0,1:T(8,128)(2,1)} %all-gather.7.cloned.1.call-done, bf16[4,512,2048]{2,1,0:T(8,128)(2,1)} %all-gather.5.cloned.1.call-done), kind=kOutput, calls=%fused_computation.27 | convolution fusion | flops 4364173312 | bytes 16785408 | tf_op jit(solution)/shard_map/dot_general | solution.py:179
  282.2 32.0 %all-gather.9.cloned.1.call-done = bf16[2048,2560]{1,0:T(8,128)(2,1)} async-done(((bf16[256,2560]{1,0:T(8,128)(2,1)}), bf16[2048,2560]{1,0:T(8,128)(2,1)}) %all-gather.9.cloned.1.call-update) | async-done | bytes 10485776 | tf_op jit(solution)/shard_map/all_gather | solution.py:139
  314.2 10.0 convolution_convert_fusion.2
  328.0 7.9 fusion.21
  335.9 75.0 %all-reduce.5.cloned.1.call-done = bf16[512,2048]{1,0:T(8,128)(2,1)} async-done(((bf16[512,2048]{1,0:T(8,128)(2,1)}), bf16[512,2048]{1,0:T(8,128)(2,1)}) %all-reduce.5.cloned.1.call-update) | async-done | bytes 2097168 | tf_op jit(solution)/shard_map/psum | solution.py:202
  419.9 11.5 fusion.63
  431.4 14.9 %copy.217 = f32[128,9,2048]{2,0,1:T(8,128)} copy(f32[128,9,2048]{2,1,0:T(8,128)} %fusion.63) | data formatting | bytes 18874368 | tf_op jit(solution)/shard_map/rsj,srd->jrd/dot_general | solution.py:226
  446.3 10.4 convolution_bitcast_fusion
  469.1 44.3 %all-gather.11.cloned.1.call-done = bf16[512,2048]{1,0:T(8,128)(2,1)} async-done(((bf16[128,2048]{1,0:T(8,128)(2,1)}), bf16[512,2048]{1,0:T(8,128)(2,1)}) %all-gather.11.cloned.1.call-update) | async-done | bytes 2097168 | tf_op jit(solution)/shard_map/all_gather | solution.py:244
  513.4 8.9 fusion.136
  558.3 7.4 convert_bitcast_fusion
  568.9 8.7 copy.177
  577.6 10.1 convolution_convert_fusion.1
  587.7 12.3 %copy.178 = bf16[2048,2048]{1,0:T(8,128)(2,1)} copy(bf16[2048,2048]{0,1:T(8,128)(2,1)} %convolution_convert_fusion.1) | data formatting | bytes 16777216 | tf_op jit(solution)/shard_map/convert.9
  600.0 10.2 convolution_convert_fusion
  610.2 17.8 %pad_maximum_fusion = bf16[2048,6144]{1,0:T(8,128)(2,1)} fusion(bf16[2048,2560]{1,0:T(8,128)(2,1)} %convolution_convert_fusion, bf16[2048,2048]{1,0:T(8,128)(2,1)} %copy.178, bf16[2048,1536]{1,0:T(8,128)(2,1)} %copy.177), kind=kLoop, calls=%fused_computation | loop fusion | flops 75497472 | bytes 50331648 | tf_op jit(solution)/shard_map/concatenate | solution.py:345
  645.6 7.0 add_convert_fusion
  653.3 192.2 %all-reduce.7.cloned.1.call-done = bf16[4,512,2048]{2,1,0:T(8,128)(2,1)} async-done(((bf16[4,512,2048]{2,1,0:T(8,128)(2,1)}), bf16[4,512,2048]{2,1,0:T(8,128)(2,1)}) %all-reduce.7.cloned.1.call-update) | async-done | bytes 8388624 | tf_op jit(solution)/shard_map/psum | solution.py:300
  863.6 141.9 %reduce-scatter.2.cloned.1.call-done = bf16[256,6144]{1,0:T(8,128)(2,1)} async-done(((bf16[2048,6144]{1,0:T(8,128)(2,1)}), bf16[256,6144]{1,0:T(8,128)(2,1)}) %reduce-scatter.2.cloned.1.call-update) | async-done | bytes 3145744 | tf_op jit(solution)/shard_map/reduce_scatter | solution.py:344
  1013.4 124.9 %all-reduce.9.cloned.1.call-done = f32[50,2048]{1,0:T(8,128)} async-done(((f32[50,2048]{1,0:T(8,128)}), f32[50,2048]{1,0:T(8,128)}) %all-reduce.9.cloned.1.call-update) | async-done | bytes 409616 | tf_op jit(solution)/shard_map/psum | solution.py:339
  1140.0 41.4 %all-reduce = (f32[]{:T(128)}, f32[37,36]{1,0:T(8,128)S(1)}) all-reduce(f32[]{:T(128)S(6)} %add.361, f32[37,36]{1,0:T(8,128)S(1)} %copy-done.55), channel_id=1, replica_groups=mesh['dp'=8,'tensor'=4] {'dp','tensor'}, use_global_device_ids=true, to_apply=%region_14.15 | all-reduce | flops 1333 | bytes 10664 | tf_op jit(solution)/shard_map/psum | solution.py:356
  1184.1 7.0 fusion.119
  (296 shorter events, 168.3 us)
Async XLA Ops:
  7.2 91.2 %all-gather.7.cloned.1.call-start = ((), (), s32[]{:S(2)}) async-start(), calls=%async_computation.2 | async-start | bytes 16515072 | tf_op jit(solution)/shard_map/all_gather | solution.py:138
  11.7 238.5 %all-gather.5.cloned.1.call-start = ((), (), s32[]{:S(2)}) async-start(), calls=%async_computation.1 | async-start | bytes 10485760 | tf_op jit(solution)/shard_map/all_gather | solution.py:160
  18.3 295.9 %all-gather.9.cloned.1.call-start = ((), (), s32[]{:S(2)}) async-start(), calls=%async_computation.3 | async-start | bytes 11796480 | tf_op jit(solution)/shard_map/all_gather | solution.py:139
  21.3 389.5 %all-reduce.5.cloned.1.call-start = ((), (), s32[]{:S(2)}) async-start(), calls=%async_computation.4 | async-start | bytes 4194304 | tf_op jit(solution)/shard_map/psum | solution.py:202
  23.9 233.3 %copy-start.33 = (f32[512,32]{0,1:T(8,128)}, f32[512,32]{0,1:T(8,128)S(1)}, u32[]{:S(2)}) copy-start(f32[512,32]{0,1:T(8,128)S(1)} %get-tuple-element.144) | copy-start | bytes 196612
  23.9 233.3 %copy-start.35 = (f32[512,32]{0,1:T(8,128)}, f32[512,32]{0,1:T(8,128)S(1)}, u32[]{:S(2)}) copy-start(f32[512,32]{0,1:T(8,128)S(1)} %get-tuple-element.143) | copy-start | bytes 196612
  264.9 49.3 %copy-start.40 = (bf16[512,512]{1,0:T(8,128)(2,1)}, bf16[512,512]{1,0:T(8,128)(2,1)S(1)}, u32[]{:S(2)}) copy-start(bf16[512,512]{1,0:T(8,128)(2,1)S(1)} %copy.158) | copy-start | bytes 1572868
  324.2 189.2 %all-gather.11.cloned.1.call-start = ((), (), s32[]{:S(2)}) async-start(), calls=%async_computation.5 | async-start | bytes 2621440 | tf_op jit(solution)/shard_map/all_gather | solution.py:244
  446.3 10.4 copy-start.52
  468.4 377.2 %all-reduce.7.cloned.1.call-start = ((), (), s32[]{:S(2)}) async-start(), calls=%async_computation.6 | async-start | bytes 16777216 | tf_op jit(solution)/shard_map/psum | solution.py:300
  533.1 9.2 copy-start.12
  534.0 8.3 copy-start.13
  555.8 449.7 %reduce-scatter.2.cloned.1.call-start = ((), (), s32[]{:S(2)}) async-start(), calls=%async_computation.7 | async-start | bytes 28311552 | tf_op jit(solution)/shard_map/reduce_scatter | solution.py:344
  558.3 7.4 copy-start.30
  628.1 510.2 %all-reduce.9.cloned.1.call-start = ((), (), s32[]{:S(2)}) async-start(), calls=%async_computation.8 | async-start | bytes 917504 | tf_op jit(solution)/shard_map/psum | solution.py:339
  633.7 9.9 copy-start.54
  645.6 200.0 %copy-start.60 = (f32[4,128]{1,0:T(4,128)S(1)}, f32[4,128]{1,0:T(4,128)}, u32[]{:S(2)}) copy-start(f32[4,128]{1,0:T(4,128)} %copy-done.59) | copy-start | bytes 6148
  645.6 200.0 %copy-start.62 = (f32[4,128]{1,0:T(4,128)S(1)}, f32[4,128]{1,0:T(4,128)}, u32[]{:S(2)}) copy-start(f32[4,128]{1,0:T(4,128)} %copy-done.61) | copy-start | bytes 6148
  652.6 196.6 %copy-start.38 = (f32[4,2048]{1,0:T(4,128)S(1)}, f32[4,2048]{1,0:T(4,128)}, u32[]{:S(2)}) copy-start(f32[4,2048]{1,0:T(4,128)} %copy-done.37) | copy-start | bytes 98308
  1008.2 131.8 %copy-start.55 = (f32[37,36]{1,0:T(8,128)S(1)}, f32[37,36]{1,0:T(8,128)}, u32[]{:S(2)}) copy-start(f32[37,36]{1,0:T(8,128)} %pad_maximum_fusion.17) | copy-start | bytes 15988
  1184.1 8.9 copy-start.6
  1184.1 11.1 copy-start.17
  1184.1 12.2 copy-start.18
  1191.1 11.8 copy-start.9
  (68 other events, 267.1 us)
Sparse Core Ops, SparseCore 0:
  11.9 86.5 all-gather.6
  100.6 149.6 all-gather.4
  252.7 61.4 all-gather.8
  324.3 86.4 all-reduce.4
  468.5 44.8 all-gather.10
  556.0 289.5 all-reduce.6
  849.6 155.8 reduce-scatter.1
  1012.3 125.9 all-reduce.8
where the time goes:
time: 1230 us; the launch traced here: 1220 us
  waiting for transfers between devices  828 us (67%)
  matrix products  129 us (10%)
  local copies, waits for them, and re-layouts  100 us (8%)
  other arithmetic  99.8 us (8%)
  blocking collectives  41.4 us (3%)
  between operations  20 us (2%)
    psum x1, waiting for transfers between devices, shards(): lax.psum(d_normed.astype(jnp.bfloat16), 'tensor').astype(jnp.float32)  192 us
    all_gather x1, waiting for transfers between devices, shards(): normed = lax.all_gather(normed_own, 'tensor', axis=1, tiled=True)  144 us
    reduce_scatter x1, waiting for transfers between devices, shards(): lax.psum_scatter(jnp.concatenate([jnp.concatenate([attn_part, up_part], a...  142 us
    psum x1, waiting for transfers between devices, shards(): lax.psum((small_grad, mix_grad), ('dp', 'tensor'))  125 us
    psum x1, waiting for transfers between devices, shards(): lax.psum(partial_value.astype(jnp.bfloat16), 'tensor').astype(jnp.float32)  75 us
    all_gather x1, waiting for transfers between devices, shards(): lax.all_gather(in_weights.astype(bfloat), 'dp', axis=0, tiled=True)  74.4 us
    all_gather x1, waiting for transfers between devices, shards(): lax.all_gather(d_newest.astype(bfloat), 'tensor', axis=0, tiled=True)  44.3 us
    psum x1, blocking collectives, shards(): big_total = lax.psum(big_square, ('dp', 'tensor'))  41.4 us
  transfers between devices with their start and end apart: 8, of which 8 were waited for; matrix products, arithmetic and copies ran while one was open for 15% of the time, Pallas kernels for 0%

commit v1 on v0

--- a/solution.py
+++ b/solution.py
@@ -1,6 +1,8 @@
 import jax
 import jax.numpy as jnp
 from jax import lax
+from jax.experimental import pallas as pl
+from jax.experimental.pallas import tpu as pltpu
 from jax.sharding import PartitionSpec as P
 
 D = 2048
@@ -29,6 +31,7 @@
 highest_precision = lax.Precision.HIGHEST
 bfloat = jnp.bfloat16
 single = jnp.float32
+MESH = pl.DeviceIdType.MESH
 
 
 def rope_tables(length):
@@ -98,6 +101,288 @@
     weight = weight - rate * (step_ratio + decay_rate * weight)
     average = average_keep * average + (1.0 - average_keep) * weight
     return (weight, moment, second, average)
+
+
+def enter(partners):
+    barrier = pltpu.get_barrier_semaphore()
+    for present, device in partners:
+
+        @pl.when(present)
+        def _():
+            pl.semaphore_signal(barrier, inc=1, device_id=device, device_id_type=MESH)
+
+    pl.semaphore_wait(barrier, sum(present.astype(jnp.int32) for present, _ in partners))
+
+
+def row_chunks(streams, rows, cut):
+    return [(s, r, rows // cut) for s in range(streams) for r in range(0, rows, rows // cut)]
+
+
+def line_gather_kernel(size, chunks, own, out, send_sem, recv_sem, local_sem):
+    here = lax.axis_index("tensor")
+    sides = ((0, 1), (1, -1))
+    enter([(here < size - 1, {"tensor": here + 1}), (here > 0, {"tensor": here - 1})])
+
+    def onward(side, way, step, place):
+        s, r, n = chunks[place]
+        origin = here - way * step
+        target = out.at[s, origin, pl.ds(r, n)]
+        return pltpu.make_async_remote_copy(
+            src_ref=own.at[s, pl.ds(r, n)] if step == 0 else target,
+            dst_ref=target,
+            send_sem=send_sem.at[side, step, place],
+            recv_sem=recv_sem.at[side, step, place],
+            device_id={"tensor": here + way},
+            device_id_type=MESH,
+        )
+
+    def has_next(way):
+        return here < size - 1 if way > 0 else here > 0
+
+    def has_origin(way, step):
+        return here >= step if way > 0 else here < size - step
+
+    for place in range(len(chunks)):
+        for side, way in sides:
+            pl.when(has_next(way))(onward(side, way, 0, place).start)
+    local = pltpu.make_async_copy(own, out.at[:, here], local_sem)
+    local.start()
+    for step in range(1, size):
+        for place in range(len(chunks)):
+            for side, way in sides:
+
+                @pl.when(has_origin(way, step))
+                def _():
+                    s, r, n = chunks[place]
+                    landed = out.at[s, here - way * step, pl.ds(r, n)]
+                    pltpu.make_async_remote_copy(
+                        src_ref=landed,
+                        dst_ref=landed,
+                        send_sem=send_sem.at[side, step - 1, place],
+                        recv_sem=recv_sem.at[side, step - 1, place],
+                        device_id={"tensor": here - way},
+                        device_id_type=MESH,
+                    ).wait_recv()
+                    pl.when(has_next(way))(onward(side, way, step, place).start)
+
+    for step in range(size):
+        for place in range(len(chunks)):
+            for side, way in sides:
+
+                @pl.when(jnp.logical_and(has_next(way), has_origin(way, step)))
+                def _():
+                    onward(side, way, step, place).wait_send()
+
+    local.wait()
+
+
+def line_gather(own, size, cut, identity):
+    streams, rows, width = own.shape
+    chunks = row_chunks(streams, rows, cut)
+    return pl.pallas_call(
+        lambda *refs: line_gather_kernel(size, chunks, *refs),
+        out_shape=jax.ShapeDtypeStruct((streams, size, rows, width), own.dtype),
+        in_specs=[pl.BlockSpec(memory_space=pl.ANY)],
+        out_specs=pl.BlockSpec(memory_space=pl.ANY),
+        scratch_shapes=[
+            pltpu.SemaphoreType.DMA((2, size, len(chunks))),
+            pltpu.SemaphoreType.DMA((2, size, len(chunks))),
+            pltpu.SemaphoreType.DMA,
+        ],
+        compiler_params=pltpu.CompilerParams(collective_id=identity, has_side_effects=True),
+        cost_estimate=pl.CostEstimate(
+            flops=0, bytes_accessed=size * own.size * 40, transcendentals=0
+        ),
+        name="line_gather_%d" % identity,
+    )(own)
+
+
+def line_scatter_kernel(size, chunks, parts, out, held, left, right, load_sem, send_sem, recv_sem):
+    here = lax.axis_index("tensor")
+    enter([(here < size - 1, {"tensor": here + 1}), (here > 0, {"tensor": here - 1})])
+    sides = ((0, 1, left), (1, -1, right))
+
+    def has_next(way):
+        return here < size - 1 if way > 0 else here > 0
+
+    def load(place, dest):
+        s, r, n = chunks[place]
+        return pltpu.make_async_copy(
+            parts.at[s, dest, pl.ds(r, n)],
+            held.at[s, dest, pl.ds(r, n)],
+            load_sem.at[dest, place],
+        )
+
+    def onward(side, way, dest, place, landing):
+        s, r, n = chunks[place]
+        return pltpu.make_async_remote_copy(
+            src_ref=held.at[s, dest, pl.ds(r, n)],
+            dst_ref=landing.at[s, dest, pl.ds(r, n)],
+            send_sem=send_sem.at[side, dest, place],
+            recv_sem=recv_sem.at[side, dest, place],
+            device_id={"tensor": here + way},
+            device_id_type=MESH,
+        )
+
+    def arrived(side, way, dest, place, landing):
+        s, r, n = chunks[place]
+        spot = landing.at[s, dest, pl.ds(r, n)]
+        pltpu.make_async_remote_copy(
+            src_ref=spot,
+            dst_ref=spot,
+            send_sem=send_sem.at[side, dest, place],
+            recv_sem=recv_sem.at[side, dest, place],
+            device_id={"tensor": here - way},
+            device_id_type=MESH,
+        ).wait_recv()
+
+    def reach(way, far):
+        return here + far < size if way > 0 else here >= far
+
+    for far in range(size - 1, -1, -1):
+        for place in range(len(chunks)):
+            for side, way, landing in sides[: 2 if far else 1]:
+                pl.when(reach(way, far))(load(place, here + way * far).start)
+    for far in range(size - 1, 0, -1):
+        for place in range(len(chunks)):
+            for side, way, landing in sides:
+
+                @pl.when(reach(way, far))
+                def _():
+                    s, r, n = chunks[place]
+                    dest = here + way * far
+                    load(place, dest).wait()
+
+                    @pl.when(has_next(-way))
+                    def _():
+                        arrived(side, way, dest, place, landing)
+                        spot = (s, dest, pl.ds(r, n))
+                        held[spot] = (
+                            held[spot].astype(single) + landing[spot].astype(single)
+                        ).astype(held.dtype)
+
+                    onward(side, way, dest, place, landing).start()
+
+    for place in range(len(chunks)):
+        s, r, n = chunks[place]
+        load(place, here).wait()
+        spot = (s, here, pl.ds(r, n))
+        out[s, pl.ds(r, n)] = held[spot].astype(single)
+        for side, way, landing in sides:
+
+            @pl.when(has_next(-way))
+            def _():
+                arrived(side, way, here, place, landing)
+                out[s, pl.ds(r, n)] += landing[spot].astype(single)
+
+    for far in range(size - 1, 0, -1):
+        for place in range(len(chunks)):
+            for side, way, landing in sides:
+                pl.when(reach(way, far))(
+                    onward(side, way, here + way * far, place, landing).wait_send
+                )
+
+
+def line_scatter(parts, size, cut, identity):
+    streams, _, rows, width = parts.shape
+    chunks = row_chunks(streams, rows, cut)
+    return pl.pallas_call(
+        lambda *refs: line_scatter_kernel(size, chunks, *refs),
+        out_shape=jax.ShapeDtypeStruct((streams, rows, width), single),
+        in_specs=[pl.BlockSpec(memory_space=pl.ANY)],
+        out_specs=pl.BlockSpec(memory_space=pltpu.VMEM),
+        scratch_shapes=[pltpu.VMEM(parts.shape, parts.dtype) for _ in range(3)]
+        + [
+            pltpu.SemaphoreType.DMA((size, len(chunks))),
+            pltpu.SemaphoreType.DMA((2, size, len(chunks))),
+            pltpu.SemaphoreType.DMA((2, size, len(chunks))),
+        ],
+        compiler_params=pltpu.CompilerParams(
+            collective_id=identity, has_side_effects=True, vmem_limit_bytes=56 * 2**20
+        ),
+        cost_estimate=pl.CostEstimate(
+            flops=0, bytes_accessed=parts.size * 40, transcendentals=0
+        ),
+        name="line_scatter_%d" % identity,
+    )(parts)
+
+
+def cube_sum_kernel(bits, value, out, total, landing, send_a, recv_a, send_b, recv_b):
+    rows, columns = value.shape
+
+    def partner(axis, size):
+        place = lax.axis_index(axis)
+        bit = lax.rem(place // size, 2)
+        return bit, {axis: place + (1 - 2 * bit) * size}
+
+    ends = [partner(*entry) for entry in bits]
+    enter([(jnp.bool_(True), device) for _, device in ends])
+    total[...] = value[...]
+    regions = [(0, rows, 0, columns)]
+    for step, (bit, device) in enumerate(ends):
+        r, n, c, m = regions[-1]
+        if n > 8:
+            n = n // 2
+            keep, give = (r + bit * n, n, c, m), (r + (1 - bit) * n, n, c, m)
+        else:
+            m = m // 2
+            keep, give = (r, n, c + bit * m, m), (r, n, c + (1 - bit) * m, m)
+        regions.append(keep)
+
+        def spot(region):
+            return (
+                pl.ds(pl.multiple_of(region[0], 8), region[1]),
+                pl.ds(pl.multiple_of(region[2], 128), region[3]),
+            )
+
+        copy = pltpu.make_async_remote_copy(
+            src_ref=total.at[spot(give)],
+            dst_ref=landing.at[step, pl.ds(0, n), pl.ds(0, m)],
+            send_sem=send_a.at[step],
+            recv_sem=recv_a.at[step],
+            device_id=device,
+            device_id_type=MESH,
+        )
+        copy.start()
+        copy.wait()
+        total[spot(keep)] += landing[step, pl.ds(0, n), pl.ds(0, m)]
+    out[spot(regions[-1])] = total[spot(regions[-1])]
+    for step in range(len(ends) - 1, -1, -1):
+        region = out.at[spot(regions[step + 1])]
+        copy = pltpu.make_async_remote_copy(
+            src_ref=region,
+            dst_ref=region,
+            send_sem=send_b.at[step],
+            recv_sem=recv_b.at[step],
+            device_id=ends[step][1],
+            device_id_type=MESH,
+        )
+        copy.start()
+        copy.wait()
+
+
+def cube_sum(value, bits, identity):
+    steps = len(bits)
+    rows, columns = value.shape
+    return pl.pallas_call(
+        lambda *refs: cube_sum_kernel(bits, *refs),
+        out_shape=jax.ShapeDtypeStruct(value.shape, value.dtype),
+        in_specs=[pl.BlockSpec(memory_space=pltpu.VMEM)],
+        out_specs=pl.BlockSpec(memory_space=pltpu.VMEM),
+        scratch_shapes=[
+            pltpu.VMEM(value.shape, value.dtype),
+            pltpu.VMEM((steps, rows // 2, columns), value.dtype),
+        ]
+        + [pltpu.SemaphoreType.DMA((steps,))] * 4,
+        compiler_params=pltpu.CompilerParams(
+            collective_id=identity, has_side_effects=True, vmem_limit_bytes=32 * 2**20
+        ),
+        name="cube_sum_%d" % identity,
+    )(value)
+
+
+def axis_bits(axis):
+    return [(axis, 2**bit) for bit in range(lax.axis_size(axis).bit_length() - 1)]
 
 
 def shards(
@@ -157,7 +442,7 @@
         :, None, :
     ]
     normed_own = (unit_flows * gain_all + shift_all).astype(bfloat)
-    normed = lax.all_gather(normed_own, "tensor", axis=1, tiled=True)
+    normed = line_gather(normed_own, groups, 1, 0).reshape(STREAMS, length, D)
     attn_weights = full_in[:, :attn_width].reshape(D, heads_group, 3, HD)
     up_weights = full_in[:, attn_width:]
     cosine_table, sine_table = rope_tables(length)
@@ -199,8 +484,9 @@
     attended = attended.reshape(length, heads_group, HD).astype(bfloat)
     joined = jnp.concatenate([attended.reshape(length, proj_width), hidden], axis=1)
     partial_value = contract_last(joined, full_out)
-    summed = lax.psum(partial_value.astype(jnp.bfloat16), "tensor").astype(jnp.float32)
-    branch = lax.dynamic_slice_in_dim(summed, group_index * own_rows, own_rows, 0)
+    branch = line_scatter(
+        partial_value.astype(bfloat).reshape(1, groups, own_rows, D), groups, 4, 1
+    )[0]
     newest = flow_rows[3] + branch + small_params[8] + small_params[9]
     inv_rms = lax.rsqrt(jnp.mean(newest * newest, axis=-1, keepdims=True) + mix_eps)
     mix_normed = (newest * inv_rms * gain_mix).astype(bfloat)
@@ -241,7 +527,7 @@
         - newest * inv_rms**3 * jnp.mean(scaled_back * newest, axis=-1, keepdims=True)
     )
     grad_bias_out = jnp.sum(d_newest, axis=0)
-    branch_grads = lax.all_gather(d_newest.astype(bfloat), "tensor", axis=0, tiled=True)
+    branch_grads = line_gather(d_newest.astype(bfloat)[None], groups, 4, 2).reshape(length, D)
     d_joined = jnp.dot(branch_grads, full_out, preferred_element_type=single)
     d_attended = d_joined[:, :proj_width].reshape(length, heads_group, HD).astype(bfloat)
     d_up = (d_joined[:, proj_width:] * gelu_slope(up_pre)).astype(bfloat)
@@ -297,8 +583,9 @@
     ]
     d_norm_parts.append(contract_last(d_up, up_weights))
     d_normed = jnp.stack(d_norm_parts)
-    d_sum = lax.psum(d_normed.astype(jnp.bfloat16), "tensor").astype(jnp.float32)
-    d_own = lax.dynamic_slice_in_dim(d_sum, group_index * own_rows, own_rows, 1)
+    d_own = line_scatter(
+        d_normed.astype(bfloat).reshape(STREAMS, groups, own_rows, D), groups, 1, 3
+    )
     d_unit = d_own * gain_all
     d_flows = inverse * (
         d_unit
@@ -336,24 +623,29 @@
         axis=0,
     )
     mix_grad = jnp.concatenate([grad_mix_out, grad_mix_bias[None]], axis=0)
-    small_parameter_total, mix_total = lax.psum((small_grad, mix_grad), ("dp", "tensor"))
     attn_part = jnp.einsum(
         "pld,lhpe->dhpe", normed[:3], d_pres, preferred_element_type=single
-    ).reshape(lax.axis_size("dp") * shard_rows, attn_width)
+    ).reshape(D, attn_width)
     up_part = contract_first(normed[3], d_up)
-    weight_grads = lax.psum_scatter(
-        jnp.concatenate(
-            [jnp.concatenate([attn_part, up_part], axis=1), contract_first(branch_grads, joined)],
-            axis=1,
-        ).astype(jnp.bfloat16),
-        "dp",
-        scatter_dimension=0,
-        tiled=True,
-    ).astype(jnp.float32)
-    grad_in = weight_grads[:, : attn_width + units_group]
-    grad_out = weight_grads[:, attn_width + units_group :]
+
+    def owned(part):
+        return lax.psum_scatter(
+            part.astype(bfloat), "dp", scatter_dimension=0, tiled=True
+        ).astype(single)
+
+    grad_out = owned(contract_first(branch_grads, joined))
+    grad_in = owned(jnp.concatenate([attn_part, up_part], axis=1))
     big_square = jnp.sum(grad_in * grad_in) + jnp.sum(grad_out * grad_out)
-    big_total = lax.psum(big_square, ("dp", "tensor"))
+    small_rows = small_grad.shape[0]
+    mix_row = jnp.concatenate([mix_grad.reshape(-1), big_square[None]])
+    mix_row = jnp.pad(mix_row, (0, D - mix_row.shape[0]))
+    packed = jnp.concatenate(
+        [small_grad, mix_row[None], jnp.zeros((63 - small_rows, D), single)], axis=0
+    )
+    packed = cube_sum(packed, axis_bits("dp") + axis_bits("tensor"), 4)
+    small_parameter_total = packed[:small_rows]
+    mix_total = packed[small_rows, : mix_grad.size].reshape(mix_grad.shape)
+    big_total = packed[small_rows, mix_grad.size]
     grad_norm = jnp.sqrt(
         big_total
         + jnp.sum(small_parameter_total * small_parameter_total)

time: 1230 us -> 741 us (0.60)
  waiting for transfers between devices: 828 us -> 0.07 us
  Pallas kernels: 0 us -> 386 us
  blocking collectives: 41.4 us -> 0 us
  matrix products: 129 us -> 113 us
    psum x3 -> x0, waiting for transfers between devices: 392 us -> none  [the longest x1 192 us: shards(): lax.psum(d_normed.astype(jnp.bfloat16), 'tensor').astype(jnp.float32)]
    pallas_call x0 -> x5, Pallas kernels: none -> 386 us  [the longest x2 179 us: line_gather(): pl.pallas_call(lambda *refs: line_gather_kernel(size, chunks, *refs), out...]
    all_gather x2 -> x0, waiting for transfers between devices: 188 us -> none  [the longest x1 144 us: shards(): normed = lax.all_gather(normed_own, 'tensor', axis=1, tiled=True)]
    reduce_scatter x1 -> x2, waiting for transfers between devices: 142 us -> 0.01 us  [owned(): lax.psum_scatter(part.astype(bfloat), 'dp', scatter_dimension=0, tiled=True)]
    all_gather x1, waiting for transfers between devices: 74.4 us -> 0.01 us  [shards(): lax.all_gather(in_weights.astype(bfloat), 'dp', axis=0, tiled=True)]
    psum x1 -> x0, blocking collectives: 41.4 us -> none  [shards(): big_total = lax.psum(big_square, ('dp', 'tensor'))]
    unnamed x174 -> x224, local copies, waits for them, and re-layouts: 27.9 us -> 63 us
    all_gather x1, waiting for transfers between devices: 32 us -> 0.01 us  [shards(): lax.all_gather(out_weights.astype(bfloat), 'dp', axis=0, tiled=True)]
  transfers between devices with their start and end apart: 8 -> 4, of which waited for: 8 -> 0; matrix products, arithmetic and copies ran while one was open for 15% -> 24% of each run, Pallas kernels for 0% -> 38%
where the time goes in v1:
time: 741 us; the launch traced here: 733 us
  Pallas kernels  386 us (52%)
  matrix products  113 us (15%)
  local copies, waits for them, and re-layouts  110 us (15%)
  other arithmetic  104 us (14%)
  between operations  20 us (3%)
    pallas_call x2, Pallas kernels, line_gather(): pl.pallas_call(lambda *refs: line_gather_kernel(size, chunks, *refs), out...  179 us
    pallas_call x2, Pallas kernels, line_scatter(): pl.pallas_call(lambda *refs: line_scatter_kernel(size, chunks, *refs), ou...  174 us
    unnamed x224, local copies, waits for them, and re-layouts  63 us
    pallas_call x1, Pallas kernels, cube_sum(): pl.pallas_call(lambda *refs: cube_sum_kernel(bits, *refs), out_shape=jax....  33 us
    dot_general x1, matrix products, shards(): jnp.dot(normed[3], up_weights, preferred_element_type=single) + bias_units  18 us
    dot_general x3, matrix products, contract_last(): lax.dot_general(left_side, right_side, (((left_side.ndim - 1,), (right_si...  17.8 us
    concatenate x1, other arithmetic, shards(): grad_in = owned(jnp.concatenate([attn_part, up_part], axis=1))  17.5 us
    dot_general x3, matrix products, contract_first(): lax.dot_general(left_side, right_side, (((0,), (0,)), ((), ())), preferre...  17.5 us
  transfers between devices with their start and end apart: 4, of which 0 were waited for; matrix products, arithmetic and copies ran while one was open for 24% of the time, Pallas kernels for 38%

profile of v1, /device:TPU:0, one launch (start us, length us, event | category | flops | bytes accessed | tf_op | source)
XLA Modules:
  0.0 733.0 jit_solution(17519462002265185959)
XLA Ops:
  29.0 140.8 %line_gather_0.1 = bf16[4,4,128,2048]{3,2,1,0:T(8,128)(2,1)} custom-call(bf16[4,128,2048]{2,1,0:T(8,128)(2,1)} %add_convert_fusion.1.refs_0_), custom_call_target="tpu_custom_call" | custom-call | bytes 167772160 | tf_op jit(solution)/shard_map/line_gather_0/pallas_call | solution.py:182
  174.1 7.0 fusion.14
  199.5 18.0 %fusion.7 = (bf16[512,2048]{1,0:T(8,128)(2,1)}, f32[512,2048]{1,0:T(8,128)}) fusion(f32[2048]{0:T(1024)} %dynamic_slice.14, bf16[512,2048]{1,0:T(8,128)(2,1)} %bitcast.286, bf16[2048,3584]{0,1:T(8,128)(2,1)} %all-gather.3.cloned.1.call-done), kind=kOutput, calls=%fused_computation.19 | convolution fusion | flops 4364173312 | bytes 16785408 | tf_op jit(solution)/shard_map/dot_general | solution.py:464
  217.5 10.0 %convolution_convert_fusion.2 = bf16[512,2048]{1,0:T(8,128)(2,1)} fusion(bf16[2048,2560]{1,0:T(8,128)(2,1)} %all-gather.5.cloned.1.call-done, bf16[512,2048]{1,0:T(8,128)(2,1)} %get-tuple-element.262, bf16[512,512]{1,0:T(8,128)(2,1)S(1)} %copy.191), kind=kOutput, calls=%fused_computation.76 | convolution fusion | flops 5375000576 | bytes 15204352 | tf_op jit(solution)/shard_map/dot_general | solution.py:73
  227.5 35.8 %line_scatter_1.1 = f32[1,128,2048]{2,1,0:T(8,128)} custom-call(bf16[1,4,128,2048]{3,2,1,0:T(8,128)(2,1)} %bitcast.283), custom_call_target="tpu_custom_call" | custom-call | bytes 41943040 | tf_op jit(solution)/shard_map/line_scatter_1/pallas_call | solution.py:289
  269.8 8.6 %convolution_bitcast_fusion = f32[128,4,1]{2,1,0:T(4,128)S(1)} fusion(bf16[4,128,2048]{2,1,0:T(8,128)(2,1)S(1)} %copy-done.27, f32[128,2048,1]{1,0,2:T(8,128)S(1)} %bitcast.272), kind=kOutput, calls=%fused_computation.106 | convolution fusion | flops 12582912 | bytes 3147776 | tf_op jit(solution)/shard_map/srd,rd->rs/dot_general | solution.py:510
  284.4 11.8 %fusion.64 = f32[128,9,2048]{2,1,0:T(8,128)} fusion(f32[128,4,9]{2,1,0:T(4,128)S(1)} %copy.192, bf16[4,128,2048]{2,1,0:T(8,128)(2,1)} %param.21), kind=kOutput, calls=%fused_computation.112 | convolution fusion | flops 113246208 | bytes 11552768 | tf_op jit(solution)/shard_map/rsj,srd->jrd/dot_general | solution.py:512
  296.2 14.7 %copy.275 = f32[128,9,2048]{2,0,1:T(8,128)} copy(f32[128,9,2048]{2,1,0:T(8,128)} %fusion.64) | data formatting | bytes 18874368 | tf_op jit(solution)/shard_map/rsj,srd->jrd/dot_general | solution.py:512
  314.0 37.8 %line_gather_2.1 = bf16[1,4,128,2048]{3,2,1,0:T(8,128)(2,1)} custom-call(bf16[1,128,2048]{2,1,0:T(8,128)(2,1)} %convert_bitcast_fusion.1.refs_0_), custom_call_target="tpu_custom_call" | custom-call | bytes 41943040 | tf_op jit(solution)/shard_map/line_gather_2/pallas_call | solution.py:182
  351.9 10.2 %convolution_convert_fusion = bf16[2048,2560]{1,0:T(8,128)(2,1)} fusion(bf16[512,2048]{1,0:T(8,128)(2,1)} %bitcast.281, bf16[512,2048]{1,0:T(8,128)(2,1)} %get-tuple-element.262, bf16[512,512]{1,0:T(8,128)(2,1)S(1)} %copy-done.56), kind=kOutput, calls=%fused_computation.1 | convolution fusion | flops 5379194880 | bytes 15204352 | tf_op jit(solution)/shard_map/dot_general | solution.py:82
  363.6 8.4 %fusion.137 = f32[512,2560]{1,0:T(8,128)S(1)} fusion(bf16[512,2048]{1,0:T(8,128)(2,1)S(1)} %bitcast.282, bf16[2048,2560]{1,0:T(8,128)(2,1)} %all-gather.5.cloned.1.call-done), kind=kOutput, calls=%fused_computation.272 | convolution fusion | flops 5368709120 | bytes 17825792 | tf_op jit(solution)/shard_map/dot_general | solution.py:531
  395.4 7.2 convolution_convert_fusion.1
  402.6 17.5 %pad_maximum_fusion = bf16[2048,3584]{0,1:T(8,128)(2,1)} fusion(bf16[2048,2048]{0,1:T(8,128)(2,1)S(1)} %convolution_convert_fusion.1, bf16[2048,1536]{0,1:T(8,128)(2,1)S(1)} %bitcast.269), kind=kLoop, calls=%fused_computation | loop fusion | flops 29360128 | bytes 29360128 | tf_op jit(solution)/shard_map/concatenate | solution.py:637
  425.3 5.2 copy.213
  430.4 5.3 copy.216
  435.8 6.6 bitcast_convert_fusion.10
  445.4 6.2 slice.479
  455.8 6.9 fusion.29
  467.1 138.2 %line_scatter_3.1 = f32[4,128,2048]{2,1,0:T(8,128)} custom-call(bf16[4,4,128,2048]{3,2,1,0:T(8,128)(2,1)} %pad_maximum_fusion.1.refs_0_), custom_call_target="tpu_custom_call" | custom-call | bytes 167772160 | tf_op jit(solution)/shard_map/line_scatter_3/pallas_call | solution.py:289
  637.4 33.0 %cube_sum_4.1 = f32[64,2048]{1,0:T(8,128)S(1)} custom-call(f32[64,2048]{1,0:T(8,128)S(1)} %concatenate.113.refs_0_), custom_call_target="tpu_custom_call" | custom-call | tf_op jit(solution)/shard_map/cube_sum_4/pallas_call | solution.py:367
  674.4 8.3 %fusion.118 = (bf16[256,3584]{0,1:T(8,128)(2,1)}, f32[256,3584]{0,1:T(8,128)}, f32[256,3584]{0,1:T(8,128)}, f32[256,3584]{0,1:T(8,128)}) fusion(f32[256,3584]{0,1:T(8,128)} %copy.183, f32[]{:T(128)S(6)} %div.102, bf16[256,3584]{0,1:T(8,128)(2,1)S(1)} %copy-done.11, f32[256,3584]{0,1:T(8,128)} %copy.212, f32[256,3584]{0,1:T(8,128)} %copy.213), kind=kLoop, calls=%fused_computation.256 | loop fusion | flops 16515072 | bytes 25690116 | tf_op jit(solution)/shard_map/convert_element_type | solution.py:680
  698.0 5.4 add_multiply_fusion
  703.5 5.3 copy.220
  712.8 7.3 fusion.115
  (346 shorter events, 157.7 us)
Async XLA Ops:
  7.2 177.8 %all-gather.3.cloned.1.call-start = ((), (), s32[]{:S(2)}) async-start(), calls=%async_computation.2 | async-start | bytes 16515072 | tf_op jit(solution)/shard_map/all_gather | solution.py:423
  15.8 201.7 %all-gather.5.cloned.1.call-start = ((), (), s32[]{:S(2)}) async-start(), calls=%async_computation.3 | async-start | bytes 11796480 | tf_op jit(solution)/shard_map/all_gather | solution.py:424
  19.0 610.7 %reduce-scatter.5.cloned.1.call-start = ((), (), s32[]{:S(2)}) async-start(), calls=%async_computation.5 | async-start | bytes 11796480 | tf_op jit(solution)/shard_map/reduce_scatter | solution.py:632
  23.6 146.2 %copy-start.80 = (f32[4,128]{1,0:T(4,128)}, f32[4,128]{1,0:T(4,128)S(1)}, u32[]{:S(2)}) copy-start(f32[4,128]{1,0:T(4,128)S(1)} %add_rsqrt_fusion) | copy-start | bytes 6148
  25.4 237.9 %copy-start.76 = (f32[1,2048]{1,0:T(1,128)}, f32[1,2048]{1,0:T(1,128)S(1)}, u32[]{:S(2)}) copy-start(f32[1,2048]{1,0:T(1,128)S(1)} %get-tuple-element.226) | copy-start | bytes 24580
  29.0 145.1 %copy-start.27 = (bf16[4,128,2048]{2,1,0:T(8,128)(2,1)S(1)}, bf16[4,128,2048]{2,1,0:T(8,128)(2,1)}, u32[]{:S(2)}) copy-start(bf16[4,128,2048]{2,1,0:T(8,128)(2,1)} %param.21) | copy-start | bytes 6291460
  172.1 22.6 %copy-start.48 = (f32[512,32]{0,1:T(8,128)}, f32[512,32]{0,1:T(8,128)S(1)}, u32[]{:S(2)}) copy-start(f32[512,32]{0,1:T(8,128)S(1)} %get-tuple-element.256) | copy-start | bytes 196612
  172.1 22.6 %copy-start.50 = (f32[512,32]{0,1:T(8,128)}, f32[512,32]{0,1:T(8,128)S(1)}, u32[]{:S(2)}) copy-start(f32[512,32]{0,1:T(8,128)S(1)} %get-tuple-element.255) | copy-start | bytes 196612
  199.5 18.0 %copy-start.55 = (bf16[512,512]{1,0:T(8,128)(2,1)}, bf16[512,512]{1,0:T(8,128)(2,1)S(1)}, u32[]{:S(2)}) copy-start(bf16[512,512]{1,0:T(8,128)(2,1)S(1)} %copy.191) | copy-start | bytes 1572868
  217.5 45.8 %copy-start.77 = (f32[1,2048]{1,0:T(1,128)S(1)}, f32[1,2048]{1,0:T(1,128)}, u32[]{:S(2)}) copy-start(f32[1,2048]{1,0:T(1,128)} %get-tuple-element.227) | copy-start | bytes 24580
  227.5 38.6 %copy-start.36 = (f32[50,2048]{1,0:T(8,128)S(1)}, f32[50,2048]{1,0:T(8,128)}, u32[]{:S(2)}) copy-start(f32[50,2048]{1,0:T(8,128)} %param.30) | copy-start | bytes 1228804
  227.5 40.1 %copy-start.73 = (f32[37,36]{1,0:T(8,128)S(1)}, f32[37,36]{1,0:T(8,128)}, u32[]{:S(2)}) copy-start(f32[37,36]{1,0:T(8,128)} %param.34) | copy-start | bytes 15988
  227.5 40.1 %copy-start.96 = (f32[36]{0:T(128)S(1)}, f32[36]{0:T(128)}, u32[]{:S(2)}) copy-start(f32[36]{0:T(128)} %slice_bitcast_fusion.4) | copy-start | bytes 436
  313.1 38.7 %copy-start.56 = (bf16[512,512]{1,0:T(8,128)(2,1)S(1)}, bf16[512,512]{1,0:T(8,128)(2,1)}, u32[]{:S(2)}) copy-start(bf16[512,512]{1,0:T(8,128)(2,1)} %copy-done.55) | copy-start | bytes 1572868
  362.0 270.2 %reduce-scatter.3.cloned.1.call-start = ((), (), s32[]{:S(2)}) async-start(), calls=%async_computation.4 | async-start | bytes 16515072 | tf_op jit(solution)/shard_map/reduce_scatter | solution.py:632
  430.4 21.2 %slice-start.1 = ((s8[6291456]{0:T(1024)(128)(4,1)}), s8[2097152]{0:T(1024)(128)(4,1)S(1)}, s32[]{:S(2)}) async-start(s8[6291456]{0:T(1024)(128)(4,1)} %bitcast.264), calls=%async_computation.7 | async-start | bytes 4194304
  435.7 15.9 %slice-start.2 = ((s8[6291456]{0:T(1024)(128)(4,1)}), s8[4194304]{0:T(1024)(128)(4,1)S(1)}, s32[]{:S(2)}) async-start(s8[6291456]{0:T(1024)(128)(4,1)} %bitcast.264), calls=%async_computation.8 | async-start | bytes 8388608
  435.7 19.8 %slice-start.5 = ((s8[14680064]{0:T(1024)(128)(4,1)}), s8[2097152]{0:T(1024)(128)(4,1)S(1)}, s32[]{:S(2)}) async-start(s8[14680064]{0:T(1024)(128)(4,1)} %bitcast.279), calls=%async_computation.11 | async-start | bytes 4194304
  435.7 19.9 %slice-start.6 = ((s8[14680064]{0:T(1024)(128)(4,1)}), s8[4194304]{0:T(1024)(128)(4,1)S(1)}, s32[]{:S(2)}) async-start(s8[14680064]{0:T(1024)(128)(4,1)} %bitcast.279), calls=%async_computation.12 | async-start | bytes 8388608
  467.1 138.2 %copy-start.1 = (bf16[4,128,2048]{2,1,0:T(8,128)(2,1)S(1)}, bf16[4,128,2048]{2,1,0:T(8,128)(2,1)}, u32[]{:S(2)}) copy-start(bf16[4,128,2048]{2,1,0:T(8,128)(2,1)} %param.19) | copy-start | bytes 6291460
  467.1 138.2 %copy-start.53 = (f32[4,2048]{1,0:T(4,128)S(1)}, f32[4,2048]{1,0:T(4,128)}, u32[]{:S(2)}) copy-start(f32[4,2048]{1,0:T(4,128)} %copy-done.52) | copy-start | bytes 98308
  467.1 138.2 %copy-start.79 = (f32[4,128]{1,0:T(4,128)S(1)}, f32[4,128]{1,0:T(4,128)}, u32[]{:S(2)}) copy-start(f32[4,128]{1,0:T(4,128)} %copy-done.78) | copy-start | bytes 6148
  467.1 138.2 %copy-start.81 = (f32[4,128]{1,0:T(4,128)S(1)}, f32[4,128]{1,0:T(4,128)}, u32[]{:S(2)}) copy-start(f32[4,128]{1,0:T(4,128)} %copy-done.80) | copy-start | bytes 6148
  632.3 42.2 %copy-start.11 = (bf16[256,3584]{0,1:T(8,128)(2,1)S(1)}, bf16[256,3584]{0,1:T(8,128)(2,1)}, u32[]{:S(2)}) copy-start(bf16[256,3584]{0,1:T(8,128)(2,1)} %reduce-scatter.3.cloned.1.call-done) | copy-start | bytes 5505028
  (86 other events, 362.6 us)
Sparse Core Ops, SparseCore 0:
  15.9 86.5 all-gather.2
  105.0 63.2 all-gather.4
  362.2 80.5 reduce-scatter.4
  446.1 103.5 reduce-scatter.2

commit v2 on v1

--- a/solution.py
+++ b/solution.py
@@ -383,6 +383,536 @@
 
 def axis_bits(axis):
     return [(axis, 2**bit) for bit in range(lax.axis_size(axis).bit_length() - 1)]
+
+
+def plus_flips(place, bits):
+    moved = place
+    for bit in bits:
+        moved = moved + (1 - 2 * lax.rem(place // 2**bit, 2)) * 2**bit
+    return moved
+
+
+def cube_routes(count):
+    bits = list(range(1, count))
+    pieces = []
+    for turn in range(len(bits)):
+        order = bits[turn:] + bits[:turn]
+        arrivals = [()]
+        steps = []
+        for bit in order:
+            fresh = [held + (bit,) for held in arrivals]
+            steps.append([(bit, held, whole) for held, whole in zip(arrivals, fresh)])
+            arrivals = arrivals + fresh
+        pieces.append((arrivals, steps))
+    return pieces
+
+
+class CubeGather:
+    def __init__(self, whole, rows, count, sems):
+        self.whole, self.rows, self.count = whole, rows, count
+        self.send_sem, self.recv_sem, self.pair_send, self.pair_recv = sems
+        self.routes = cube_routes(count.bit_length() - 1)
+        self.me = lax.axis_index("dp")
+        self.piece_rows = rows // len(self.routes)
+
+    def region(self, piece, held):
+        first = plus_flips(self.me, held) * self.rows + piece * self.piece_rows
+        return self.whole.at[pl.ds(pl.multiple_of(first, 16), self.piece_rows)]
+
+    def hop(self, piece, bit, held, slot, pair=False):
+        block = self.region(piece, held)
+        return pltpu.make_async_remote_copy(
+            src_ref=block,
+            dst_ref=block,
+            send_sem=(self.pair_send if pair else self.send_sem).at[piece, slot],
+            recv_sem=(self.pair_recv if pair else self.recv_sem).at[piece, slot],
+            device_id={"dp": plus_flips(self.me, (bit,))},
+            device_id_type=MESH,
+        )
+
+    def slot(self, piece, held):
+        return self.routes[piece][0].index(held)
+
+    def sends_of(self, piece, held):
+        found = []
+        for step in self.routes[piece][1]:
+            for bit, source, landed in step:
+                if source == held:
+                    found.append(self.hop(piece, bit, held, self.slot(piece, landed)))
+        found.append(self.hop(piece, 0, held, self.slot(piece, held), True))
+        return found
+
+    def start(self):
+        for piece in range(len(self.routes)):
+            for copy in self.sends_of(piece, ()):
+                copy.start()
+
+    def step(self, index):
+        for piece, (_, steps) in enumerate(self.routes):
+            for bit, _, landed in steps[index]:
+                self.hop(piece, bit, landed, self.slot(piece, landed)).wait_recv()
+                for copy in self.sends_of(piece, landed):
+                    copy.start()
+
+    def steps(self):
+        return len(self.routes)
+
+    def finish(self):
+        for piece, (arrivals, _) in enumerate(self.routes):
+            for held in arrivals:
+                self.hop(piece, 0, (0,) + held, self.slot(piece, held), True).wait_recv()
+
+    def drain(self):
+        for piece, (arrivals, _) in enumerate(self.routes):
+            for held in arrivals:
+                for copy in self.sends_of(piece, held):
+                    copy.wait_send()
+
+
+FLOW_ORDER = (1, 2, 3, 0)
+
+
+def forward_kernel(
+    size,
+    count,
+    flows,
+    w_in,
+    w_out,
+    small,
+    rope,
+    all_in,
+    all_out,
+    all_normed,
+    joined_out,
+    slope_out,
+    heads_out,
+    chances_out,
+    newest,
+    w_in_low,
+    w_out_low,
+    normed,
+    heads,
+    chances,
+    joined,
+    slope,
+    total,
+    give,
+    terms,
+    stage_sem,
+    line_send,
+    line_recv,
+    term_send,
+    term_recv,
+    save_sem,
+    flow_sem,
+    *cube_sems,
+):
+    here = lax.axis_index("tensor")
+    me = lax.axis_index("dp")
+    own = flows.shape[1]
+    rows_in = w_in.shape[0]
+    length = own * size
+    width_in, width_out = w_in.shape[1], w_out.shape[1]
+    head_width = heads.shape[2]
+    group_heads = head_width // HD
+    attn_width = 3 * head_width
+    units = width_in - attn_width
+    bits = count.bit_length() - 1
+    sides = ((0, 1), (1, -1))
+    tile = 512
+
+    def rows_of(block):
+        return pl.ds(pl.multiple_of(block * own, own), own)
+
+    def stage(source, width):
+        spans = [(0, min(width, D))] + ([(D, width - D)] if width > D else [])
+        return [
+            pltpu.make_async_copy(
+                source.at[:, pl.ds(first, span)],
+                total.at[pl.ds(place * rows_in, rows_in), pl.ds(0, span)],
+                stage_sem.at[place],
+            )
+            for place, (first, span) in enumerate(spans)
+        ]
+
+    def settle(source, width, target):
+        for place, copy in enumerate(stage(source, width)):
+            copy.wait()
+            span = min(D, width - place * D)
+
+            def cast(index, carry):
+                low = pl.multiple_of(index * 16, 16)
+                into = pl.multiple_of(me * rows_in + index * 16, 16)
+                target[pl.ds(into, 16), pl.ds(place * D, span)] = total[
+                    pl.ds(place * rows_in + low, 16), pl.ds(0, span)
+                ].astype(bfloat)
+                return carry
+
+            lax.fori_loop(0, rows_in // 16, cast, 0)
+
+    for copy in stage(w_in, width_in):
+        copy.start()
+    others = [lax.rem(here + step, size) for step in range(1, size)]
+    enter(
+        [(jnp.bool_(True), {"tensor": other}) for other in others]
+        + [(jnp.bool_(True), {"dp": plus_flips(me, (bit,))}) for bit in range(bits)]
+    )
+
+    def line_hop(side, way, step, flow):
+        block = normed.at[flow, rows_of(here - way * step)]
+        return pltpu.make_async_remote_copy(
+            src_ref=block,
+            dst_ref=block,
+            send_sem=line_send.at[side, step, flow],
+            recv_sem=line_recv.at[side, step, flow],
+            device_id={"tensor": here + way},
+            device_id_type=MESH,
+        )
+
+    def line_landed(side, way, step, flow):
+        block = normed.at[flow, rows_of(here - way * step)]
+        return pltpu.make_async_remote_copy(
+            src_ref=block,
+            dst_ref=block,
+            send_sem=line_send.at[side, step - 1, flow],
+            recv_sem=line_recv.at[side, step - 1, flow],
+            device_id={"tensor": here - way},
+            device_id_type=MESH,
+        )
+
+    def has_next(way):
+        return here < size - 1 if way > 0 else here > 0
+
+    def has_origin(way, step):
+        return here >= step if way > 0 else here < size - step
+
+    def keep_flow(flow, block):
+        return pltpu.make_async_copy(
+            normed.at[flow, rows_of(block)],
+            all_normed.at[flow, rows_of(block)],
+            flow_sem.at[flow, block],
+        )
+
+    for flow in FLOW_ORDER:
+        which = 2 if flow == 3 else 0
+
+        def normalize(index, carry):
+            spot = pl.ds(pl.multiple_of(index * 16, 16), 16)
+            values = flows[flow, spot].astype(single)
+            centred = values - jnp.mean(values, axis=-1, keepdims=True)
+            inverse = lax.rsqrt(jnp.mean(centred * centred, axis=-1, keepdims=True) + norm_eps)
+            into = pl.ds(pl.multiple_of(here * own + index * 16, 16), 16)
+            normed[flow, into] = (
+                centred * inverse * small[which : which + 1, :] + small[which + 1 : which + 2, :]
+            ).astype(bfloat)
+            return carry
+
+        lax.fori_loop(0, own // 16, normalize, 0)
+        for side, way in sides:
+            pl.when(has_next(way))(line_hop(side, way, 0, flow).start)
+        keep_flow(flow, here).start()
+
+    cube_in = CubeGather(w_in_low, rows_in, count, cube_sems[:4])
+    cube_out = CubeGather(w_out_low, rows_in, count, cube_sems[4:])
+    settle(w_in, width_in, w_in_low)
+    cube_in.start()
+    for copy in stage(w_out, width_out):
+        copy.start()
+    settle(w_out, width_out, w_out_low)
+
+    def line_step(step, flow_list):
+        for flow in flow_list:
+            for side, way in sides:
+
+                @pl.when(has_origin(way, step))
+                def _():
+                    line_landed(side, way, step, flow).wait_recv()
+                    pl.when(has_next(way))(line_hop(side, way, step, flow).start)
+                    keep_flow(flow, here - way * step).start()
+
+    def at_distance(step, action):
+        if step == 0:
+            action(here)
+            return
+        for side, way in sides:
+
+            @pl.when(has_origin(way, step))
+            def _():
+                action(here - way * step)
+
+    def project(block, part):
+        rows = rows_of(block)
+        source = normed[part, rows]
+        pre = jnp.dot(
+            source,
+            jnp.concatenate(
+                [
+                    w_in_low[:, pl.ds((head * 3 + part) * HD, HD)]
+                    for head in range(group_heads)
+                ],
+                axis=1,
+            ),
+            preferred_element_type=single,
+        )
+        first = pl.multiple_of(here * head_width, HD)
+        pre = pre + small[5 + part : 6 + part, pl.ds(first, head_width)]
+        if part == 2:
+            heads[part, rows] = pre.astype(bfloat)
+            return
+        cosine, sine_low, sine_high = rope[0, rows], rope[1, rows], rope[2, rows]
+        for head in range(group_heads):
+            values = pre[:, head * HD : (head + 1) * HD]
+            turned = (
+                values * cosine
+                + pltpu.roll(values, HD - ROT // 2, 1) * sine_low
+                + pltpu.roll(values, ROT // 2, 1) * sine_high
+            )
+            heads[part, rows, pl.ds(head * HD, HD)] = turned.astype(bfloat)
+
+    def expand(block):
+        rows = rows_of(block)
+
+        def one(index, carry):
+            first = pl.multiple_of(index * tile, tile)
+            pre = jnp.dot(
+                normed[3, rows],
+                w_in_low[:, pl.ds(attn_width + first, tile)],
+                preferred_element_type=single,
+            )
+            pre = pre + small[pl.ds(10 + here, 1), pl.ds(first, tile)]
+            normal = 0.5 * (1.0 + lax.erf(pre * 0.7071067811865476))
+            joined[rows, pl.ds(head_width + first, tile)] = (pre * normal).astype(bfloat)
+            slope[rows, pl.ds(first, tile)] = (
+                normal + pre * jnp.exp(-0.5 * pre * pre) * 0.3989422804014327
+            ).astype(bfloat)
+            return carry
+
+        lax.fori_loop(0, units // tile, one, 0)
+
+    def contract(block):
+        rows = rows_of(block)
+
+        def one(index, carry):
+            first = pl.multiple_of(index * tile, tile)
+            total[rows, pl.ds(first, tile)] = contract_last(
+                joined[rows, pl.ds(head_width, units)],
+                w_out_low[pl.ds(first, tile), pl.ds(head_width, units)],
+            )
+            return carry
+
+        lax.fori_loop(0, D // tile, one, 0)
+
+    def attend(block):
+        rows = rows_of(block)
+        places = block * own + lax.broadcasted_iota(jnp.int32, (own, length), 0)
+        allowed = lax.broadcasted_iota(jnp.int32, (own, length), 1) <= places
+        for head in range(group_heads):
+            lanes = pl.ds(head * HD, HD)
+            scores = contract_last(heads[0, rows, lanes], heads[1, :, lanes]) * HD ** (-0.5)
+            scores = jnp.where(allowed, scores, masked_score)
+            raised = jnp.exp(scores - jnp.max(scores, axis=-1, keepdims=True))
+            low = (raised / jnp.sum(raised, axis=-1, keepdims=True)).astype(bfloat)
+            chances[head, rows] = low
+            joined[rows, lanes] = jnp.dot(
+                low, heads[2, :, lanes], preferred_element_type=single
+            ).astype(bfloat)
+
+    def term_hop(dest):
+        return pltpu.make_async_remote_copy(
+            src_ref=give.at[rows_of(dest)],
+            dst_ref=terms.at[here],
+            send_sem=term_send.at[dest],
+            recv_sem=term_recv.at[here],
+            device_id={"tensor": dest},
+            device_id_type=MESH,
+        )
+
+    def finish_block(block):
+        attend(block)
+        rows = rows_of(block)
+
+        def one(index, carry):
+            first = pl.multiple_of(index * tile, tile)
+            spot = (rows, pl.ds(first, tile))
+            give[spot] = (
+                total[spot]
+                + contract_last(
+                    joined[rows, pl.ds(0, head_width)],
+                    w_out_low[pl.ds(first, tile), pl.ds(0, head_width)],
+                )
+            ).astype(bfloat)
+            return carry
+
+        lax.fori_loop(0, D // tile, one, 0)
+        pl.when(block != here)(term_hop(block).start)
+
+    def save(place, source, target):
+        return pltpu.make_async_copy(source, target, save_sem.at[place])
+
+    line_step(1, FLOW_ORDER[:2])
+    cube_in.step(0)
+    cube_out.start()
+    line_step(1, FLOW_ORDER[2:])
+    for index in range(1, cube_in.steps()):
+        cube_in.step(index)
+    cube_in.finish()
+    save(0, w_in_low, all_in).start()
+
+    def early(block):
+        project(block, 1)
+        project(block, 2)
+        expand(block)
+        project(block, 0)
+
+    at_distance(0, early)
+    line_step(2, FLOW_ORDER[:2])
+    at_distance(1, early)
+    cube_out.step(0)
+    line_step(2, FLOW_ORDER[2:])
+    at_distance(2, early)
+    for index in range(1, cube_out.steps()):
+        cube_out.step(index)
+    cube_out.finish()
+    save(1, w_out_low, all_out).start()
+    for step in range(size - 1):
+        at_distance(step, contract)
+    for step in range(3, size):
+        line_step(step, FLOW_ORDER[:2])
+
+    def keys_values(block):
+        project(block, 1)
+        project(block, 2)
+
+    for step in range(3, size):
+        at_distance(step, keys_values)
+    for step in range(min(3, size)):
+        at_distance(step, finish_block)
+    for step in range(3, size):
+        line_step(step, FLOW_ORDER[2:3])
+
+        def late(block):
+            expand(block)
+            contract(block)
+
+        at_distance(step, late)
+        line_step(step, FLOW_ORDER[3:])
+
+        def last(block):
+            project(block, 0)
+            finish_block(block)
+
+        at_distance(step, last)
+    saves = [
+        save(2, joined, joined_out),
+        save(3, slope, slope_out),
+        save(4, heads, heads_out),
+        save(5, chances, chances_out),
+    ]
+    for copy in saves:
+        copy.start()
+    for other in others:
+        pltpu.make_async_remote_copy(
+            src_ref=terms.at[other],
+            dst_ref=terms.at[other],
+            send_sem=term_send.at[other],
+            recv_sem=term_recv.at[other],
+            device_id={"tensor": other},
+            device_id_type=MESH,
+        ).wait_recv()
+    terms[here] = give[rows_of(here)]
+
+    def gather_terms(index, carry):
+        spot = pl.ds(pl.multiple_of(index * 16, 16), 16)
+        branch = terms[0, spot].astype(single)
+        for term in range(1, size):
+            branch = branch + terms[term, spot].astype(single)
+        newest[spot] = flows[3, spot].astype(single) + branch + small[8:9, :] + small[9:10, :]
+        return carry
+
+    lax.fori_loop(0, own // 16, gather_terms, 0)
+    for step in range(size):
+        for flow in FLOW_ORDER:
+            for side, way in sides:
+
+                @pl.when(jnp.logical_and(has_next(way), has_origin(way, step)))
+                def _():
+                    line_hop(side, way, step, flow).wait_send()
+
+    cube_in.drain()
+    cube_out.drain()
+    for other in others:
+        term_hop(other).wait_send()
+    for flow in FLOW_ORDER:
+        for block in range(size):
+            keep_flow(flow, block).wait()
+    save(0, w_in_low, all_in).wait()
+    save(1, w_out_low, all_out).wait()
+    for copy in saves:
+        copy.wait()
+
+
+def forward(flows, w_in, w_out, small, size, count, identity):
+    own = flows.shape[1]
+    length = own * size
+    rows, width_in = w_in.shape
+    width_out = w_out.shape[1]
+    head_width = HEADS // size * HD
+    units = FF // size
+    cosine, sine = rope_tables(length)
+    half = ROT // 2
+    blank = jnp.zeros((length, HD - ROT), single)
+    none = jnp.zeros((length, half), single)
+    rope = jnp.stack(
+        [
+            jnp.concatenate([cosine, blank + 1.0], axis=1),
+            jnp.concatenate([-sine[:, :half], none, blank], axis=1),
+            jnp.concatenate([none, sine[:, half:], blank], axis=1),
+        ]
+    )
+    pieces = count.bit_length() - 2
+    cube = [pltpu.SemaphoreType.DMA((pieces, 2**pieces))] * 8
+    low = lambda *shape: jax.ShapeDtypeStruct(shape, bfloat)
+    hbm = pl.BlockSpec(memory_space=pl.ANY)
+    vmem = pl.BlockSpec(memory_space=pltpu.VMEM)
+    return pl.pallas_call(
+        lambda *refs: forward_kernel(size, count, *refs),
+        out_shape=[
+            low(D, width_in),
+            low(D, width_out),
+            low(STREAMS, length, D),
+            low(length, width_out),
+            low(length, units),
+            low(3, length, head_width),
+            low(HEADS // size, length, length),
+            jax.ShapeDtypeStruct((own, D), single),
+        ],
+        in_specs=[vmem, hbm, hbm, vmem, vmem],
+        out_specs=[hbm] * 7 + [vmem],
+        scratch_shapes=[
+            pltpu.VMEM((D, width_in), bfloat),
+            pltpu.VMEM((D, width_out), bfloat),
+            pltpu.VMEM((STREAMS, length, D), bfloat),
+            pltpu.VMEM((3, length, head_width), bfloat),
+            pltpu.VMEM((HEADS // size, length, length), bfloat),
+            pltpu.VMEM((length, width_out), bfloat),
+            pltpu.VMEM((length, units), bfloat),
+            pltpu.VMEM((length, D), single),
+            pltpu.VMEM((length, D), bfloat),
+            pltpu.VMEM((size, own, D), bfloat),
+            pltpu.SemaphoreType.DMA((2,)),
+            pltpu.SemaphoreType.DMA((2, size, STREAMS)),
+            pltpu.SemaphoreType.DMA((2, size, STREAMS)),
+            pltpu.SemaphoreType.DMA((size,)),
+            pltpu.SemaphoreType.DMA((size,)),
+            pltpu.SemaphoreType.DMA((6,)),
+            pltpu.SemaphoreType.DMA((STREAMS, size)),
+        ]
+        + cube,
+        compiler_params=pltpu.CompilerParams(
+            collective_id=identity, has_side_effects=True, vmem_limit_bytes=60 * 2**20
+        ),
+        name="forward_%d" % identity,
+    )(flows, w_in, w_out, small, rope)
 
 
 def shards(
@@ -415,21 +945,15 @@
     own_rows = in_streams.shape[1]
     length = own_rows * groups
     up_rows = FF // D
-    block_rows = min(512, length)
-    block_count = length // block_rows
     score_scale = HD ** (-0.5)
     shard_rows = D // lax.axis_size("dp")
-    full_in, full_out = (
-        lax.all_gather(in_weights.astype(bfloat), "dp", axis=0, tiled=True),
-        lax.all_gather(out_weights.astype(bfloat), "dp", axis=0, tiled=True),
+    full_in, full_out, normed, joined, slope, heads, chances, newest = forward(
+        in_streams, in_weights, out_weights, small_params, groups, lax.axis_size("dp"), 0
+    )
+    queries, key_heads, value_heads = (
+        heads[part].reshape(length, heads_group, HD) for part in range(3)
     )
     gain_mix = small_params[4]
-    bias_heads = lax.dynamic_slice_in_dim(
-        small_params[5:8].reshape(3, HEADS, HD), group_index * heads_group, heads_group, 1
-    )
-    bias_units = lax.dynamic_slice_in_dim(
-        small_params[10 : 10 + up_rows].reshape(FF), group_index * units_group, units_group, 0
-    )
     mix_low = small_params[10 + up_rows :].astype(bfloat)
     flow_rows = in_streams.astype(single)
     centred = flow_rows - jnp.mean(flow_rows, axis=-1, keepdims=True)
@@ -438,56 +962,10 @@
     gain_all = jnp.stack([small_params[0], small_params[0], small_params[0], small_params[2]])[
         :, None, :
     ]
-    shift_all = jnp.stack([small_params[1], small_params[1], small_params[1], small_params[3]])[
-        :, None, :
-    ]
-    normed_own = (unit_flows * gain_all + shift_all).astype(bfloat)
-    normed = line_gather(normed_own, groups, 1, 0).reshape(STREAMS, length, D)
     attn_weights = full_in[:, :attn_width].reshape(D, heads_group, 3, HD)
     up_weights = full_in[:, attn_width:]
     cosine_table, sine_table = rope_tables(length)
 
-    def project(part_index):
-        return (
-            jnp.einsum(
-                "ld,dhe->lhe",
-                normed[part_index],
-                attn_weights[:, :, part_index, :],
-                preferred_element_type=single,
-            )
-            + bias_heads[part_index][None]
-        )
-
-    queries = rotate(project(0), cosine_table, sine_table).astype(bfloat)
-    key_heads = rotate(project(1), cosine_table, sine_table).astype(bfloat)
-    value_heads = project(2).astype(bfloat)
-    up_pre = jnp.dot(normed[3], up_weights, preferred_element_type=single) + bias_units
-    hidden = gelu_value(up_pre).astype(bfloat)
-
-    def forward_block(block_index):
-        first_row = block_index * block_rows
-        scores = (
-            jnp.einsum("qhe,khe->hqk", queries, key_heads, preferred_element_type=single)
-            * score_scale
-        )
-        scores = jnp.where(causal_mask(first_row, block_rows, length)[None], scores, masked_score)
-        row_top = jnp.max(scores, axis=-1, keepdims=True)
-        raised = jnp.exp(scores - row_top)
-        row_sum = jnp.sum(raised, axis=-1, keepdims=True)
-        weights_low = (raised / row_sum).astype(bfloat)
-        mixed_heads = jnp.einsum(
-            "hqk,khe->qhe", weights_low, value_heads, preferred_element_type=single
-        )
-        return (mixed_heads, (row_top + jnp.log(row_sum))[..., 0])
-
-    attended, log_sums = lax.map(forward_block, jnp.arange(block_count, dtype=jnp.int32))
-    attended = attended.reshape(length, heads_group, HD).astype(bfloat)
-    joined = jnp.concatenate([attended.reshape(length, proj_width), hidden], axis=1)
-    partial_value = contract_last(joined, full_out)
-    branch = line_scatter(
-        partial_value.astype(bfloat).reshape(1, groups, own_rows, D), groups, 4, 1
-    )[0]
-    newest = flow_rows[3] + branch + small_params[8] + small_params[9]
     inv_rms = lax.rsqrt(jnp.mean(newest * newest, axis=-1, keepdims=True) + mix_eps)
     mix_normed = (newest * inv_rms * gain_mix).astype(bfloat)
     mix_pre = contract_last(mix_normed, mix_low)
@@ -530,42 +1008,20 @@
     branch_grads = line_gather(d_newest.astype(bfloat)[None], groups, 4, 2).reshape(length, D)
     d_joined = jnp.dot(branch_grads, full_out, preferred_element_type=single)
     d_attended = d_joined[:, :proj_width].reshape(length, heads_group, HD).astype(bfloat)
-    d_up = (d_joined[:, proj_width:] * gelu_slope(up_pre)).astype(bfloat)
-
-    def backward_block(carried, block_index):
-        key_sum, value_sum = carried
-        first_row = block_index * block_rows
-        scores = (
-            jnp.einsum("qhe,khe->hqk", queries, key_heads, preferred_element_type=single)
-            * score_scale
-        )
-        scores = jnp.where(causal_mask(first_row, block_rows, length)[None], scores, masked_score)
-        chances = jnp.exp(scores - log_sums[block_index][..., None])
-        chances_low = chances.astype(bfloat)
-        d_chances = jnp.einsum(
-            "qhe,khe->hqk", d_attended, value_heads, preferred_element_type=single
-        )
-        centre = jnp.sum(d_chances * chances, axis=-1, keepdims=True)
-        d_scores = (chances * (d_chances - centre)).astype(bfloat)
-        d_picked = (
-            jnp.einsum("hqk,khe->qhe", d_scores, key_heads, preferred_element_type=single)
-            * score_scale
-        )
-        key_sum = (
-            key_sum
-            + jnp.einsum("hqk,qhe->khe", d_scores, queries, preferred_element_type=single)
-            * score_scale
-        )
-        value_sum = value_sum + jnp.einsum(
-            "hqk,qhe->khe", chances_low, d_attended, preferred_element_type=single
-        )
-        return ((key_sum, value_sum), d_picked)
-
-    zero_heads = jnp.zeros((length, heads_group, HD), single)
-    (d_key_heads, value_head_gradient), d_queries = lax.scan(
-        backward_block, (zero_heads, zero_heads), jnp.arange(block_count, dtype=jnp.int32)
-    )
-    d_queries = d_queries.reshape(length, heads_group, HD)
+    d_up = (d_joined[:, proj_width:] * slope).astype(bfloat)
+
+    d_chances = jnp.einsum("qhe,khe->hqk", d_attended, value_heads, preferred_element_type=single)
+    centre = jnp.sum(d_chances * chances, axis=-1, keepdims=True)
+    d_scores = (chances * (d_chances - centre)).astype(bfloat)
+    d_queries = (
+        jnp.einsum("hqk,khe->qhe", d_scores, key_heads, preferred_element_type=single) * score_scale
+    )
+    d_key_heads = (
+        jnp.einsum("hqk,qhe->khe", d_scores, queries, preferred_element_type=single) * score_scale
+    )
+    value_head_gradient = jnp.einsum(
+        "hqk,qhe->khe", chances, d_attended, preferred_element_type=single
+    )
     d_pre_q = rotate_back(d_queries, cosine_table, sine_table).astype(bfloat)
     d_pre_k = rotate_back(d_key_heads, cosine_table, sine_table).astype(bfloat)
     d_pre_v = value_head_gradient.astype(bfloat)

time: 741 us -> 703 us (0.949)
  matrix products: 113 us -> 81.3 us
  other arithmetic: 104 us -> 78.4 us
  Pallas kernels: 386 us -> 401 us
    pallas_call x0 -> x1, Pallas kernels: none -> 187 us  [forward(): pl.pallas_call(lambda *refs: forward_kernel(size, count, *refs), out_shap...]
    pallas_call x2 -> x1, Pallas kernels: 179 us -> 38.3 us  [line_gather(): pl.pallas_call(lambda *refs: line_gather_kernel(size, chunks, *refs), out...]
    pallas_call x2 -> x1, Pallas kernels: 174 us -> 139 us  [line_scatter(): pl.pallas_call(lambda *refs: line_scatter_kernel(size, chunks, *refs), ou...]
    dot_general x8 -> x4, matrix products: 27.3 us -> 3.78 us  [the longest x1 2.09 us: shards(): jnp.einsum('qhe,khe->hqk', d_attended, value_heads, preferred_element_typ...]
    convert_element_type x5 -> x1, other arithmetic: 13.3 us -> 0.62 us  [shards(): d_scores = (chances * (d_chances - centre)).astype(bfloat)]
    slice x1 -> x2, local copies, waits for them, and re-layouts: 3.36 us -> 14.9 us  [shards(): attn_weights = full_in[:, :attn_width].reshape(D, heads_group, 3, HD)]
    dot_general x3 -> x2, matrix products: 17.8 us -> 8.84 us  [contract_last(): lax.dot_general(left_side, right_side, (((left_side.ndim - 1,), (right_si...]
    unnamed x224 -> x114, local copies, waits for them, and re-layouts: 63 us -> 55.8 us
  transfers between devices with their start and end apart: 4 -> 2, of which waited for: 0 -> 0; matrix products, arithmetic and copies ran while one was open for 24% -> 21% of each run, Pallas kernels for 38% -> 20%
where the time goes in v2:
time: 703 us; the launch traced here: 693 us
  Pallas kernels  401 us (57%)
  local copies, waits for them, and re-layouts  112 us (16%)
  matrix products  81.3 us (12%)
  other arithmetic  78.4 us (11%)
  between operations  19.9 us (3%)
    pallas_call x1, Pallas kernels, forward(): pl.pallas_call(lambda *refs: forward_kernel(size, count, *refs), out_shap...  187 us
    pallas_call x1, Pallas kernels, line_scatter(): pl.pallas_call(lambda *refs: line_scatter_kernel(size, chunks, *refs), ou...  139 us
    unnamed x114, local copies, waits for them, and re-layouts  55.8 us
    pallas_call x1, Pallas kernels, line_gather(): pl.pallas_call(lambda *refs: line_gather_kernel(size, chunks, *refs), out...  38.3 us
    pallas_call x1, Pallas kernels, cube_sum(): pl.pallas_call(lambda *refs: cube_sum_kernel(bits, *refs), out_shape=jax....  36.2 us
    dot_general x3, matrix products, contract_first(): lax.dot_general(left_side, right_side, (((0,), (0,)), ((), ())), preferre...  17.6 us
    concatenate x1, other arithmetic, shards(): grad_in = owned(jnp.concatenate([attn_part, up_part], axis=1))  17.3 us
    slice x2, local copies, waits for them, and re-layouts, shards(): attn_weights = full_in[:, :attn_width].reshape(D, heads_group, 3, HD)  14.9 us
  transfers between devices with their start and end apart: 2, of which 0 were waited for; matrix products, arithmetic and copies ran while one was open for 21% of the time, Pallas kernels for 20%

profile of v2, /device:TPU:0, one launch (start us, length us, event | category | flops | bytes accessed | tf_op | source)
XLA Modules:
  0.0 692.8 jit_solution(10983413502226360366)
XLA Ops:
  10.7 187.4 %forward_0.1 = (bf16[2048,3584]{1,0:T(8,128)(2,1)}, bf16[2048,2560]{1,0:T(8,128)(2,1)}, bf16[4,512,2048]{2,1,0:T(8,128)(2,1)}, bf16[512,2560]{1,0:T(8,128)(2,1)}...) custom-call(bf16[4,128,2048]{2,1,0:T(8,128)(2,1)} %refs_0_.1, ...), custom_call_target="tpu_custom_call" | custom-call | tf_op jit(solution)/shard_map/forward_0/pallas_call | solution.py:877
  201.5 8.6 %convolution_bitcast_fusion = f32[128,4,1]{2,1,0:T(4,128)S(1)} fusion(bf16[4,128,2048]{2,1,0:T(8,128)(2,1)S(1)} %copy-done.15, f32[128,2048,1]{1,0,2:T(8,128)S(1)} %bitcast.215), kind=kOutput, calls=%fused_computation.74 | convolution fusion | flops 12582912 | bytes 3147776 | tf_op jit(solution)/shard_map/srd,rd->rs/dot_general | solution.py:988
  216.1 11.5 %fusion.43 = f32[128,9,2048]{2,1,0:T(8,128)} fusion(f32[128,4,9]{2,1,0:T(4,128)S(1)} %copy.219, bf16[4,128,2048]{2,1,0:T(8,128)(2,1)} %param.21), kind=kOutput, calls=%fused_computation.80 | convolution fusion | flops 113246208 | bytes 11552768 | tf_op jit(solution)/shard_map/rsj,srd->jrd/dot_general | solution.py:990
  227.6 14.8 %copy.299 = f32[128,9,2048]{2,0,1:T(8,128)} copy(f32[128,9,2048]{2,1,0:T(8,128)} %fusion.43) | data formatting | bytes 18874368 | tf_op jit(solution)/shard_map/rsj,srd->jrd/dot_general | solution.py:990
  246.4 38.3 %line_gather_2.1 = bf16[1,4,128,2048]{3,2,1,0:T(8,128)(2,1)} custom-call(bf16[1,128,2048]{2,1,0:T(8,128)(2,1)} %convert_bitcast_fusion.1.refs_0_), custom_call_target="tpu_custom_call" | custom-call | bytes 41943040 | tf_op jit(solution)/shard_map/line_gather_2/pallas_call | solution.py:182
  284.7 10.3 %convolution_convert_fusion = bf16[2048,2560]{1,0:T(8,128)(2,1)} fusion(bf16[512,2048]{1,0:T(8,128)(2,1)} %bitcast.226, bf16[512,2560]{1,0:T(8,128)(2,1)} %get-tuple-element.37), kind=kOutput, calls=%fused_computation.1 | convolution fusion | flops 5373952000 | bytes 15204352 | tf_op jit(solution)/shard_map/dot_general | solution.py:82
  296.5 8.6 %fusion.102 = f32[512,2560]{1,0:T(8,128)S(1)} fusion(bf16[512,2048]{1,0:T(8,128)(2,1)S(1)} %bitcast.227, bf16[2048,2560]{1,0:T(8,128)(2,1)} %get-tuple-element.33), kind=kOutput, calls=%fused_computation.207 | convolution fusion | flops 5368709120 | bytes 17825792 | tf_op jit(solution)/shard_map/dot_general | solution.py:1009
  326.8 6.4 convert_bitcast_fusion
  338.1 7.2 %convolution_convert_fusion.1 = bf16[2048,2048]{0,1:T(8,128)(2,1)S(1)} fusion(bf16[512,2048]{1,0:T(8,128)(2,1)S(1)} %get-tuple-element.195, bf16[4,512,2048]{2,1,0:T(8,128)(2,1)} %get-tuple-element.36), kind=kOutput, calls=%fused_computation.7 | convolution fusion | flops 4299161600 | bytes 12582912 | tf_op jit(solution)/shard_map/dot_general | solution.py:82
  345.3 17.3 %pad_maximum_fusion = bf16[2048,3584]{0,1:T(8,128)(2,1)} fusion(bf16[2048,2048]{0,1:T(8,128)(2,1)S(1)} %convolution_convert_fusion.1, bf16[2048,1536]{0,1:T(8,128)(2,1)S(1)} %bitcast.216), kind=kLoop, calls=%fused_computation | loop fusion | flops 29360128 | bytes 29360128 | tf_op jit(solution)/shard_map/concatenate | solution.py:1093
  365.0 5.1 copy.246
  370.2 6.3 slice.361
  377.8 6.0 slice.218
  383.8 9.0 %copy.231 = bf16[2048,1536]{0,1:T(8,128)(2,1)} copy(bf16[2048,1536]{1,0:T(8,128)(2,1)} %slice.218) | data formatting | bytes 12582912 | tf_op jit(solution)/shard_map/slice | solution.py:965
  403.1 8.5 %fusion.27 = bf16[512,2048]{1,0:T(8,128)(2,1)S(1)} fusion(bf16[512,2048]{1,0:T(8,128)(2,1)S(1)} %copy-done.21, bf16[2048,3584]{1,0:T(8,128)(2,1)} %get-tuple-element.34), kind=kOutput, calls=%fused_computation.53 | convolution fusion | flops 4296015872 | bytes 12582912 | tf_op jit(solution)/shard_map/dot_general | solution.py:73
  416.1 138.7 %line_scatter_3.1 = f32[4,128,2048]{2,1,0:T(8,128)} custom-call(bf16[4,4,128,2048]{3,2,1,0:T(8,128)(2,1)} %pad_maximum_fusion.1.refs_0_), custom_call_target="tpu_custom_call" | custom-call | bytes 167772160 | tf_op jit(solution)/shard_map/line_scatter_3/pallas_call | solution.py:289
  555.1 5.1 copy.243
  560.3 5.1 copy.244
  565.4 5.3 copy.247
  593.6 36.2 %cube_sum_4.1 = f32[64,2048]{1,0:T(8,128)S(1)} custom-call(f32[64,2048]{1,0:T(8,128)S(1)} %concatenate.104.refs_0_), custom_call_target="tpu_custom_call" | custom-call | tf_op jit(solution)/shard_map/cube_sum_4/pallas_call | solution.py:367
  633.9 8.8 %fusion.87 = (bf16[256,3584]{0,1:T(8,128)(2,1)S(1)}, f32[256,3584]{0,1:T(8,128)}, f32[256,3584]{0,1:T(8,128)}, f32[256,3584]{0,1:T(8,128)}) fusion(f32[256,3584]{0,1:T(8,128)} %copy.246, f32[]{:T(128)S(6)} %div.89, bf16[256,3584]{0,1:T(8,128)(2,1)} %reduce-scatter.3.cloned.1.call-done, f32[256,3584]{0,1:T(8,128)} %copy.243, f32[256,3584]{0,1:T(8,128)} %copy.244), kind=kLoop, calls=%fused_computation.194 | loop fusion | flops 16515072 | bytes 25690116 | tf_op jit(solution)/shard_map/convert_element_type | solution.py:1136
  642.7 5.1 copy.248
  647.8 5.5 add_multiply_fusion
  671.4 8.1 %fusion.84 = (bf16[256,2560]{1,0:T(8,128)(2,1)}, f32[256,2560]{1,0:T(8,128)S(1)}, f32[256,2560]{1,0:T(8,128)}, f32[256,2560]{1,0:T(8,128)}) fusion(f32[256,2560]{1,0:T(8,128)} %refs_2_.1, f32[]{:T(128)S(6)} %div.89, bf16[256,2560]{1,0:T(8,128)(2,1)} %reduce-scatter.5.cloned.1.call-done, f32[256,2560]{1,0:T(8,128)} %param.27, f32[256,2560]{1,0:T(8,128)} %param.28), kind=kLoop, calls=%fused_computation.193 | loop fusion | flops 11796480 | bytes 18350084 | tf_op jit(solution)/shard_map/convert_element_type | solution.py:1141
  (212 shorter events, 109.9 us)
Async XLA Ops:
  7.2 578.8 %reduce-scatter.5.cloned.1.call-start = ((), (), s32[]{:S(2)}) async-start(), calls=%async_computation.3 | async-start | bytes 11796480 | tf_op jit(solution)/shard_map/reduce_scatter | solution.py:1088
  10.7 190.3 %copy-start.16 = (f32[50,2048]{1,0:T(8,128)S(1)}, f32[50,2048]{1,0:T(8,128)}, u32[]{:S(2)}) copy-start(f32[50,2048]{1,0:T(8,128)} %refs_3_.1) | copy-start | bytes 1228804
  201.1 9.0 %copy-start.25 = (bf16[128,2048]{1,0:T(8,128)(2,1)}, bf16[128,2048]{1,0:T(8,128)(2,1)S(1)}, u32[]{:S(2)}) copy-start(bf16[128,2048]{1,0:T(8,128)(2,1)S(1)} %multiply_convert_fusion) | copy-start | bytes 1572868
  201.4 14.2 %copy-start.47 = (f32[128,36]{0,1:T(8,128)}, f32[128,36]{0,1:T(8,128)S(1)}, u32[]{:S(2)}) copy-start(f32[128,36]{0,1:T(8,128)S(1)} %get-tuple-element.241) | copy-start | bytes 55300
  201.5 8.6 %copy-start.13 = (bf16[8,128,2048]{2,1,0:T(8,128)(2,1)S(1)}, bf16[8,128,2048]{2,1,0:T(8,128)(2,1)}, u32[]{:S(2)}) copy-start(bf16[8,128,2048]{2,1,0:T(8,128)(2,1)} %param.20) | copy-start | bytes 12582916
  210.1 4.3 copy-start.40
  214.4 13.2 %copy-start.38 = (f32[128,36]{0,1:T(8,128)}, f32[128,36]{0,1:T(8,128)S(1)}, u32[]{:S(2)}) copy-start(f32[128,36]{0,1:T(8,128)S(1)} %reshape.262) | copy-start | bytes 55300
  215.9 11.7 %copy-start.36 = (f32[128,4,9]{0,2,1:T(8,128)}, f32[128,4,9]{0,2,1:T(8,128)S(1)}, u32[]{:S(2)}) copy-start(f32[128,4,9]{0,2,1:T(8,128)S(1)} %reshape.261) | copy-start | bytes 55300
  295.0 293.7 %reduce-scatter.3.cloned.1.call-start = ((), (), s32[]{:S(2)}) async-start(), calls=%async_computation.2 | async-start | bytes 16515072 | tf_op jit(solution)/shard_map/reduce_scatter | solution.py:1088
  309.2 11.3 %copy-start.3 = (bf16[4,512,512]{2,1,0:T(8,128)(2,1)S(1)}, bf16[4,512,512]{2,1,0:T(8,128)(2,1)}, u32[]{:S(2)}) copy-start(bf16[4,512,512]{2,1,0:T(8,128)(2,1)} %get-tuple-element.32) | copy-start | bytes 6291460
  326.5 6.7 copy-start.9
  338.1 7.2 %copy-start.20 = (bf16[512,2048]{1,0:T(8,128)(2,1)}, bf16[512,2048]{1,0:T(8,128)(2,1)S(1)}, u32[]{:S(2)}) copy-start(bf16[512,2048]{1,0:T(8,128)(2,1)S(1)} %get-tuple-element.195) | copy-start | bytes 6291460
  370.2 6.4 copy-start.39
  370.2 6.4 copy-start.48
  370.2 7.3 %copy-start.10 = (bf16[4,128,512]{2,1,0:T(8,128)(2,1)S(1)}, bf16[4,128,512]{2,1,0:T(8,128)(2,1)}, u32[]{:S(2)}) copy-start(bf16[4,128,512]{2,1,0:T(8,128)(2,1)} %copy-done.9) | copy-start | bytes 1572868
  370.2 7.3 %copy-start.28 = (bf16[512,4,1,96]{0,3,1,2:T(8,128)(2,1)S(1)}, bf16[512,4,1,96]{0,3,1,2:T(8,128)(2,1)}, u32[]{:S(2)}) copy-start(bf16[512,4,1,96]{0,3,1,2:T(8,128)(2,1)} %copy-done.27) | copy-start | bytes 1179652
  370.2 7.3 %copy-start.30 = (bf16[512,4,32]{0,2,1:T(8,128)(2,1)S(1)}, bf16[512,4,32]{0,2,1:T(8,128)(2,1)}, u32[]{:S(2)}) copy-start(bf16[512,4,32]{0,2,1:T(8,128)(2,1)} %copy-done.29) | copy-start | bytes 393220
  370.2 7.3 %copy-start.32 = (bf16[512,4,32]{0,2,1:T(8,128)(2,1)S(1)}, bf16[512,4,32]{0,2,1:T(8,128)(2,1)}, u32[]{:S(2)}) copy-start(bf16[512,4,32]{0,2,1:T(8,128)(2,1)} %copy-done.31) | copy-start | bytes 393220
  396.1 7.0 %copy-start.21 = (bf16[512,2048]{1,0:T(8,128)(2,1)S(1)}, bf16[512,2048]{1,0:T(8,128)(2,1)}, u32[]{:S(2)}) copy-start(bf16[512,2048]{1,0:T(8,128)(2,1)} %copy-done.20) | copy-start | bytes 6291460
  565.4 5.3 copy-start
  581.8 11.2 %copy-start.44 = (f32[1332]{0:T(1024)S(1)}, f32[1332]{0:T(1024)}, u32[]{:S(2)}) copy-start(f32[1332]{0:T(1024)} %reshape.270) | copy-start | bytes 15988
  581.8 11.3 %copy-start.42 = (f32[2048]{0:T(1024)S(1)}, f32[2048]{0:T(1024)}, u32[]{:S(2)}) copy-start(f32[2048]{0:T(1024)} %get-tuple-element.196) | copy-start | bytes 24580
  581.8 11.3 %copy-start.43 = (f32[2048]{0:T(1024)S(1)}, f32[2048]{0:T(1024)}, u32[]{:S(2)}) copy-start(f32[2048]{0:T(1024)} %get-tuple-element.174) | copy-start | bytes 24580
  671.4 8.1 %copy-start.18 = (f32[256,2560]{1,0:T(8,128)S(1)}, f32[256,2560]{1,0:T(8,128)}, u32[]{:S(2)}) copy-start(f32[256,2560]{1,0:T(8,128)} %param.29) | copy-start | bytes 7864324
  (30 other events, 54.2 us)
Sparse Core Ops, SparseCore 0:
  295.1 83.2 reduce-scatter.4
  381.9 103.5 reduce-scatter.2

commit v3 on v2

v3 whole, which is shorter than its diff:
```python
import jax
import jax.numpy as jnp
import numpy as np
from jax import lax
from jax.experimental import pallas as pl
from jax.experimental.pallas import tpu as pltpu
from jax.sharding import PartitionSpec as P

D = 2048
HEADS = 16
HD = 128
ROT = 32
FF = 8192
STREAMS = 4
LAYER = 8
STEP = 10
LAYERS = 9
MIXH = 36


norm_eps = 1e-05
mix_eps = 1e-06
beta_first = 0.9
beta_second = 0.95
adam_eps = 1e-08
decay_rate = 0.01
learn_rate = 0.03
small_rate = 0.2
clip_norm = 1.0
average_keep = 0.5
masked_score = -1e30
highest_precision = lax.Precision.HIGHEST
bfloat = jnp.bfloat16
single = jnp.float32
MESH = pl.DeviceIdType.MESH


def contract_last(left_side, right_side):
    return lax.dot_general(
        left_side,
        right_side,
        (((left_side.ndim - 1,), (right_side.ndim - 1,)), ((), ())),
        preferred_element_type=single,
    )


def contract_first(left_side, right_side):
    return lax.dot_general(
        left_side, right_side, (((0,), (0,)), ((), ())), preferred_element_type=single
    )


def adamw_step(weight, moment, second, average, gradient, factor, rate):
    clipped = gradient * factor
    moment = beta_first * moment + (1.0 - beta_first) * clipped
    second = beta_second * second + (1.0 - beta_second) * clipped * clipped
    step_ratio = (
        moment
        / (1.0 - beta_first**STEP)
        / (jnp.sqrt(second / (1.0 - beta_second**STEP)) + adam_eps)
    )
    weight = weight - rate * (step_ratio + decay_rate * weight)
    average = average_keep * average + (1.0 - average_keep) * weight
    return (weight, moment, second, average)


def enter(partners):
    barrier = pltpu.get_barrier_semaphore()
    for present, device in partners:

        @pl.when(present)
        def _():
            pl.semaphore_signal(barrier, inc=1, device_id=device, device_id_type=MESH)

    pl.semaphore_wait(barrier, sum(present.astype(jnp.int32) for present, _ in partners))


class LineSum:
    def __init__(self, size, give, landing, send_sem, recv_sem, cut):
        self.size, self.give, self.landing = size, give, landing
        self.send_sem, self.recv_sem, self.cut = send_sem, recv_sem, cut
        self.here = lax.axis_index("tensor")
        self.own = landing.shape[1]
        self.rows = self.own // cut
        self.near = lax.select(2 * self.here < size, 1, -1)

    def has_next(self, way):
        return jnp.logical_and(self.here + way >= 0, self.here + way < self.size)

    def spot(self, dest, place):
        return pl.ds(pl.multiple_of(dest * self.own + place * self.rows, 16), self.rows)

    def landed(self, way, dest, place):
        rows = pl.ds(pl.multiple_of(place * self.rows, 16), self.rows)
        return self.landing.at[dest + (1 + way) // 2, rows]

    def hop(self, way, dest, place):
        return pltpu.make_async_remote_copy(
            src_ref=self.give.at[self.spot(dest, place)],
            dst_ref=self.landed(way, dest, place),
            send_sem=self.send_sem.at[(1 - way) // 2, dest, place],
            recv_sem=self.recv_sem.at[(1 - way) // 2, dest, place],
            device_id={"tensor": self.here + way},
            device_id_type=MESH,
        )

    def arrive(self, way, dest, place):
        block = self.landed(way, dest, place)
        pltpu.make_async_remote_copy(
            src_ref=block,
            dst_ref=block,
            send_sem=self.send_sem.at[(1 - way) // 2, dest, place],
            recv_sem=self.recv_sem.at[(1 - way) // 2, dest, place],
            device_id={"tensor": self.here - way},
            device_id_type=MESH,
        ).wait_recv()

    def relay(self, way, dest):
        @pl.when((dest - self.here) * way > 0)
        def _():
            def one(place, carry):
                @pl.when(self.has_next(-way))
                def _():
                    self.arrive(way, dest, place)
                    spot = self.spot(dest, place)
                    self.give[spot] = (
                        self.give[spot].astype(single)
                        + self.landed(way, dest, place)[...].astype(single)
                    ).astype(bfloat)

                self.hop(way, dest, place).start()
                return carry

            lax.fori_loop(0, self.cut, one, 0)

    def far(self, rank, way):
        return (self.size - 1) * ((1 + way) // 2) - rank * way

    def collect(self, place, into):
        rows = pl.ds(place * self.rows, self.rows)
        into[rows] = self.give[self.spot(self.here, place)].astype(single)
        for way in (1, -1):

            @pl.when(self.has_next(-way))
            def _():
                self.arrive(way, self.here, place)
                into[rows] += self.landed(way, self.here, place)[...].astype(single)

    def drain(self):
        for rank in range(self.size - 1):
            for way in (1, -1):
                dest = self.far(rank, way)

                @pl.when((dest - self.here) * way > 0)
                def _():
                    for place in range(self.cut):
                        self.hop(way, dest, place).wait_send()


def cube_sum_steps(bits, value, out, total, landing, send_a, recv_a, send_b, recv_b):
    rows, columns = value.shape

    def partner(axis, size):
        place = lax.axis_index(axis)
        bit = lax.rem(place // size, 2)
        return bit, {axis: place + (1 - 2 * bit) * size}

    ends = [partner(*entry) for entry in bits]
    enter([(jnp.bool_(True), device) for _, device in ends])
    total[...] = value[...]
    regions = [(0, rows, 0, columns)]
    for step, (bit, device) in enumerate(ends):
        r, n, c, m = regions[-1]
        if n > 8:
            n = n // 2
            keep, give = (r + bit * n, n, c, m), (r + (1 - bit) * n, n, c, m)
        else:
            m = m // 2
            keep, give = (r, n, c + bit * m, m), (r, n, c + (1 - bit) * m, m)
        regions.append(keep)

        def spot(region):
            return (
                pl.ds(pl.multiple_of(region[0], 8), region[1]),
                pl.ds(pl.multiple_of(region[2], 128), region[3]),
            )

        copy = pltpu.make_async_remote_copy(
            src_ref=total.at[spot(give)],
            dst_ref=landing.at[step, pl.ds(0, n), pl.ds(0, m)],
            send_sem=send_a.at[step],
            recv_sem=recv_a.at[step],
            device_id=device,
            device_id_type=MESH,
        )
        copy.start()
        copy.wait()
        total[spot(keep)] += landing[step, pl.ds(0, n), pl.ds(0, m)]
    out[spot(regions[-1])] = total[spot(regions[-1])]
    for step in range(len(ends) - 1, -1, -1):
        region = out.at[spot(regions[step + 1])]
        copy = pltpu.make_async_remote_copy(
            src_ref=region,
            dst_ref=region,
            send_sem=send_b.at[step],
            recv_sem=recv_b.at[step],
            device_id=ends[step][1],
            device_id_type=MESH,
        )
        copy.start()
        copy.wait()


def axis_bits(axis):
    return [(axis, 2**bit) for bit in range(lax.axis_size(axis).bit_length() - 1)]


def plus_flips(place, bits):
    moved = place
    for bit in bits:
        moved = moved + (1 - 2 * lax.rem(place // 2**bit, 2)) * 2**bit
    return moved


def cube_routes(count):
    bits = list(range(1, count))
    pieces = []
    for turn in range(len(bits)):
        order = bits[turn:] + bits[:turn]
        arrivals = [()]
        steps = []
        for bit in order:
            fresh = [tuple(sorted(held + (bit,))) for held in arrivals]
            steps.append([(bit, held, whole) for held, whole in zip(arrivals, fresh)])
            arrivals = arrivals + fresh
        pieces.append((arrivals, steps))
    return pieces


class CubeGather:
    def __init__(self, whole, rows, count, sems):
        self.whole, self.rows, self.count = whole, rows, count
        self.send_sem, self.recv_sem, self.pair_send, self.pair_recv = sems
        self.routes = cube_routes(count.bit_length() - 1)
        self.me = lax.axis_index("dp")
        self.piece_rows = rows // len(self.routes)

    def region(self, piece, held):
        first = plus_flips(self.me, held) * self.rows + piece * self.piece_rows
        return self.whole.at[pl.ds(pl.multiple_of(first, 16), self.piece_rows)]

    def hop(self, piece, bit, held, slot, pair=False):
        block = self.region(piece, held)
        return pltpu.make_async_remote_copy(
            src_ref=block,
            dst_ref=block,
            send_sem=(self.pair_send if pair else self.send_sem).at[piece, slot],
            recv_sem=(self.pair_recv if pair else self.recv_sem).at[piece, slot],
            device_id={"dp": plus_flips(self.me, (bit,))},
            device_id_type=MESH,
        )

    def slot(self, piece, held):
        return self.routes[piece][0].index(held)

    def sends_of(self, piece, held):
        found = []
        for step in self.routes[piece][1]:
            for bit, source, landed in step:
                if source == held:
                    found.append(self.hop(piece, bit, held, self.slot(piece, landed)))
        found.append(self.hop(piece, 0, held, self.slot(piece, held), True))
        return found

    def start(self):
        for piece in range(len(self.routes)):
            for copy in self.sends_of(piece, ()):
                copy.start()

    def step(self, index):
        for piece, (_, steps) in enumerate(self.routes):
            for bit, _, landed in steps[index]:
                self.hop(piece, bit, landed, self.slot(piece, landed)).wait_recv()
                for copy in self.sends_of(piece, landed):
                    copy.start()

    def steps(self):
        return len(self.routes)

    def finish(self):
        for piece, (arrivals, _) in enumerate(self.routes):
            for held in arrivals:
                self.hop(piece, 0, (0,) + held, self.slot(piece, held), True).wait_recv()

    def drain(self):
        for piece, (arrivals, _) in enumerate(self.routes):
            for held in arrivals:
                for copy in self.sends_of(piece, held):
                    copy.wait_send()


FLOW_ORDER = (1, 2, 3, 0)
CUT = 4
SMALL_MIX = 10 + FF // D


def rope_lanes(length):
    half = ROT // 2
    inverse = 10000.0 ** (-2.0 * np.arange(half) / ROT)
    angles = np.arange(length)[:, None] * inverse[None, :]
    tables = np.zeros((3, length, HD), np.float32)
    tables[0] = 1.0
    tables[0, :, :half] = tables[0, :, half:ROT] = np.cos(angles)
    tables[1, :, :half] = -np.sin(angles)
    tables[2, :, half:ROT] = np.sin(angles)
    return tables


def forward_kernel(
    size,
    count,
    flows,
    w_in,
    w_out,
    small,
    rope,
    stored,
    cotangent,
    mix,
    all_in,
    all_out,
    all_normed,
    joined_out,
    slope_out,
    heads_out,
    chances_out,
    newest,
    d_newest,
    d_branch,
    weights,
    row_grads,
    mix_in_grad,
    mix_out_grad,
    w_in_low,
    w_out_low,
    normed,
    heads,
    chances,
    joined,
    slope,
    total,
    give,
    terms,
    back,
    earlier,
    dots,
    scales,
    sums,
    mix_low,
    mix_table,
    stage_sem,
    back_sem,
    earlier_sem,
    line_send,
    line_recv,
    term_send,
    term_recv,
    save_sem,
    flow_sem,
    *cube_sems,
):
    here = lax.axis_index("tensor")
    me = lax.axis_index("dp")
    own = flows.shape[1]
    rows_in = w_in.shape[0]
    length = own * size
    width_in, width_out = w_in.shape[1], w_out.shape[1]
    head_width = heads.shape[2]
    group_heads = head_width // HD
    attn_width = 3 * head_width
    units = width_in - attn_width
    bits = count.bit_length() - 1
    sides = ((0, 1), (1, -1))
    tile = 512

    def rows_of(block):
        return pl.ds(pl.multiple_of(block * own, own), own)

    def stage(source, width):
        spans = [(0, min(width, D))] + ([(D, width - D)] if width > D else [])
        return [
            pltpu.make_async_copy(
                source.at[:, pl.ds(first, span)],
                total.at[pl.ds(place * rows_in, rows_in), pl.ds(0, span)],
                stage_sem.at[place],
            )
            for place, (first, span) in enumerate(spans)
        ]

    def settle(source, width, target):
        for place, copy in enumerate(stage(source, width)):
            copy.wait()
            span = min(D, width - place * D)

            def cast(index, carry):
                low = pl.multiple_of(index * 16, 16)
                into = pl.multiple_of(me * rows_in + index * 16, 16)
                target[pl.ds(into, 16), pl.ds(place * D, span)] = total[
                    pl.ds(place * rows_in + low, 16), pl.ds(0, span)
                ].astype(bfloat)
                return carry

            lax.fori_loop(0, rows_in // 16, cast, 0)

    for copy in stage(w_in, width_in):
        copy.start()
    load_back = pltpu.make_async_copy(cotangent, back, back_sem)
    load_back.start()

    def load_earlier(layer):
        return pltpu.make_async_copy(
            stored.at[layer], earlier.at[layer % 2], earlier_sem.at[layer % 2]
        )

    load_earlier(0).start()
    enter(
        [(here < size - 1, {"tensor": here + 1}), (here > 0, {"tensor": here - 1})]
        + [(jnp.bool_(True), {"dp": plus_flips(me, (bit,))}) for bit in range(bits)]
    )

    def line_hop(side, way, step, flow):
        block = normed.at[flow, rows_of(here - way * step)]
        return pltpu.make_async_remote_copy(
            src_ref=block,
            dst_ref=block,
            send_sem=line_send.at[side, step, flow],
            recv_sem=line_recv.at[side, step, flow],
            device_id={"tensor": here + way},
            device_id_type=MESH,
        )

    def line_landed(side, way, step, flow):
        block = normed.at[flow, rows_of(here - way * step)]
        return pltpu.make_async_remote_copy(
            src_ref=block,
            dst_ref=block,
            send_sem=line_send.at[side, step - 1, flow],
            recv_sem=line_recv.at[side, step - 1, flow],
            device_id={"tensor": here - way},
            device_id_type=MESH,
        )

    def has_next(way):
        return here < size - 1 if way > 0 else here > 0

    def has_origin(way, step):
        return here >= step if way > 0 else here < size - step

    def keep_flow(flow, block):
        return pltpu.make_async_copy(
            normed.at[flow, rows_of(block)],
            all_normed.at[flow, rows_of(block)],
            flow_sem.at[flow, block],
        )

    for flow in FLOW_ORDER:
        which = 2 if flow == 3 else 0

        def normalize(index, carry):
            spot = pl.ds(pl.multiple_of(index * 16, 16), 16)
            values = flows[flow, spot].astype(single)
            centred = values - jnp.mean(values, axis=-1, keepdims=True)
            inverse = lax.rsqrt(jnp.mean(centred * centred, axis=-1, keepdims=True) + norm_eps)
            into = pl.ds(pl.multiple_of(here * own + index * 16, 16), 16)
            normed[flow, into] = (
                centred * inverse * small[which : which + 1, :] + small[which + 1 : which + 2, :]
            ).astype(bfloat)
            return carry

        lax.fori_loop(0, own // 16, normalize, 0)
        if flow:
            for side, way in sides:
                pl.when(has_next(way))(line_hop(side, way, 0, flow).start)
        keep_flow(flow, here).start()

    cube_in = CubeGather(w_in_low, rows_in, count, cube_sems[:4])
    cube_out = CubeGather(w_out_low, rows_in, count, cube_sems[4:])
    settle(w_in, width_in, w_in_low)
    cube_in.start()
    for copy in stage(w_out, width_out):
        copy.start()
    settle(w_out, width_out, w_out_low)
    mix_low[...] = jnp.zeros_like(mix_low)
    mix_low[0:MIXH] = small[SMALL_MIX : SMALL_MIX + MIXH].astype(bfloat)
    mix_table[...] = jnp.zeros_like(mix_table)
    mix_table[0:MIXH, 0:MIXH] = mix[0:MIXH]
    mix_table[HD : HD + 1, 0:MIXH] = mix[MIXH : MIXH + 1]
    lane = lax.broadcasted_iota(jnp.int32, (16, HD), 1)
    load_back.wait()
    for layer in range(LAYER):
        if layer + 1 < LAYER:
            load_earlier(layer + 1).start()
        load_earlier(layer).wait()

        def correlate(index, carry):
            spot = pl.ds(pl.multiple_of(index * 16, 16), 16)
            held = earlier[layer % 2, spot].astype(single)
            found = jnp.zeros((16, HD), single) if layer == 0 else dots[spot]
            for stream in range(STREAMS):
                value = jnp.sum(back[stream, spot].astype(single) * held, axis=-1, keepdims=True)
                found = found + jnp.where(lane == stream * LAYERS + layer, value, 0.0)
            dots[spot] = found
            return carry

        lax.fori_loop(0, own // 16, correlate, 0)

    def line_step(step, flow_list):
        for flow in flow_list:
            for side, way in sides:

                @pl.when(has_origin(way, step))
                def _():
                    line_landed(side, way, step, flow).wait_recv()
                    pl.when(has_next(way))(line_hop(side, way, step, flow).start)
                    keep_flow(flow, here - way * step).start()

    def at_distance(step, action):
        if step == 0:
            action(here)
            return

        def one(side, carry):
            block = here - step + 2 * step * side

            @pl.when(jnp.logical_and(block >= 0, block < size))
            def _():
                action(block)

            return carry

        lax.fori_loop(0, 2, one, 0)

    def project(block, part):
        rows = rows_of(block)
        source = normed[part, rows]
        pre = jnp.dot(
            source,
            jnp.concatenate(
                [
                    w_in_low[:, pl.ds((head * 3 + part) * HD, HD)]
                    for head in range(group_heads)
                ],
                axis=1,
            ),
            preferred_element_type=single,
        )
        first = pl.multiple_of(here * head_width, HD)
        pre = pre + small[5 + part : 6 + part, pl.ds(first, head_width)]
        if part == 2:
            heads[part, rows] = pre.astype(bfloat)
            return
        cosine, sine_low, sine_high = rope[0, rows], rope[1, rows], rope[2, rows]
        for head in range(group_heads):
            values = pre[:, head * HD : (head + 1) * HD]
            turned = (
                values * cosine
                + pltpu.roll(values, HD - ROT // 2, 1) * sine_low
                + pltpu.roll(values, ROT // 2, 1) * sine_high
            )
            heads[part, rows, pl.ds(head * HD, HD)] = turned.astype(bfloat)

    def expand(block):
        rows = rows_of(block)

        def one(index, carry):
            first = pl.multiple_of(index * tile, tile)
            pre = jnp.dot(
                normed[3, rows],
                w_in_low[:, pl.ds(attn_width + first, tile)],
                preferred_element_type=single,
            )
            pre = pre + small[pl.ds(10 + here, 1), pl.ds(first, tile)]
            normal = 0.5 * (1.0 + lax.erf(pre * 0.7071067811865476))
            joined[rows, pl.ds(head_width + first, tile)] = (pre * normal).astype(bfloat)
            slope[rows, pl.ds(first, tile)] = (
                normal + pre * jnp.exp(-0.5 * pre * pre) * 0.3989422804014327
            ).astype(bfloat)
            return carry

        lax.fori_loop(0, units // tile, one, 0)

    def contract(block):
        rows = rows_of(block)

        def one(index, carry):
            first = pl.multiple_of(index * tile, tile)
            total[rows, pl.ds(first, tile)] = contract_last(
                joined[rows, pl.ds(head_width, units)],
                w_out_low[pl.ds(first, tile), pl.ds(head_width, units)],
            )
            return carry

        lax.fori_loop(0, D // tile, one, 0)

    def attend(block):
        rows = rows_of(block)
        places = block * own + lax.broadcasted_iota(jnp.int32, (own, length), 0)
        allowed = lax.broadcasted_iota(jnp.int32, (own, length), 1) <= places
        for head in range(group_heads):
            lanes = pl.ds(head * HD, HD)
            scores = contract_last(heads[0, rows, lanes], heads[1, :, lanes]) * HD ** (-0.5)
            scores = jnp.where(allowed, scores, masked_score)
            raised = jnp.exp(scores - jnp.max(scores, axis=-1, keepdims=True))
            low = (raised / jnp.sum(raised, axis=-1, keepdims=True)).astype(bfloat)
            chances[head, rows] = low
            joined[rows, lanes] = jnp.dot(
                low, heads[2, :, lanes], preferred_element_type=single
            ).astype(bfloat)

    def finish_block(block):
        attend(block)
        rows = rows_of(block)

        def one(index, carry):
            first = pl.multiple_of(index * tile, tile)
            spot = (rows, pl.ds(first, tile))
            give[spot] = (
                total[spot]
                + contract_last(
                    joined[rows, pl.ds(0, head_width)],
                    w_out_low[pl.ds(first, tile), pl.ds(0, head_width)],
                )
            ).astype(bfloat)
            return carry

        lax.fori_loop(0, D // tile, one, 0)

    def save(place, source, target):
        return pltpu.make_async_copy(source, target, save_sem.at[place])

    chain = LineSum(size, give, terms, term_send, term_recv, CUT)
    ending = jnp.logical_or(here == 0, here == size - 1)

    def query_pass(side, way, step):
        @pl.when(has_origin(way, step))
        def _():
            line_landed(side, way, step, 0).wait_recv()
            pl.when(has_next(way))(line_hop(side, way, step, 0).start)
            keep_flow(0, here - way * step).start()

    def query_side(side, way):
        for step in range(size - 1, 0, -1):
            query_pass(side, way, step)
        pl.when(has_next(way))(line_hop(side, way, 0, 0).start)

    cube_in.step(0)
    cube_out.start()
    line_step(1, FLOW_ORDER[:3])
    lower = 2 * here < size
    pl.when(lower)(lambda: query_side(0, 1))
    pl.when(jnp.logical_not(lower))(lambda: query_side(1, -1))
    for index in range(1, cube_in.steps()):
        cube_in.step(index)
    cube_in.finish()
    save(0, w_in_low, all_in).start()

    def early(block):
        project(block, 1)
        project(block, 2)
        expand(block)

    at_distance(0, early)
    line_step(2, FLOW_ORDER[:3])
    at_distance(1, early)
    cube_out.step(0)
    at_distance(2, early)
    project(here, 0)

    @pl.when(jnp.logical_not(ending))
    def _():
        pl.when(lower)(lambda: query_side(1, -1))
        pl.when(jnp.logical_not(lower))(lambda: query_side(0, 1))

    for index in range(1, cube_out.steps()):
        cube_out.step(index)
    cube_out.finish()
    save(1, w_out_low, all_out).start()
    for step in range(min(3, size)):
        at_distance(step, contract)
    for step in range(3, size):
        line_step(step, FLOW_ORDER[:3])

        def rest(block):
            early(block)
            contract(block)

        at_distance(step, rest)
    finish_block(here)

    @pl.when(jnp.logical_not(ending))
    def _():
        def one(index, carry):
            block = lax.rem(here + 1 + index, size)
            project(block, 0)
            finish_block(block)
            return carry

        lax.fori_loop(0, size - 1, one, 0)

    for rank in range(size - 1):
        step = size - 1 - rank

        @pl.when(ending)
        def _():
            dest = lax.select(here == 0, size - 1 - rank, rank)
            side = lax.select(here == 0, 1, 0)
            block = normed.at[0, rows_of(dest)]
            pltpu.make_async_remote_copy(
                src_ref=block,
                dst_ref=block,
                send_sem=line_send.at[side, step - 1, 0],
                recv_sem=line_recv.at[side, step - 1, 0],
                device_id={"tensor": lax.select(here == 0, 1, size - 2)},
                device_id_type=MESH,
            ).wait_recv()
            keep_flow(0, dest).start()
            project(dest, 0)
            finish_block(dest)

        for way in (chain.near, -chain.near):
            chain.relay(way, chain.far(rank, way))

    saves = [
        save(2, joined, joined_out),
        save(3, slope, slope_out),
        save(4, heads, heads_out),
        save(5, chances, chances_out),
    ]
    for copy in saves:
        copy.start()
    for place in range(CUT):
        chain.collect(place, newest)

    def sixteen(index):
        spot = pl.ds(pl.multiple_of(index * 16, 16), 16)
        return spot, pl.ds(pl.multiple_of(here * own + index * 16, 16), 16)

    def compose(index, carry):
        spot, inner = sixteen(index)
        value = flows[3, spot].astype(single) + newest[spot] + small[8:9, :] + small[9:10, :]
        newest[spot] = value
        inverse = lax.rsqrt(jnp.mean(value * value, axis=-1, keepdims=True) + mix_eps)
        scales[spot] = jnp.broadcast_to(inverse, (16, HD))
        give[inner] = (value * inverse * small[4:5, :]).astype(bfloat)
        found = dots[spot]
        for stream in range(STREAMS):
            dot = jnp.sum(back[stream, spot].astype(single) * value, axis=-1, keepdims=True)
            found = found + jnp.where(lane == stream * LAYERS + LAYER, dot, 0.0)
        dots[spot] = found
        return carry

    lax.fori_loop(0, own // 16, compose, 0)
    mix_normed = give[rows_of(here)]
    mix_pre = contract_last(mix_normed, mix_low[...])
    normal = 0.5 * (1.0 + lax.erf(mix_pre * 0.7071067811865476))
    act = mix_pre * normal
    act_slope = normal + mix_pre * jnp.exp(-0.5 * mix_pre * mix_pre) * 0.3989422804014327
    table = mix_table[0:HD]
    weights[...] = (
        jnp.dot(act, table, precision=highest_precision, preferred_element_type=single)
        + mix_table[HD : HD + 1]
    )
    d_mixing = dots[...]
    d_act = lax.dot_general(
        d_mixing,
        table,
        (((1,), (1,)), ((), ())),
        precision=highest_precision,
        preferred_element_type=single,
    )
    d_mix_pre = (d_act * act_slope).astype(bfloat)
    out_grad = lax.dot_general(
        act,
        d_mixing,
        (((0,), (0,)), ((), ())),
        precision=highest_precision,
        preferred_element_type=single,
    )
    mix_out_grad[...] = jnp.zeros_like(mix_out_grad)
    mix_out_grad[0:MIXH] = out_grad[0:MIXH]
    mix_out_grad[MIXH : MIXH + 1] = jnp.sum(d_mixing, axis=0, keepdims=True)

    def spread(index, carry):
        lanes = pl.ds(pl.multiple_of(index * tile, tile), tile)
        total[0:own, lanes] = jnp.dot(
            d_mix_pre, mix_low[:, lanes], preferred_element_type=single
        )
        mix_in_grad[:, lanes] = contract_first(d_mix_pre, give[rows_of(here), lanes])[
            0 : mix_in_grad.shape[0]
        ]
        return carry

    lax.fori_loop(0, D // tile, spread, 0)
    sums[...] = jnp.zeros_like(sums)

    def descend(index, carry):
        spot, inner = sixteen(index)
        value, inverse = newest[spot], scales[spot][:, 0:1]
        d_normed = total[spot]
        scaled = d_normed * small[4:5, :]
        middle = jnp.mean(scaled * value, axis=-1, keepdims=True)
        result = inverse * scaled - value * (inverse * inverse * inverse * middle)
        for stream in range(STREAMS):
            column = stream * LAYERS + LAYER
            result = result + weights[spot][:, column : column + 1] * back[stream, spot].astype(
                single
            )
        d_newest[spot] = result
        d_branch[spot] = result.astype(bfloat)
        gain = d_normed * value * inverse
        sums[0] += gain[0:8] + gain[8:16]
        sums[1] += result[0:8] + result[8:16]
        return carry

    lax.fori_loop(0, own // 16, descend, 0)
    row_grads[0:1] = jnp.sum(sums[0], axis=0, keepdims=True)
    row_grads[1:2] = jnp.sum(sums[1], axis=0, keepdims=True)
    for step in range(size):
        for flow in FLOW_ORDER:
            for side, way in sides:

                @pl.when(jnp.logical_and(has_next(way), has_origin(way, step)))
                def _():
                    line_hop(side, way, step, flow).wait_send()

    cube_in.drain()
    cube_out.drain()
    chain.drain()
    for flow in FLOW_ORDER:
        for block in range(size):
            keep_flow(flow, block).wait()
    save(0, w_in_low, all_in).wait()
    save(1, w_out_low, all_out).wait()
    for copy in saves:
        copy.wait()


def forward(flows, w_in, w_out, small, rope, stored, cotangent, mix_weights, size, count, identity):
    own = flows.shape[1]
    length = own * size
    rows, width_in = w_in.shape
    width_out = w_out.shape[1]
    head_width = HEADS // size * HD
    units = FF // size
    pieces = count.bit_length() - 2
    cube = [pltpu.SemaphoreType.DMA((pieces, 2**pieces))] * 8
    low = lambda *shape: jax.ShapeDtypeStruct(shape, bfloat)
    hbm = pl.BlockSpec(memory_space=pl.ANY)
    vmem = pl.BlockSpec(memory_space=pltpu.VMEM)
    return pl.pallas_call(
        lambda *refs: forward_kernel(size, count, *refs),
        out_shape=[
            low(D, width_in),
            low(D, width_out),
            low(STREAMS, length, D),
            low(length, width_out),
            low(length, units),
            low(3, length, head_width),
            low(HEADS // size, length, length),
            jax.ShapeDtypeStruct((own, D), single),
            jax.ShapeDtypeStruct((own, D), single),
            low(own, D),
            jax.ShapeDtypeStruct((own, HD), single),
            jax.ShapeDtypeStruct((8, D), single),
            jax.ShapeDtypeStruct((40, D), single),
            jax.ShapeDtypeStruct((40, HD), single),
        ],
        in_specs=[vmem, hbm, hbm, vmem, vmem, hbm, hbm, vmem],
        out_specs=[hbm] * 7 + [vmem] * 7,
        scratch_shapes=[
            pltpu.VMEM((D, width_in), bfloat),
            pltpu.VMEM((D, width_out), bfloat),
            pltpu.VMEM((STREAMS, length, D), bfloat),
            pltpu.VMEM((3, length, head_width), bfloat),
            pltpu.VMEM((HEADS // size, length, length), bfloat),
            pltpu.VMEM((length, width_out), bfloat),
            pltpu.VMEM((length, units), bfloat),
            pltpu.VMEM((length, D), single),
            pltpu.VMEM((length, D), bfloat),
            pltpu.VMEM((size + 1, own, D), bfloat),
            pltpu.VMEM((STREAMS, own, D), bfloat),
            pltpu.VMEM((2, own, D), bfloat),
            pltpu.VMEM((own, HD), single),
            pltpu.VMEM((own, HD), single),
            pltpu.VMEM((2, 8, D), single),
            pltpu.VMEM((HD, D), bfloat),
            pltpu.VMEM((HD + 8, HD), single),
            pltpu.SemaphoreType.DMA((2,)),
            pltpu.SemaphoreType.DMA,
            pltpu.SemaphoreType.DMA((2,)),
            pltpu.SemaphoreType.DMA((2, size, STREAMS)),
            pltpu.SemaphoreType.DMA((2, size, STREAMS)),
            pltpu.SemaphoreType.DMA((2, size, CUT)),
            pltpu.SemaphoreType.DMA((2, size, CUT)),
            pltpu.SemaphoreType.DMA((6,)),
            pltpu.SemaphoreType.DMA((STREAMS, size)),
        ]
        + cube,
        compiler_params=pltpu.CompilerParams(
            collective_id=identity, has_side_effects=True, vmem_limit_bytes=60 * 2**20
        ),
        name="forward_%d" % identity,
    )(flows, w_in, w_out, small, rope, stored, cotangent, mix_weights)


def backward_kernel(
    size,
    d_branch,
    rope,
    all_in,
    all_out,
    slope_in,
    heads_in,
    chances_in,
    all_back,
    all_up,
    all_pre,
    all_normed,
    d_residual,
    bias_grads,
    w_in_low,
    w_out_low,
    slope,
    heads,
    chances,
    back,
    d_heads,
    d_up,
    d_pre,
    part,
    terms,
    d_normed,
    load_sem,
    line_send,
    line_recv,
    term_send,
    term_recv,
    save_sem,
):
    here = lax.axis_index("tensor")
    own = d_branch.shape[0]
    length = own * size
    head_width = heads.shape[2]
    group_heads = head_width // HD
    attn_width = 3 * head_width
    units = slope.shape[1]
    sides = ((0, 1), (1, -1))
    tile = 512
    scale = HD ** (-0.5)

    def rows_of(block):
        return pl.ds(pl.multiple_of(block * own, own), own)

    loads = [
        pltpu.make_async_copy(source, target, load_sem.at[place])
        for place, (source, target) in enumerate(
            [
                (all_out, w_out_low),
                (slope_in, slope),
                (all_in, w_in_low),
                (heads_in, heads),
                (chances_in, chances),
            ]
        )
    ]
    enter([(here < size - 1, {"tensor": here + 1}), (here > 0, {"tensor": here - 1})])

    def has_next(way):
        return here < size - 1 if way > 0 else here > 0

    def has_origin(way, step):
        return here >= step if way > 0 else here < size - step

    def line_hop(side, way, step):
        block = back.at[rows_of(here - way * step)]
        return pltpu.make_async_remote_copy(
            src_ref=d_branch if step == 0 else block,
            dst_ref=block,
            send_sem=line_send.at[side, step],
            recv_sem=line_recv.at[side, step],
            device_id={"tensor": here + way},
            device_id_type=MESH,
        )

    def line_landed(side, way, step):
        block = back.at[rows_of(here - way * step)]
        return pltpu.make_async_remote_copy(
            src_ref=block,
            dst_ref=block,
            send_sem=line_send.at[side, step - 1],
            recv_sem=line_recv.at[side, step - 1],
            device_id={"tensor": here - way},
            device_id_type=MESH,
        )

    for side, way in sides:
        pl.when(has_next(way))(line_hop(side, way, 0).start)
    for copy in loads:
        copy.start()
    back[rows_of(here)] = d_branch[...]

    def pull(block):
        rows = rows_of(block)
        d_heads[rows] = jnp.dot(
            back[rows], w_out_low[:, 0:head_width], preferred_element_type=single
        ).astype(bfloat)

        def one(index, carry):
            first = pl.multiple_of(index * tile, tile)
            d_hidden = jnp.dot(
                back[rows],
                w_out_low[:, pl.ds(head_width + first, tile)],
                preferred_element_type=single,
            )
            d_up[rows, pl.ds(first, tile)] = (
                d_hidden * slope[rows, pl.ds(first, tile)].astype(single)
            ).astype(bfloat)
            return carry

        lax.fori_loop(0, units // tile, one, 0)

    def push(block):
        rows = rows_of(block)

        def one(index, carry):
            first = pl.multiple_of(index * tile, tile)
            part[rows, pl.ds(first, tile)] = contract_last(
                d_up[rows], w_in_low[pl.ds(first, tile), pl.ds(attn_width, units)]
            ).astype(bfloat)
            return carry

        lax.fori_loop(0, D // tile, one, 0)

    chain = LineSum(size, part, terms, term_send, term_recv, CUT)
    ending = jnp.logical_or(here == 0, here == size - 1)

    def stage(step):
        for way in (chain.near, -chain.near):
            chain.relay(way, chain.far(size - 1 - step, way))

    loads[0].wait()
    loads[1].wait()
    pull(here)
    for step in range(1, size):
        for side, way in sides:

            @pl.when(has_origin(way, step))
            def _():
                line_landed(side, way, step).wait_recv()
                pl.when(has_next(way))(line_hop(side, way, step).start)

        if step == 1:
            loads[2].wait()

        def both(side, carry):
            block = here - step + 2 * step * side

            @pl.when(jnp.logical_and(block >= 0, block < size))
            def _():
                pull(block)
                push(block)

            return carry

        lax.fori_loop(0, 2, both, 0)
        pl.when(ending)(lambda: stage(step))
    saves = [
        pltpu.make_async_copy(source, target, save_sem.at[place])
        for place, (source, target) in enumerate(
            [(back, all_back), (d_up, all_up), (d_pre, all_pre)]
        )
    ]
    saves[0].start()
    saves[1].start()
    loads[3].wait()
    loads[4].wait()
    bias_grads[...] = jnp.zeros_like(bias_grads)
    half_rows = length // 2

    def turn_back(gradients, rows):
        return (
            gradients * rope[0, rows]
            - pltpu.roll(gradients, HD - ROT // 2, 1) * rope[1, rows]
            - pltpu.roll(gradients, ROT // 2, 1) * rope[2, rows]
        )

    for head in range(group_heads):
        lanes = pl.ds(head * HD, HD)
        d_keys = jnp.zeros((length, HD), single)
        d_values = jnp.zeros((length, HD), single)
        query_bias = jnp.zeros((1, HD), single)
        for half in range(2):
            rows = pl.ds(half * half_rows, half_rows)
            low = chances[head, rows]
            chance = low.astype(single)
            d_chance = contract_last(d_heads[rows, lanes], heads[2, :, lanes])
            centre = jnp.sum(d_chance * chance, axis=-1, keepdims=True)
            d_score = (chance * (d_chance - centre)).astype(bfloat)
            d_query = (
                jnp.dot(d_score, heads[1, :, lanes], preferred_element_type=single) * scale
            )
            d_query = turn_back(d_query, rows).astype(bfloat)
            d_pre[0, rows, lanes] = d_query
            query_bias = query_bias + jnp.sum(d_query.astype(single), axis=0, keepdims=True)
            d_keys = d_keys + contract_first(d_score, heads[0, rows, lanes])
            d_values = d_values + contract_first(low, d_heads[rows, lanes])
        whole = pl.ds(0, length)
        d_key = turn_back(d_keys * scale, whole).astype(bfloat)
        d_value = d_values.astype(bfloat)
        d_pre[1, :, lanes] = d_key
        d_pre[2, :, lanes] = d_value
        bias_grads[0:1, lanes] = query_bias
        bias_grads[1:2, lanes] = jnp.sum(d_key.astype(single), axis=0, keepdims=True)
        bias_grads[2:3, lanes] = jnp.sum(d_value.astype(single), axis=0, keepdims=True)
    saves[2].start()
    for step in range(1, size - 1):
        pl.when(jnp.logical_not(ending))(lambda: stage(step))
    for which in range(3):

        def one(index, carry):
            first = pl.multiple_of(index * tile, tile)
            d_normed[which, :, pl.ds(first, tile)] = contract_last(
                d_pre[which],
                jnp.concatenate(
                    [
                        w_in_low[pl.ds(first, tile), pl.ds((head * 3 + which) * HD, HD)]
                        for head in range(group_heads)
                    ],
                    axis=1,
                ),
            ).astype(bfloat)
            return carry

        lax.fori_loop(0, D // tile, one, 0)
        saves.append(
            pltpu.make_async_copy(
                d_normed.at[which], all_normed.at[which], save_sem.at[3 + which]
            )
        )
        saves[-1].start()
    push(here)
    def unit_sum(index, carry):
        lanes = pl.ds(pl.multiple_of(index * 256, 256), 256)
        bias_grads[3:4, lanes] = jnp.sum(d_up[:, lanes].astype(single), axis=0, keepdims=True)
        return carry

    lax.fori_loop(0, units // 256, unit_sum, 0)
    pl.when(jnp.logical_not(ending))(lambda: stage(size - 1))
    for place in range(CUT):
        chain.collect(place, d_residual)
    for step in range(size):
        for side, way in sides:

            @pl.when(jnp.logical_and(has_next(way), has_origin(way, step)))
            def _():
                line_hop(side, way, step).wait_send()

    chain.drain()
    for copy in saves:
        copy.wait()


def backward(d_branch, rope, all_in, all_out, slope, heads, chances, size, identity):
    own = d_branch.shape[0]
    length = own * size
    head_width = heads.shape[2]
    units = slope.shape[1]
    low = lambda *shape: jax.ShapeDtypeStruct(shape, bfloat)
    wide = lambda *shape: jax.ShapeDtypeStruct(shape, single)
    hbm = pl.BlockSpec(memory_space=pl.ANY)
    vmem = pl.BlockSpec(memory_space=pltpu.VMEM)
    return pl.pallas_call(
        lambda *refs: backward_kernel(size, *refs),
        out_shape=[
            low(length, D),
            low(length, units),
            low(3, length, head_width),
            low(3, length, D),
            wide(own, D),
            wide(8, D),
        ],
        in_specs=[vmem] * 2 + [hbm] * 5,
        out_specs=[hbm] * 4 + [vmem] * 2,
        scratch_shapes=[
            pltpu.VMEM(all_in.shape, bfloat),
            pltpu.VMEM(all_out.shape, bfloat),
            pltpu.VMEM(slope.shape, bfloat),
            pltpu.VMEM(heads.shape, bfloat),
            pltpu.VMEM(chances.shape, bfloat),
            pltpu.VMEM((length, D), bfloat),
            pltpu.VMEM((length, head_width), bfloat),
            pltpu.VMEM((length, units), bfloat),
            pltpu.VMEM((3, length, head_width), bfloat),
            pltpu.VMEM((length, D), bfloat),
            pltpu.VMEM((size + 1, own, D), bfloat),
            pltpu.VMEM((3, length, D), bfloat),
            pltpu.SemaphoreType.DMA((5,)),
            pltpu.SemaphoreType.DMA((2, size)),
            pltpu.SemaphoreType.DMA((2, size)),
            pltpu.SemaphoreType.DMA((2, size, CUT)),
            pltpu.SemaphoreType.DMA((2, size, CUT)),
            pltpu.SemaphoreType.DMA((6,)),
        ],
        compiler_params=pltpu.CompilerParams(
            collective_id=identity, has_side_effects=True, vmem_limit_bytes=60 * 2**20
        ),
        name="backward_%d" % identity,
    )(d_branch, rope, all_in, all_out, slope, heads, chances)


def scatter_kernel(
    size,
    count,
    all_normed,
    d_normed,
    back_in,
    joined_in,
    up_in,
    pre_in,
    flows_in,
    small,
    d_residual,
    d_newest,
    grad_in,
    grad_out,
    d_flows,
    norm_grads,
    squares,
    back,
    joined,
    d_up,
    d_pre,
    tiles,
    kept_in,
    kept_out,
    pair_in,
    pair_out,
    give_in,
    give_out,
    land_in,
    land_out,
    parts,
    terms,
    flows,
    total,
    sums,
    work,
    load_sem,
    tile_sem,
    flow_sem,
    give_sem,
    pair_sem,
    credit,
    cube_send,
    cube_recv,
    line_send,
    line_recv,
    save_sem,
):
    here = lax.axis_index("tensor")
    me = lax.axis_index("dp")
    bits = count.bit_length() - 1
    routes = cube_routes(bits)
    pieces = len(routes)
    subsets = sorted(routes[0][0], key=lambda held: -len(held))
    own = flows.shape[1]
    length = own * size
    rows = pair_in.shape[0]
    piece_rows = rows // pieces
    lane_rows = tiles.shape[3]
    head_width = d_pre.shape[2]
    group_heads = head_width // HD
    attn_width = 3 * head_width
    units = d_up.shape[1]
    tile = 512
    kept, pair, give, land = (
        (kept_out, kept_in),
        (pair_out, pair_in),
        (give_out, give_in),
        (land_out, land_in),
    )
    widths = (kept_out.shape[1], kept_in.shape[1])

    loads = [
        pltpu.make_async_copy(source, target, load_sem.at[place])
        for place, (source, target) in enumerate(
            [(d_normed.at[which], parts.at[which]) for which in range(3)]
            + [(back_in, back), (joined_in, joined), (up_in, d_up), (pre_in, d_pre)]
        )
    ]

    def first_lane(held):
        return pl.multiple_of(plus_flips(me, held) * rows // lane_rows * lane_rows, HD)

    def load_tile(slot, held):
        return pltpu.make_async_copy(
            all_normed.at[:, :, pl.ds(first_lane(held), lane_rows)],
            tiles.at[slot],
            tile_sem.at[slot],
        )

    def load_flow(flow):
        return pltpu.make_async_copy(
            flows_in.at[flow], flows.at[flow % 2], flow_sem.at[flow % 2]
        )

    for copy in loads:
        copy.start()
    load_tile(0, (0,) + subsets[0]).start()
    load_tile(1, subsets[0]).start()
    load_flow(3).start()
    load_flow(0).start()
    enter(
        [(here < size - 1, {"tensor": here + 1}), (here > 0, {"tensor": here - 1})]
        + [(jnp.bool_(True), {"dp": plus_flips(me, (bit,))}) for bit in range(bits)]
    )
    ending = jnp.logical_or(here == 0, here == size - 1)
    chains = [
        LineSum(size, parts.at[which], terms.at[which], line_send.at[which], line_recv.at[which], 1)
        for which in range(3)
    ]

    def relay(rank):
        for sign in (1, -1):
            for chain in chains:
                chain.relay(sign * chain.near, chain.far(rank, sign * chain.near))

    for which in range(3):
        loads[which].wait()
    for rank in range(size - 1):
        pl.when(ending)(lambda: relay(rank))

    def own_rows(value, held):
        if lane_rows == rows:
            return value
        work[:, 0 : value.shape[1]] = value
        first = lax.rem(plus_flips(me, held) * rows, lane_rows)
        return work[pl.ds(pl.multiple_of(first, 16), rows), 0 : value.shape[1]]

    def products(which, held, slot, emit):
        if which == 0:
            source = back[:, pl.ds(first_lane(held), lane_rows)]

            def one(index, carry):
                first = pl.multiple_of(index * tile, tile)
                emit(own_rows(contract_first(source, joined[:, pl.ds(first, tile)]), held), first)
                return carry

            lax.fori_loop(0, widths[0] // tile, one, 0)
            return
        for part in range(3):
            value = own_rows(contract_first(tiles[slot, part], d_pre[part]), held)
            for head in range(group_heads):
                emit(value[:, head * HD : (head + 1) * HD], (head * 3 + part) * HD)

        def one(index, carry):
            first = pl.multiple_of(index * tile, tile)
            value = contract_first(tiles[slot, 3], d_up[:, pl.ds(first, tile)])
            emit(own_rows(value, held), attn_width + first)
            return carry

        lax.fori_loop(0, units // tile, one, 0)

    def place_of(held):
        return sum(2 ** (bit - 1) for bit in held)

    def pass_pair(which):
        return pltpu.make_async_remote_copy(
            src_ref=give[which],
            dst_ref=pair[which],
            send_sem=give_sem.at[which],
            recv_sem=pair_sem.at[which],
            device_id={"dp": plus_flips(me, (0,))},
            device_id_type=MESH,
        )

    def kept_rows(piece, held):
        return pl.ds(place_of(held) * rows + piece * piece_rows, piece_rows)

    def land_rows(piece, landed):
        slot = piece * (len(subsets) - 1) + place_of(landed) - 1
        return pl.ds(slot * piece_rows, piece_rows)

    def cube_hop(which, piece, bit, landed):
        return pltpu.make_async_remote_copy(
            src_ref=kept[which].at[kept_rows(piece, landed)],
            dst_ref=land[which].at[land_rows(piece, landed)],
            send_sem=cube_send.at[which, piece, place_of(landed)],
            recv_sem=cube_recv.at[which, piece, place_of(landed)],
            device_id={"dp": plus_flips(me, (bit,))},
            device_id_type=MESH,
        )

    def needs(piece, held):
        return [
            (bit, landed)
            for step in routes[piece][1]
            for bit, source, landed in step
            if source == held
        ]

    def add_landed(which, piece, held):
        for bit, landed in needs(piece, held):
            cube_hop(which, piece, bit, landed).wait_recv()

        def one(index, carry):
            def column(at, inner):
                lanes = pl.ds(pl.multiple_of(at * tile, tile), tile)
                spot = pl.ds(
                    pl.multiple_of(kept_rows(piece, held).start + index * 16, 16), 16
                )
                value = kept[which][spot, lanes].astype(single)
                for _, landed in needs(piece, held):
                    arrived = pl.ds(
                        pl.multiple_of(land_rows(piece, landed).start + index * 16, 16), 16
                    )
                    value = value + land[which][arrived, lanes].astype(single)
                kept[which][spot, lanes] = value.astype(bfloat)
                if not held:
                    value = value * value
                    value = value[0:8] + value[8:16]
                    for group in range(tile // HD):
                        inner = inner + value[:, group * HD : (group + 1) * HD]
                return inner

            return lax.fori_loop(0, widths[which] // tile, column, carry)

        found = lax.fori_loop(0, piece_rows // 16, one, jnp.zeros((8, HD), single))
        if not held:
            squares[...] += found

    for copy in loads[3:]:
        copy.wait()
    last = len(subsets) - 1
    for index, held in enumerate(subsets):
        load_tile(0, (0,) + held).wait()
        for which in range(2):
            if index > 0:
                pass_pair(which).wait_send()

            def emit(value, first):
                give[which][:, pl.ds(first, value.shape[1])] = value.astype(bfloat)

            products(which, (0,) + held, 0, emit)
            if index > 0:
                pl.semaphore_wait(credit.at[which], 1)
            pass_pair(which).start()
        if index < last:
            load_tile(0, (0,) + subsets[index + 1]).start()
        load_tile(1, held).wait()
        for which in range(2):
            pass_pair(which).wait_recv()

            def emit(value, first):
                lanes = pl.ds(first, value.shape[1])
                kept[which][pl.ds(place_of(held) * rows, rows), lanes] = (
                    value + pair[which][:, lanes].astype(single)
                ).astype(bfloat)

            products(which, held, 1, emit)
            if index < last:
                pl.semaphore_signal(
                    credit.at[which],
                    inc=1,
                    device_id={"dp": plus_flips(me, (0,))},
                    device_id_type=MESH,
                )
            for piece, (_, steps) in enumerate(routes):
                for bit, _, landed in steps[-1]:
                    if landed == held:
                        cube_hop(which, piece, bit, landed).start()
        if index < last:
            load_tile(1, subsets[index + 1]).start()

    sums[...] = jnp.zeros_like(sums)

    def descend(flow, gradient):
        load_flow(flow).wait()
        gain = 2 if flow == 3 else 0

        def one(index, carry):
            spot = pl.ds(pl.multiple_of(index * 16, 16), 16)
            values = flows[flow % 2, spot].astype(single)
            centred = values - jnp.mean(values, axis=-1, keepdims=True)
            inverse = lax.rsqrt(jnp.mean(centred * centred, axis=-1, keepdims=True) + norm_eps)
            unit = centred * inverse
            incoming = gradient[spot]
            scaled = incoming * small[gain : gain + 1, :]
            result = inverse * (
                scaled
                - jnp.mean(scaled, axis=-1, keepdims=True)
                - unit * jnp.mean(scaled * unit, axis=-1, keepdims=True)
            )
            if flow == 3:
                result = result + d_newest[spot]
            d_flows[flow, spot] = result.astype(bfloat)
            unit = unit * incoming
            sums[gain] += unit[0:8] + unit[8:16]
            sums[gain + 1] += incoming[0:8] + incoming[8:16]
            return carry

        lax.fori_loop(0, own // 16, one, 0)

    descend(3, d_residual)
    load_flow(1).start()
    pl.when(jnp.logical_not(ending))(lambda: relay(0))
    for step in range(pieces - 2, -1, -1):
        for which in range(2):
            for piece, (_, steps) in enumerate(routes):
                for bit, _, landed in steps[step]:
                    add_landed(which, piece, landed)
                    cube_hop(which, piece, bit, landed).start()
    for rank in range(1, size - 1):
        pl.when(jnp.logical_not(ending))(lambda: relay(rank))
    for which in range(3):
        chains[which].collect(0, total)
        descend(which, total)
        if which == 0:
            load_flow(2).start()
    norm_grads[...] = jnp.zeros_like(norm_grads)
    for row in range(4):
        norm_grads[row : row + 1] = jnp.sum(sums[row], axis=0, keepdims=True)
    squares[...] = jnp.zeros_like(squares)
    saves = []
    for which, target in enumerate((grad_out, grad_in)):
        for piece in range(pieces):
            add_landed(which, piece, ())
        saves.append(
            pltpu.make_async_copy(kept[which].at[pl.ds(0, rows)], target, save_sem.at[which])
        )
        saves[-1].start()
    for which in range(2):
        pass_pair(which).wait_send()
        for piece, (_, steps) in enumerate(routes):
            for step in steps:
                for bit, _, landed in step:
                    cube_hop(which, piece, bit, landed).wait_send()
    for chain in chains:
        chain.drain()
    for copy in saves:
        copy.wait()


def scatter(
    all_normed, d_normed, back, joined, d_up, d_pre, flows, small, d_residual, d_newest,
    size, count, identity,
):
    own = flows.shape[1]
    length = own * size
    rows = D // count
    lane_rows = max(rows, HD)
    head_width = d_pre.shape[2]
    width_out = joined.shape[1]
    width_in = 3 * head_width + d_up.shape[1]
    pieces = count.bit_length() - 2
    held = 2**pieces
    low = lambda *shape: jax.ShapeDtypeStruct(shape, bfloat)
    wide = lambda *shape: jax.ShapeDtypeStruct(shape, single)
    hbm = pl.BlockSpec(memory_space=pl.ANY)
    vmem = pl.BlockSpec(memory_space=pltpu.VMEM)
    landed = pieces * (held - 1) * (rows // pieces)
    return pl.pallas_call(
        lambda *refs: scatter_kernel(size, count, *refs),
        out_shape=[
            low(rows, width_in),
            low(rows, width_out),
            low(STREAMS, own, D),
            wide(8, D),
            wide(8, HD),
        ],
        in_specs=[hbm] * 7 + [vmem] * 3,
        out_specs=[hbm] * 2 + [vmem] * 3,
        scratch_shapes=[
            pltpu.VMEM(back.shape, bfloat),
            pltpu.VMEM(joined.shape, bfloat),
            pltpu.VMEM(d_up.shape, bfloat),
            pltpu.VMEM(d_pre.shape, bfloat),
            pltpu.VMEM((2, STREAMS, length, lane_rows), bfloat),
            pltpu.VMEM((held * rows, width_in), bfloat),
            pltpu.VMEM((held * rows, width_out), bfloat),
            pltpu.VMEM((rows, width_in), bfloat),
            pltpu.VMEM((rows, width_out), bfloat),
            pltpu.VMEM((rows, width_in), bfloat),
            pltpu.VMEM((rows, width_out), bfloat),
            pltpu.VMEM((landed, width_in), bfloat),
            pltpu.VMEM((landed, width_out), bfloat),
            pltpu.VMEM((3, length, D), bfloat),
            pltpu.VMEM((3, size + 1, own, D), bfloat),
            pltpu.VMEM((2, own, D), bfloat),
            pltpu.VMEM((own, D), single),
            pltpu.VMEM((4, 8, D), single),
            pltpu.VMEM((lane_rows if lane_rows > rows else 8, 512), single),
            pltpu.SemaphoreType.DMA((7,)),
            pltpu.SemaphoreType.DMA((2,)),
            pltpu.SemaphoreType.DMA((2,)),
            pltpu.SemaphoreType.DMA((2,)),
            pltpu.SemaphoreType.DMA((2,)),
            pltpu.SemaphoreType.REGULAR((2,)),
            pltpu.SemaphoreType.DMA((2, pieces, held)),
            pltpu.SemaphoreType.DMA((2, pieces, held)),
            pltpu.SemaphoreType.DMA((3, 2, size, 1)),
            pltpu.SemaphoreType.DMA((3, 2, size, 1)),
            pltpu.SemaphoreType.DMA((2,)),
        ],
        compiler_params=pltpu.CompilerParams(
            collective_id=identity, has_side_effects=True, vmem_limit_bytes=63 * 2**20
        ),
        name="scatter_%d" % identity,
    )(all_normed, d_normed, back, joined, d_up, d_pre, flows, small, d_residual, d_newest)


def small_sum_kernel(
    bits,
    norm_grads,
    row_grads,
    bias_grads,
    mix_in_grad,
    mix_out_grad,
    squares,
    out,
    value,
    total,
    landing,
    send_a,
    recv_a,
    send_b,
    recv_b,
):
    here = lax.axis_index("tensor")
    value[...] = jnp.zeros_like(value)
    width = HEADS // lax.axis_size("tensor") * HD
    value[0:4] = norm_grads[0:4]
    value[4:5] = row_grads[0:1]
    lanes = pl.ds(pl.multiple_of(here * width, HD), width)
    value[5:8, lanes] = bias_grads[0:3, 0:width]
    value[8:9] = row_grads[1:2]
    value[9:10] = row_grads[1:2]
    value[pl.ds(10 + here, 1), :] = bias_grads[3:4]
    value[SMALL_MIX : SMALL_MIX + MIXH] = mix_in_grad[0:MIXH]
    for place in range(5):
        value[56:64, place * HD : (place + 1) * HD] = mix_out_grad[place * 8 : place * 8 + 8]
    value[56:64, 5 * HD : 6 * HD] = squares[...]
    cube_sum_steps(bits, value, out, total, landing, send_a, recv_a, send_b, recv_b)


def small_sum(parts, bits, identity):
    steps = len(bits)
    vmem = pl.BlockSpec(memory_space=pltpu.VMEM)
    return pl.pallas_call(
        lambda *refs: small_sum_kernel(bits, *refs),
        out_shape=jax.ShapeDtypeStruct((64, D), single),
        in_specs=[vmem] * 6,
        out_specs=vmem,
        scratch_shapes=[pltpu.VMEM((64, D), single)] * 2
        + [pltpu.VMEM((steps, 32, D), single)]
        + [pltpu.SemaphoreType.DMA((steps,))] * 4,
        compiler_params=pltpu.CompilerParams(
            collective_id=identity, has_side_effects=True, vmem_limit_bytes=8 * 2**20
        ),
        name="small_sum_%d" % identity,
    )(*parts)


def finish_kernel(grad_in, grad_out, sums, weights, newest, stored, cotangent, d_flows, *refs):
    states, refs = (refs[0:4], refs[4:8]), refs[8:]
    small, mix, refs = refs[0:4], refs[4:8], refs[8:]
    norm_out, refs = refs[0], refs[1:]
    new_states, refs = (refs[0:5], refs[5:10]), refs[10:]
    new_small, new_mix, refs = refs[0:4], refs[4:8], refs[8:]
    out_streams, grad_streams, grad_stored, refs = refs[0], refs[1], refs[2], refs[3:]
    held, refs = (refs[0:2], refs[2:4], refs[4:6]), refs[6:]
    tiles_in, tiles_out, spread, passed, grad_sem, load_sem, save_sem, tile_load, tile_save, pass_sem = refs
    grads = (grad_in, grad_out)
    parts = load_sem.shape[2]
    rows = grad_in.shape[0]
    step_rows = rows // parts

    def load_grad(which):
        return pltpu.make_async_copy(grads[which], held[0][which], grad_sem.at[which])

    def load(which, kind, place):
        spot = pl.ds(place * step_rows, step_rows)
        return pltpu.make_async_copy(
            states[which][kind].at[spot],
            held[1][which].at[kind, spot],
            load_sem.at[which, kind, place],
        )

    def save(which, kind, place):
        spot = pl.ds(place * step_rows, step_rows)
        source = held[1][which].at[kind, spot] if kind < 4 else held[2][which].at[spot]
        return pltpu.make_async_copy(
            source, new_states[which][kind].at[spot], save_sem.at[which, kind, place]
        )

    own = newest.shape[0]
    tile_rows = tiles_in.shape[2]
    tile_count = own // tile_rows
    mixes = STREAMS + LAYER

    def tile_copies(index, into):
        spot = pl.ds(index * tile_rows, tile_rows)
        first, second = (cotangent, stored) if into else (out_streams, grad_stored)
        held_tile = (tiles_in if into else tiles_out).at[index % 2]
        sem = (tile_load if into else tile_save).at[index % 2]
        pairs = [
            (first.at[:, spot], held_tile.at[0:STREAMS]),
            (second.at[:, spot], held_tile.at[STREAMS:mixes]),
        ]
        return [
            pltpu.make_async_copy(*(pair if into else pair[::-1]), sem.at[place])
            for place, pair in enumerate(pairs)
        ]

    def compose(index):
        for copy in tile_copies(index, True):
            copy.wait()
        if index > 1:
            for copy in tile_copies(index - 2, False):
                copy.wait()
        spot = pl.ds(index * tile_rows, tile_rows)
        mix_tile = weights[spot]
        slot = index % 2
        for column in range(MIXH):
            spread[column] = jnp.broadcast_to(mix_tile[:, column : column + 1], (tile_rows, HD))

        def columns(place, carry):
            lanes = pl.ds(pl.multiple_of(place * HD, HD), HD)
            value = newest[spot, lanes]
            flows = [tiles_in[slot, stream, :, lanes].astype(single) for stream in range(STREAMS)]
            results = [spread[stream * LAYERS + LAYER] * value for stream in range(STREAMS)]
            for layer in range(LAYER):
                earlier = tiles_in[slot, STREAMS + layer, :, lanes].astype(single)
                gradient = None
                for stream in range(STREAMS):
                    weight = spread[stream * LAYERS + layer]
                    results[stream] = results[stream] + weight * earlier
                    term = weight * flows[stream]
                    gradient = term if gradient is None else gradient + term
                tiles_out[slot, STREAMS + layer, :, lanes] = gradient.astype(bfloat)
            for stream in range(STREAMS):
                tiles_out[slot, stream, :, lanes] = results[stream].astype(bfloat)
            return carry

        lax.fori_loop(0, D // HD, columns, 0)
        for copy in tile_copies(index, False):
            copy.start()
        if index + 2 < tile_count:
            for copy in tile_copies(index + 2, True):
                copy.start()

    for index in range(2):
        for copy in tile_copies(index, True):
            copy.start()
    for which in range(2):
        load_grad(which).start()
        for place in range(parts):
            for kind in range(4):
                load(which, kind, place).start()
    take_flows = pltpu.make_async_copy(d_flows, passed, pass_sem.at[0])
    give_flows = pltpu.make_async_copy(passed, grad_streams, pass_sem.at[1])
    take_flows.start()
    small_total = sums[0 : small[0].shape[0]]
    mix_total = jnp.concatenate(
        [sums[56:64, place * HD : (place + 1) * HD] for place in range(5)], axis=0
    )[0 : mix[0].shape[0], 0 : mix[0].shape[1]]

    def whole_sum(values):
        return jnp.sum(jnp.sum(values, axis=1, keepdims=True), axis=0, keepdims=True)

    norm = jnp.sqrt(
        whole_sum(sums[56:64, 5 * HD : 6 * HD])
        + whole_sum(small_total * small_total)
        + whole_sum(mix_total * mix_total)
    )
    norm_out[...] = norm
    factor = clip_norm / jnp.maximum(norm, clip_norm)
    for target, result in zip(
        new_small, adamw_step(*(ref[...] for ref in small), small_total, factor, small_rate)
    ):
        target[...] = result
    for target, result in zip(
        new_mix, adamw_step(*(ref[...] for ref in mix), mix_total, factor, small_rate)
    ):
        target[...] = result
    take_flows.wait()
    give_flows.start()
    tiles_done = 0
    for which in range(2):
        columns = held[1][which].shape[2]
        load_grad(which).wait()
        for place in range(parts):
            for kind in range(4):
                load(which, kind, place).wait()

            def update(index, carry):
                spot = pl.ds(pl.multiple_of(place * step_rows + index * 16, 16), 16)

                def column(at, inner):
                    lanes = pl.ds(pl.multiple_of(at * 512, 512), 512)
                    results = adamw_step(
                        *(held[1][which][kind, spot, lanes] for kind in range(4)),
                        held[0][which][spot, lanes].astype(single),
                        factor,
                        learn_rate,
                    )
                    for kind in range(4):
                        held[1][which][kind, spot, lanes] = results[kind]
                    held[2][which][spot, lanes] = results[0].astype(bfloat)
                    return inner

                return lax.fori_loop(0, columns // 512, column, carry)

            lax.fori_loop(0, step_rows // 16, update, 0)
            for kind in range(5):
                save(which, kind, place).start()
            if tiles_done < tile_count:
                compose(tiles_done)
                tiles_done += 1
    while tiles_done < tile_count:
        compose(tiles_done)
        tiles_done += 1
    for index in range(tile_count - 2, tile_count):
        for copy in tile_copies(index, False):
            copy.wait()
    give_flows.wait()
    for which in range(2):
        for place in range(parts):
            for kind in range(5):
                save(which, kind, place).wait()


def finish(
    grads, sums, weights, newest, stored, cotangent, d_flows, in_states, out_states, small, mix
):
    wide = lambda shape: jax.ShapeDtypeStruct(shape, single)
    low = lambda shape: jax.ShapeDtypeStruct(shape, bfloat)
    hbm = pl.BlockSpec(memory_space=pl.ANY)
    vmem = pl.BlockSpec(memory_space=pltpu.VMEM)
    shapes = [in_states[0].shape, out_states[0].shape]
    parts = 4
    tile = (2, STREAMS + LAYER, 16, D)
    return pl.pallas_call(
        finish_kernel,
        out_shape=[wide((1, 1))]
        + [entry for shape in shapes for entry in [wide(shape)] * 4 + [low(shape)]]
        + [wide(small[0].shape)] * 4
        + [wide(mix[0].shape)] * 4
        + [low(cotangent.shape), low(d_flows.shape), low(stored.shape)],
        in_specs=[hbm] * 2 + [vmem] * 3 + [hbm] * 3 + [hbm] * 8 + [vmem] * 8,
        out_specs=[vmem] + [hbm] * 10 + [vmem] * 8 + [hbm] * 3,
        scratch_shapes=[pltpu.VMEM(shape, grads[0].dtype) for shape in shapes]
        + [pltpu.VMEM((4,) + shape, single) for shape in shapes]
        + [pltpu.VMEM(shape, bfloat) for shape in shapes]
        + [pltpu.VMEM(tile, bfloat)] * 2
        + [pltpu.VMEM((MIXH, tile[2], HD), single), pltpu.VMEM(d_flows.shape, bfloat)]
        + [
            pltpu.SemaphoreType.DMA((2,)),
            pltpu.SemaphoreType.DMA((2, 4, parts)),
            pltpu.SemaphoreType.DMA((2, 5, parts)),
            pltpu.SemaphoreType.DMA((2, 2)),
            pltpu.SemaphoreType.DMA((2, 2)),
            pltpu.SemaphoreType.DMA((2,)),
        ],
        compiler_params=pltpu.CompilerParams(vmem_limit_bytes=60 * 2**20),
        name="finish",
    )(
        *grads, sums, weights, newest, stored, cotangent, d_flows,
        *in_states, *out_states, *small, *mix,
    )


def shards(
    in_streams,
    stored,
    cotangent,
    in_weights,
    in_moment,
    in_second,
    in_average,
    out_weights,
    out_moment,
    output_second_moment,
    out_average,
    small_params,
    small_moment,
    small_second,
    small_average,
    mix_weights,
    mix_moment,
    mix_second,
    mix_average,
):
    groups, count = lax.axis_size("tensor"), lax.axis_size("dp")
    rope = jnp.asarray(rope_lanes(in_streams.shape[1] * groups))
    (
        full_in,
        full_out,
        normed,
        joined,
        slope,
        heads,
        chances,
        newest,
        d_newest,
        d_branch,
        weights,
        row_grads,
        mix_in_grad,
        mix_out_grad,
    ) = forward(
        in_streams,
        in_weights,
        out_weights,
        small_params,
        rope,
        stored,
        cotangent,
        mix_weights,
        groups,
        count,
        0,
    )
    branch_grads, d_up, d_pre, d_normed, d_residual, bias_grads = backward(
        d_branch, rope, full_in, full_out, slope, heads, chances, groups, 1
    )
    grad_in, grad_out, d_flows, norm_grads, squares = scatter(
        normed,
        d_normed,
        branch_grads,
        joined,
        d_up,
        d_pre,
        in_streams,
        small_params,
        d_residual,
        d_newest,
        groups,
        count,
        2,
    )
    sums = small_sum(
        (norm_grads, row_grads, bias_grads, mix_in_grad, mix_out_grad, squares),
        axis_bits("dp") + axis_bits("tensor"),
        3,
    )
    results = finish(
        (grad_in, grad_out),
        sums,
        weights,
        newest,
        stored,
        cotangent,
        d_flows,
        (in_weights, in_moment, in_second, in_average),
        (out_weights, out_moment, output_second_moment, out_average),
        (small_params, small_moment, small_second, small_average),
        (mix_weights, mix_moment, mix_second, mix_average),
    )
    out_streams, grad_streams, grad_stored = results[-3:]
    return (out_streams, grad_streams, grad_stored, results[0][0, 0], *results[1:-3])


def solution(mesh):
    in_specs = (
        P(None, ("dp", "tensor"), None),
        P(None, ("dp", "tensor"), None),
        P(None, ("dp", "tensor"), None),
        P("dp", "tensor"),
        P("dp", "tensor"),
        P("dp", "tensor"),
        P("dp", "tensor"),
        P("dp", "tensor"),
        P("dp", "tensor"),
        P("dp", "tensor"),
        P("dp", "tensor"),
        P(),
        P(),
        P(),
        P(),
        P(),
        P(),
        P(),
        P(),
    )
    out_specs = (
        P(None, ("dp", "tensor"), None),
        P(None, ("dp", "tensor"), None),
        P(None, ("dp", "tensor"), None),
        P(),
        P("dp", "tensor"),
        P("dp", "tensor"),
        P("dp", "tensor"),
        P("dp", "tensor"),
        P("dp", "tensor"),
        P("dp", "tensor"),
        P("dp", "tensor"),
        P("dp", "tensor"),
        P("dp", "tensor"),
        P("dp", "tensor"),
        P(),
        P(),
        P(),
        P(),
        P(),
        P(),
        P(),
        P(),
    )
    return jax.shard_map(shards, mesh=mesh, in_specs=in_specs, out_specs=out_specs, check_vma=False)
```

time: 703 us -> 460 us (0.65)
  local copies, waits for them, and re-layouts: 112 us -> 2.35 us
  matrix products: 81.3 us -> 0 us
  other arithmetic: 78.4 us -> 0 us
  Pallas kernels: 401 us -> 448 us
  between operations: 19.9 us -> 1.29 us
    dot_general x21 -> x0, matrix products: 81.3 us -> none  [the longest x3 17.6 us: contract_first(): lax.dot_general(left_side, right_side, (((0,), (0,)), ((), ())), preferre...]
    pallas_call x3 -> x4, Pallas kernels: 213 us -> 270 us  [the longest x1 121 us: scatter(): pl.pallas_call(lambda *refs: scatter_kernel(size, count, *refs), out_shap...]
    unnamed x114 -> x14, local copies, waits for them, and re-layouts: 55.8 us -> 2.35 us
    slice x14 -> x0, local copies, waits for them, and re-layouts: 30 us -> none  [the longest x2 14.9 us: shards(): attn_weights = full_in[:, :attn_width].reshape(D, heads_group, 3, HD)]
    convert_element_type x5 -> x0, other arithmetic: 23 us -> none  [the longest x1 8.76 us: shards(): in_new[0].astype(bfloat)]
    concatenate x4 -> x0, other arithmetic: 18.9 us -> none  [the longest x1 17.3 us: shards(): grad_in = owned(jnp.concatenate([attn_part, up_part], axis=1))]
    reduce_sum x12 -> x0, other arithmetic: 17.4 us -> none  [the longest x2 5.64 us: shards(): big_square = jnp.sum(grad_in * grad_in) + jnp.sum(grad_out * grad_out)]
    dot_general x1 -> x0, local copies, waits for them, and re-layouts: 14.8 us -> none  [shards(): jnp.einsum('rsj,srd->jrd', mixing_weights, back_flows, precision=highest_...]
  transfers between devices with their start and end apart: 2 -> 0, of which waited for: 0 -> 0; matrix products, arithmetic and copies ran while one was open for 21% -> 0% of each run, Pallas kernels for 20% -> 0%
where the time goes in v3:
time: 460 us; the launch traced here: 452 us
  Pallas kernels  448 us (97%)
    pallas_call x1, Pallas kernels, forward(): pl.pallas_call(lambda *refs: forward_kernel(size, count, *refs), out_shap...  178 us
    pallas_call x1, Pallas kernels, scatter(): pl.pallas_call(lambda *refs: scatter_kernel(size, count, *refs), out_shap...  121 us
    pallas_call x1, Pallas kernels, backward(): pl.pallas_call(lambda *refs: backward_kernel(size, *refs), out_shape=[low...  81.6 us
    pallas_call x1, Pallas kernels, small_sum(): pl.pallas_call(lambda *refs: small_sum_kernel(bits, *refs), out_shape=jax...  35.8 us
    pallas_call x1, Pallas kernels, finish(): pl.pallas_call(finish_kernel, out_shape=[wide((1, 1))] + [entry for shape...  31.8 us

profile of v3, /device:TPU:0, one launch (start us, length us, event | category | flops | bytes accessed | tf_op | source)
XLA Modules:
  0.0 451.6 jit_solution(7014485998451969474)
XLA Ops:
  0.7 178.2 %forward_0.1 = (bf16[2048,3584]{1,0:T(8,128)(2,1)}, bf16[2048,2560]{1,0:T(8,128)(2,1)}, bf16[4,512,2048]{2,1,0:T(8,128)(2,1)}, bf16[512,2560]{1,0:T(8,128)(2,1)}...) custom-call(bf16[4,128,2048]{2,1,0:T(8,128)(2,1)} %refs_6_.4, ...), custom_call_target="tpu_custom_call" | custom-call | tf_op jit(solution)/shard_map/forward_0/pallas_call | solution.py:860
  178.9 81.6 %backward_1.1 = (bf16[512,2048]{1,0:T(8,128)(2,1)}, bf16[512,2048]{1,0:T(8,128)(2,1)}, bf16[3,512,512]{2,1,0:T(8,128)(2,1)}, bf16[3,512,2048]{2,1,0:T(8,128)(2,1...) custom-call(bf16[128,2048]{1,0:T(8,128)(2,1)} %get-tuple-element.70.refs_0_, f32[3,512,128]{2,1,0:T(8,128)} %constant.2.clone.refs_4_.refs_1_, ...), custom_call_target="tpu_custom_call" | custom-call | tf_op jit(solution)/shard_map/backward_1/pallas_call | solution.py:1182
  260.5 0.0 copy-start.1
  260.5 0.0 copy-start.2
  260.5 0.0 copy-start.3
  260.5 0.0 copy-start.5
  260.5 120.6 %scatter_2.1 = (bf16[256,3584]{1,0:T(8,128)(2,1)}, bf16[256,2560]{1,0:T(8,128)(2,1)}, bf16[4,128,2048]{2,1,0:T(8,128)(2,1)}, f32[8,2048]{1,0:T(8,128)}, f32[8,128]{1,0:T(8,128)}) custom-call(bf16[4,512,2048]{2,1,0:T(8,128)(2,1)} %get-tuple-element.69.refs_0_, bf16[3,512,2048]{2,1,0:T(8,128)(2,1)} %get-tuple-element.76.refs_1_, ...), custom_call_target="tpu_custom_call" | custom-call | tf_op jit(solution)/shard_map/scatter_2/pallas_call | solution.py:1572
  381.1 0.0 copy-done.1
  381.1 0.0 copy-done.2
  381.1 0.0 copy-done.3
  381.1 0.0 copy-done.5
  381.1 0.0 copy-start.4
  381.1 0.8 copy-done.4
  382.0 0.0 copy-start.6
  382.0 0.7 copy-done.6
  382.6 35.8 %small_sum_3.1.sums = f32[64,2048]{1,0:T(8,128)S(1)} custom-call(f32[8,2048]{1,0:T(8,128)S(1)} %copy-done.4, f32[8,2048]{1,0:T(8,128)S(1)} %copy-done.2, f32[8,2048]{1,0:T(8,128)S(1)} %copy-done.3, f32[40,2048]{1,0:T(8,128)S(1)} %copy-done.1, f32[40,128]{1,0:T(8,128)S(1)} %copy-done.5, f32[8,128]{1,0:T(8,128)S(1)} %copy-done.6), custom_call_target="tpu_custom_call" | custom-call | tf_op jit(solution)/shard_map/small_sum_3/pallas_call | solution.py:1659
  418.5 0.0 copy-start
  418.5 0.8 copy-done
  419.3 31.8 %finish.1 = (f32[1,1]{1,0:T(1,128)}, f32[256,3584]{1,0:T(8,128)}, f32[256,3584]{1,0:T(8,128)}, f32[256,3584]{1,0:T(8,128)}, f32[256,3584]{1,0:T(8,128)}, /*index...) custom-call(bf16[256,3584]{1,0:T(8,128)(2,1)} %get-tuple-element.83., ...), custom_call_target="tpu_custom_call" | custom-call | tf_op jit(solution)/shard_map/finish/pallas_call | solution.py:1853
Async XLA Ops:
  260.5 120.6 %copy-start.1 = (f32[40,2048]{1,0:T(8,128)S(1)}, f32[40,2048]{1,0:T(8,128)}, u32[]{:S(2)}) copy-start(f32[40,2048]{1,0:T(8,128)} %get-tuple-element.88.refs_3_) | copy-start | bytes 983044
  260.5 120.6 %copy-start.2 = (f32[8,2048]{1,0:T(8,128)S(1)}, f32[8,2048]{1,0:T(8,128)}, u32[]{:S(2)}) copy-start(f32[8,2048]{1,0:T(8,128)} %get-tuple-element.86.refs_1_) | copy-start | bytes 196612
  260.5 120.6 %copy-start.3 = (f32[8,2048]{1,0:T(8,128)S(1)}, f32[8,2048]{1,0:T(8,128)}, u32[]{:S(2)}) copy-start(f32[8,2048]{1,0:T(8,128)} %get-tuple-element.87.refs_2_) | copy-start | bytes 196612
  260.5 120.6 %copy-start.5 = (f32[40,128]{1,0:T(8,128)S(1)}, f32[40,128]{1,0:T(8,128)}, u32[]{:S(2)}) copy-start(f32[40,128]{1,0:T(8,128)} %get-tuple-element.89.refs_4_) | copy-start | bytes 61444
  381.1 0.8 copy-start.4
  382.0 0.7 copy-start.6
  418.5 0.8 copy-start

commit v4 on v3

--- a/solution.py
+++ b/solution.py
@@ -157,62 +157,123 @@
                         self.hop(way, dest, place).wait_send()
 
 
-def cube_sum_steps(bits, value, out, total, landing, send_a, recv_a, send_b, recv_b):
-    rows, columns = value.shape
-
-    def partner(axis, size):
-        place = lax.axis_index(axis)
-        bit = lax.rem(place // size, 2)
-        return bit, {axis: place + (1 - 2 * bit) * size}
-
-    ends = [partner(*entry) for entry in bits]
-    enter([(jnp.bool_(True), device) for _, device in ends])
-    total[...] = value[...]
-    regions = [(0, rows, 0, columns)]
-    for step, (bit, device) in enumerate(ends):
-        r, n, c, m = regions[-1]
-        if n > 8:
-            n = n // 2
-            keep, give = (r + bit * n, n, c, m), (r + (1 - bit) * n, n, c, m)
-        else:
-            m = m // 2
-            keep, give = (r, n, c + bit * m, m), (r, n, c + (1 - bit) * m, m)
-        regions.append(keep)
-
-        def spot(region):
-            return (
-                pl.ds(pl.multiple_of(region[0], 8), region[1]),
-                pl.ds(pl.multiple_of(region[2], 128), region[3]),
-            )
-
-        copy = pltpu.make_async_remote_copy(
-            src_ref=total.at[spot(give)],
-            dst_ref=landing.at[step, pl.ds(0, n), pl.ds(0, m)],
-            send_sem=send_a.at[step],
-            recv_sem=recv_a.at[step],
-            device_id=device,
+class FlatSum:
+    def __init__(self, count, size, value, out, landing, crossing, sems):
+        self.count, self.size, self.value, self.out = count, size, value, out
+        self.landing, self.crossing = landing, crossing
+        self.send_a, self.recv_a, self.send_b, self.recv_b, self.send_c, self.recv_c = sems
+        self.me = lax.axis_index("dp")
+        self.here = lax.axis_index("tensor")
+        self.across = min(count, D // HD)
+        self.rows, self.lanes = landing.shape[1:]
+
+    def part(self, ref, owner):
+        row = pl.multiple_of(owner // self.across * self.rows, 8)
+        lane = pl.multiple_of(lax.rem(owner, self.across) * self.lanes, HD)
+        return ref.at[pl.ds(row, self.rows), pl.ds(lane, self.lanes)]
+
+    def over(self, first, action):
+        total, place = (self.count, self.me) if first else (self.size, self.here)
+
+        def one(step, carry):
+            action(lax.rem(place + step, total))
+            return carry
+
+        lax.fori_loop(1, total, one, 0)
+
+    def to_owner(self, other):
+        return pltpu.make_async_remote_copy(
+            src_ref=self.part(self.value, other),
+            dst_ref=self.landing.at[self.me],
+            send_sem=self.send_a.at[other],
+            recv_sem=self.recv_a.at[self.me],
+            device_id={"dp": other},
             device_id_type=MESH,
         )
-        copy.start()
-        copy.wait()
-        total[spot(keep)] += landing[step, pl.ds(0, n), pl.ds(0, m)]
-    out[spot(regions[-1])] = total[spot(regions[-1])]
-    for step in range(len(ends) - 1, -1, -1):
-        region = out.at[spot(regions[step + 1])]
-        copy = pltpu.make_async_remote_copy(
-            src_ref=region,
-            dst_ref=region,
-            send_sem=send_b.at[step],
-            recv_sem=recv_b.at[step],
-            device_id=ends[step][1],
+
+    def across_to(self, other):
+        return pltpu.make_async_remote_copy(
+            src_ref=self.crossing.at[self.here],
+            dst_ref=self.crossing.at[self.here],
+            send_sem=self.send_b.at[other],
+            recv_sem=self.recv_b.at[self.here],
+            device_id={"tensor": other},
             device_id_type=MESH,
         )
-        copy.start()
-        copy.wait()
-
-
-def axis_bits(axis):
-    return [(axis, 2**bit) for bit in range(lax.axis_size(axis).bit_length() - 1)]
+
+    def back_to(self, other):
+        return pltpu.make_async_remote_copy(
+            src_ref=self.part(self.out, self.me),
+            dst_ref=self.part(self.out, self.me),
+            send_sem=self.send_c.at[other],
+            recv_sem=self.recv_c.at[self.me],
+            device_id={"dp": other},
+            device_id_type=MESH,
+        )
+
+    def arrive(self, block, send, recv, other, axis):
+        pltpu.make_async_remote_copy(
+            src_ref=block,
+            dst_ref=block,
+            send_sem=send.at[other],
+            recv_sem=recv.at[other],
+            device_id={axis: other},
+            device_id_type=MESH,
+        ).wait_recv()
+
+    def first(self):
+        self.over(True, lambda other: self.to_owner(other).start())
+
+    def second(self):
+        self.crossing[self.here] = self.part(self.value, self.me)[...]
+
+        def add(other):
+            self.arrive(self.landing.at[other], self.send_a, self.recv_a, other, "dp")
+            self.crossing[self.here] += self.landing[other]
+
+        self.over(True, add)
+        self.over(False, lambda other: self.across_to(other).start())
+
+    def third(self):
+        self.over(
+            False,
+            lambda other: self.arrive(
+                self.crossing.at[other], self.send_b, self.recv_b, other, "tensor"
+            ),
+        )
+        result = self.crossing[0]
+        for other in range(1, self.size):
+            result = result + self.crossing[other]
+        self.part(self.out, self.me)[...] = result
+        self.over(True, lambda other: self.back_to(other).start())
+
+    def last(self):
+        self.over(
+            True,
+            lambda other: self.arrive(
+                self.part(self.out, other), self.send_c, self.recv_c, other, "dp"
+            ),
+        )
+        self.over(True, lambda other: self.to_owner(other).wait_send())
+        self.over(False, lambda other: self.across_to(other).wait_send())
+        self.over(True, lambda other: self.back_to(other).wait_send())
+
+    def partners(self):
+        def others(place, total):
+            return [lax.rem(place + step, total) for step in range(1, total)]
+
+        return [{"dp": other} for other in others(self.me, self.count)] + [
+            {"tensor": other} for other in others(self.here, self.size)
+        ]
+
+
+def flat_scratch(rows, count, size):
+    across = min(count, D // HD)
+    part = (rows * across // count, D // across)
+    return [
+        pltpu.VMEM((count,) + part, single),
+        pltpu.VMEM((size,) + part, single),
+    ] + [pltpu.SemaphoreType.DMA((n,)) for n in (count, count, size, size, count, count)]
 
 
 def plus_flips(place, bits):
@@ -273,8 +334,8 @@
         return found
 
     def start(self):
-        for piece in range(len(self.routes)):
-            for copy in self.sends_of(piece, ()):
+        for copies in zip(*(self.sends_of(piece, ()) for piece in range(len(self.routes)))):
+            for copy in copies:
                 copy.start()
 
     def step(self, index):
@@ -338,9 +399,7 @@
     d_newest,
     d_branch,
     weights,
-    row_grads,
-    mix_in_grad,
-    mix_out_grad,
+    early_grads,
     w_in_low,
     w_out_low,
     normed,
@@ -463,7 +522,7 @@
             flow_sem.at[flow, block],
         )
 
-    for flow in FLOW_ORDER:
+    def send_normal(flow):
         which = 2 if flow == 3 else 0
 
         def normalize(index, carry):
@@ -485,10 +544,13 @@
 
     cube_in = CubeGather(w_in_low, rows_in, count, cube_sems[:4])
     cube_out = CubeGather(w_out_low, rows_in, count, cube_sems[4:])
+    send_normal(FLOW_ORDER[0])
     settle(w_in, width_in, w_in_low)
     cube_in.start()
     for copy in stage(w_out, width_out):
         copy.start()
+    for flow in FLOW_ORDER[1:]:
+        send_normal(flow)
     settle(w_out, width_out, w_out_low)
     mix_low[...] = jnp.zeros_like(mix_low)
     mix_low[0:MIXH] = small[SMALL_MIX : SMALL_MIX + MIXH].astype(bfloat)
@@ -589,13 +651,11 @@
 
         lax.fori_loop(0, units // tile, one, 0)
 
-    def contract(block):
-        rows = rows_of(block)
-
+    def contract():
         def one(index, carry):
             first = pl.multiple_of(index * tile, tile)
-            total[rows, pl.ds(first, tile)] = contract_last(
-                joined[rows, pl.ds(head_width, units)],
+            total[:, pl.ds(first, tile)] = contract_last(
+                joined[:, pl.ds(head_width, units)],
                 w_out_low[pl.ds(first, tile), pl.ds(head_width, units)],
             )
             return carry
@@ -617,8 +677,7 @@
                 low, heads[2, :, lanes], preferred_element_type=single
             ).astype(bfloat)
 
-    def finish_block(block):
-        attend(block)
+    def emit(block):
         rows = rows_of(block)
 
         def one(index, carry):
@@ -681,28 +740,32 @@
         pl.when(lower)(lambda: query_side(1, -1))
         pl.when(jnp.logical_not(lower))(lambda: query_side(0, 1))
 
+        def one(index, carry):
+            project(lax.rem(here + 1 + index, size), 0)
+            return carry
+
+        lax.fori_loop(0, size - 1, one, 0)
+
+        def two(block, carry):
+            attend(block)
+            return carry
+
+        lax.fori_loop(0, size, two, 0)
+
+    for step in range(3, size):
+        line_step(step, FLOW_ORDER[:3])
+        at_distance(step, early)
+    pl.when(ending)(lambda: attend(here))
     for index in range(1, cube_out.steps()):
         cube_out.step(index)
     cube_out.finish()
     save(1, w_out_low, all_out).start()
-    for step in range(min(3, size)):
-        at_distance(step, contract)
-    for step in range(3, size):
-        line_step(step, FLOW_ORDER[:3])
-
-        def rest(block):
-            early(block)
-            contract(block)
-
-        at_distance(step, rest)
-    finish_block(here)
+    contract()
 
     @pl.when(jnp.logical_not(ending))
     def _():
         def one(index, carry):
-            block = lax.rem(here + 1 + index, size)
-            project(block, 0)
-            finish_block(block)
+            emit(lax.rem(here + 1 + index, size))
             return carry
 
         lax.fori_loop(0, size - 1, one, 0)
@@ -725,11 +788,13 @@
             ).wait_recv()
             keep_flow(0, dest).start()
             project(dest, 0)
-            finish_block(dest)
+            attend(dest)
+            emit(dest)
 
         for way in (chain.near, -chain.near):
             chain.relay(way, chain.far(rank, way))
 
+    emit(here)
     saves = [
         save(2, joined, joined_out),
         save(3, slope, slope_out),
@@ -786,18 +851,21 @@
         precision=highest_precision,
         preferred_element_type=single,
     )
-    mix_out_grad[...] = jnp.zeros_like(mix_out_grad)
-    mix_out_grad[0:MIXH] = out_grad[0:MIXH]
-    mix_out_grad[MIXH : MIXH + 1] = jnp.sum(d_mixing, axis=0, keepdims=True)
+    scales_sum = jnp.sum(d_mixing, axis=0, keepdims=True)
+    early_grads[MIXH:] = jnp.zeros((early_grads.shape[0] - MIXH, D), single)
+    for place in range((MIXH + 7) // 8):
+        rows_left = min(8, MIXH - place * 8)
+        early_grads[40 : 40 + rows_left, place * HD : (place + 1) * HD] = out_grad[
+            place * 8 : place * 8 + rows_left
+        ]
+    early_grads[40 + MIXH % 8 : 41 + MIXH % 8, MIXH // 8 * HD : MIXH // 8 * HD + HD] = scales_sum
 
     def spread(index, carry):
         lanes = pl.ds(pl.multiple_of(index * tile, tile), tile)
         total[0:own, lanes] = jnp.dot(
             d_mix_pre, mix_low[:, lanes], preferred_element_type=single
         )
-        mix_in_grad[:, lanes] = contract_first(d_mix_pre, give[rows_of(here), lanes])[
-            0 : mix_in_grad.shape[0]
-        ]
+        early_grads[0:MIXH, lanes] = contract_first(d_mix_pre, give[rows_of(here), lanes])[0:MIXH]
         return carry
 
     lax.fori_loop(0, D // tile, spread, 0)
@@ -823,8 +891,8 @@
         return carry
 
     lax.fori_loop(0, own // 16, descend, 0)
-    row_grads[0:1] = jnp.sum(sums[0], axis=0, keepdims=True)
-    row_grads[1:2] = jnp.sum(sums[1], axis=0, keepdims=True)
+    early_grads[MIXH : MIXH + 1] = jnp.sum(sums[0], axis=0, keepdims=True)
+    early_grads[MIXH + 1 : MIXH + 2] = jnp.sum(sums[1], axis=0, keepdims=True)
     for step in range(size):
         for flow in FLOW_ORDER:
             for side, way in sides:
@@ -871,12 +939,10 @@
             jax.ShapeDtypeStruct((own, D), single),
             low(own, D),
             jax.ShapeDtypeStruct((own, HD), single),
-            jax.ShapeDtypeStruct((8, D), single),
-            jax.ShapeDtypeStruct((40, D), single),
-            jax.ShapeDtypeStruct((40, HD), single),
+            jax.ShapeDtypeStruct((48, D), single),
         ],
         in_specs=[vmem, hbm, hbm, vmem, vmem, hbm, hbm, vmem],
-        out_specs=[hbm] * 7 + [vmem] * 7,
+        out_specs=[hbm] * 7 + [vmem] * 5,
         scratch_shapes=[
             pltpu.VMEM((D, width_in), bfloat),
             pltpu.VMEM((D, width_out), bfloat),
@@ -910,70 +976,140 @@
             collective_id=identity, has_side_effects=True, vmem_limit_bytes=60 * 2**20
         ),
         name="forward_%d" % identity,
-    )(flows, w_in, w_out, small, rope, stored, cotangent, mix_weights)
+    )(flows, w_in, w_out, small, jnp.asarray(rope), stored, cotangent, mix_weights)
 
 
 def backward_kernel(
     size,
+    count,
     d_branch,
+    early_grads,
     rope,
     all_in,
     all_out,
     slope_in,
     heads_in,
     chances_in,
-    all_back,
-    all_up,
-    all_pre,
+    joined_in,
     all_normed,
-    d_residual,
-    bias_grads,
-    w_in_low,
-    w_out_low,
-    slope,
+    flows_in,
+    small,
+    grad_in,
+    grad_out,
+    d_flows,
+    early_sums,
+    late_sums,
+    arena,
+    give,
+    wide,
     heads,
     chances,
     back,
-    d_heads,
     d_up,
     d_pre,
-    part,
+    parts,
     terms,
-    d_normed,
+    flows,
+    total,
+    sums,
+    work,
+    late,
+    squares,
+    arena_sem,
     load_sem,
+    tile_sem,
+    flow_sem,
+    keep_sem,
+    save_sem,
     line_send,
     line_recv,
     term_send,
     term_recv,
-    save_sem,
+    give_sem,
+    pair_sem,
+    credit,
+    ready,
+    cube_send,
+    cube_recv,
+    *flat_refs,
 ):
     here = lax.axis_index("tensor")
-    own = d_branch.shape[0]
+    me = lax.axis_index("dp")
+    bits = count.bit_length() - 1
+    routes = cube_routes(bits)
+    pieces = len(routes)
+    subsets = sorted(routes[0][0], key=lambda held: -len(held))
+    last = len(subsets) - 1
+    own = flows.shape[1]
     length = own * size
+    tile = arena.shape[2]
     head_width = heads.shape[2]
     group_heads = head_width // HD
-    attn_width = 3 * head_width
-    units = slope.shape[1]
+    units = d_up.shape[1]
+    tiles_out = (head_width + units) // tile
+    tiles_in = (3 * head_width + units) // tile
+    first_up = tiles_out + 3 * head_width // tile
+    groups = (
+        (0, tiles_out),
+        (tiles_out, first_up - tiles_out),
+        (first_up, tiles_out + tiles_in - first_up),
+    )
+    give_first = (0, tiles_out, 0)
+    rows = D // count
+    piece_rows = rows // pieces
+    lane_rows = max(rows, HD)
+    kept_first, land_first, pair_first = 0, D // 2, D - rows
     sides = ((0, 1), (1, -1))
-    tile = 512
     scale = HD ** (-0.5)
+    ending = jnp.logical_or(here == 0, here == size - 1)
 
     def rows_of(block):
         return pl.ds(pl.multiple_of(block * own, own), own)
 
-    loads = [
-        pltpu.make_async_copy(source, target, load_sem.at[place])
-        for place, (source, target) in enumerate(
-            [
-                (all_out, w_out_low),
-                (slope_in, slope),
-                (all_in, w_in_low),
-                (heads_in, heads),
-                (chances_in, chances),
-            ]
-        )
-    ]
-    enter([(here < size - 1, {"tensor": here + 1}), (here > 0, {"tensor": here - 1})])
+    def load_arena(index):
+        source, place = (all_out, index) if index < tiles_out else (all_in, index - tiles_out)
+        return pltpu.make_async_copy(
+            source.at[:, pl.ds(place * tile, tile)], arena.at[index], arena_sem.at[index]
+        )
+
+    load_branch = pltpu.make_async_copy(d_branch, back.at[rows_of(here)], load_sem.at[0])
+    load_slope = pltpu.make_async_copy(slope_in, wide.at[:, pl.ds(0, units)], load_sem.at[1])
+    load_heads = pltpu.make_async_copy(heads_in, heads, load_sem.at[2])
+    load_chances = pltpu.make_async_copy(chances_in, chances, load_sem.at[3])
+    load_joined = pltpu.make_async_copy(joined_in, wide, load_sem.at[4])
+
+    def load_flow(flow):
+        return pltpu.make_async_copy(
+            flows_in.at[flow], flows.at[flow % 2], flow_sem.at[flow % 2]
+        )
+
+    def keep_flow(flow):
+        return pltpu.make_async_copy(
+            flows.at[flow % 2], d_flows.at[flow], keep_sem.at[flow % 2]
+        )
+
+    load_rope = pltpu.make_async_copy(
+        rope, total.at[:, pl.ds(0, rope.shape[1])], load_sem.at[5]
+    )
+    load_branch.start()
+    load_rope.start()
+    for index in range(tiles_out):
+        load_arena(index).start()
+    load_slope.start()
+    for index in range(first_up, tiles_out + tiles_in):
+        load_arena(index).start()
+    load_heads.start()
+    load_chances.start()
+    for index in range(tiles_out, first_up):
+        load_arena(index).start()
+    load_flow(3).start()
+    load_flow(0).start()
+    half = len(flat_refs) // 2
+    early = FlatSum(count, size, early_grads, early_sums, *flat_refs[:2], flat_refs[2:half])
+    final = FlatSum(
+        count, size, late, late_sums, *flat_refs[half : half + 2], flat_refs[half + 2 :]
+    )
+    enter([(jnp.bool_(True), partner) for partner in early.partners()])
 
     def has_next(way):
         return here < size - 1 if way > 0 else here > 0
@@ -984,7 +1120,7 @@
     def line_hop(side, way, step):
         block = back.at[rows_of(here - way * step)]
         return pltpu.make_async_remote_copy(
-            src_ref=d_branch if step == 0 else block,
+            src_ref=block,
             dst_ref=block,
             send_sem=line_send.at[side, step],
             recv_sem=line_recv.at[side, step],
@@ -1003,54 +1139,68 @@
             device_id_type=MESH,
         )
 
+    load_branch.wait()
     for side, way in sides:
         pl.when(has_next(way))(line_hop(side, way, 0).start)
-    for copy in loads:
-        copy.start()
-    back[rows_of(here)] = d_branch[...]
+    early.first()
 
     def pull(block):
-        rows = rows_of(block)
-        d_heads[rows] = jnp.dot(
-            back[rows], w_out_low[:, 0:head_width], preferred_element_type=single
+        spot = rows_of(block)
+        wide[spot, pl.ds(units, head_width)] = jnp.dot(
+            back[spot], arena[0], preferred_element_type=single
         ).astype(bfloat)
 
         def one(index, carry):
-            first = pl.multiple_of(index * tile, tile)
+            lanes = pl.ds(pl.multiple_of(index * tile, tile), tile)
             d_hidden = jnp.dot(
-                back[rows],
-                w_out_low[:, pl.ds(head_width + first, tile)],
-                preferred_element_type=single,
+                back[spot], arena[head_width // tile + index], preferred_element_type=single
             )
-            d_up[rows, pl.ds(first, tile)] = (
-                d_hidden * slope[rows, pl.ds(first, tile)].astype(single)
-            ).astype(bfloat)
+            d_up[spot, lanes] = (d_hidden * wide[spot, lanes].astype(single)).astype(bfloat)
             return carry
 
         lax.fori_loop(0, units // tile, one, 0)
 
     def push(block):
-        rows = rows_of(block)
+        spot = rows_of(block)
 
         def one(index, carry):
-            first = pl.multiple_of(index * tile, tile)
-            part[rows, pl.ds(first, tile)] = contract_last(
-                d_up[rows], w_in_low[pl.ds(first, tile), pl.ds(attn_width, units)]
-            ).astype(bfloat)
+            lanes = pl.ds(pl.multiple_of(index * tile, tile), tile)
+            value = None
+            for place in range(units // tile):
+                term = contract_last(
+                    d_up[spot, pl.ds(place * tile, tile)], arena[first_up + place, lanes]
+                )
+                value = term if value is None else value + term
+            parts[3, spot, lanes] = value.astype(bfloat)
             return carry
 
         lax.fori_loop(0, D // tile, one, 0)
 
-    chain = LineSum(size, part, terms, term_send, term_recv, CUT)
-    ending = jnp.logical_or(here == 0, here == size - 1)
-
-    def stage(step):
-        for way in (chain.near, -chain.near):
-            chain.relay(way, chain.far(size - 1 - step, way))
-
-    loads[0].wait()
-    loads[1].wait()
+    chains = [
+        LineSum(
+            size,
+            parts.at[flow],
+            terms.at[flow],
+            term_send.at[flow],
+            term_recv.at[flow],
+            CUT if flow == 3 else 1,
+        )
+        for flow in range(STREAMS)
+    ]
+
+    def relay(flow, rank):
+        for sign in (1, -1):
+            way = sign * chains[flow].near
+            chains[flow].relay(way, chains[flow].far(rank, way))
+
+    def middle(action):
+        pl.when(jnp.logical_not(ending))(action)
+
+    for index in range(tiles_out):
+        load_arena(index).wait()
+    load_slope.wait()
     pull(here)
+    early.second()
     for step in range(1, size):
         for side, way in sides:
 
@@ -1060,7 +1210,8 @@
                 pl.when(has_next(way))(line_hop(side, way, step).start)
 
         if step == 1:
-            loads[2].wait()
+            for index in range(first_up, tiles_out + tiles_in):
+                load_arena(index).wait()
 
         def both(side, carry):
             block = here - step + 2 * step * side
@@ -1073,300 +1224,145 @@
             return carry
 
         lax.fori_loop(0, 2, both, 0)
-        pl.when(ending)(lambda: stage(step))
-    saves = [
-        pltpu.make_async_copy(source, target, save_sem.at[place])
-        for place, (source, target) in enumerate(
-            [(back, all_back), (d_up, all_up), (d_pre, all_pre)]
-        )
-    ]
-    saves[0].start()
-    saves[1].start()
-    loads[3].wait()
-    loads[4].wait()
-    bias_grads[...] = jnp.zeros_like(bias_grads)
+        pl.when(ending)(lambda: relay(3, size - 1 - step))
+        if step == min(2, size - 1):
+            early.third()
+
+    def tell(which):
+        for bit in range(bits):
+            pl.semaphore_signal(
+                ready.at[which, bit],
+                inc=1,
+                device_id={"dp": plus_flips(me, (bit,))},
+                device_id_type=MESH,
+            )
+
+    tell(0)
+    load_heads.wait()
+    load_chances.wait()
     half_rows = length // 2
-
-    def turn_back(gradients, rows):
+    late[...] = jnp.zeros_like(late)
+
+    load_rope.wait()
+
+    def turn_back(gradients, first, blocks):
+        def table(kind):
+            return jnp.concatenate(
+                [
+                    total[:, (kind * size + block) * HD : (kind * size + block + 1) * HD]
+                    for block in range(first, first + blocks)
+                ],
+                axis=0,
+            )
+
         return (
-            gradients * rope[0, rows]
-            - pltpu.roll(gradients, HD - ROT // 2, 1) * rope[1, rows]
-            - pltpu.roll(gradients, ROT // 2, 1) * rope[2, rows]
+            gradients * table(0)
+            - pltpu.roll(gradients, HD - ROT // 2, 1) * table(1)
+            - pltpu.roll(gradients, ROT // 2, 1) * table(2)
         )
 
     for head in range(group_heads):
         lanes = pl.ds(head * HD, HD)
+        d_lanes = pl.ds(units + head * HD, HD)
         d_keys = jnp.zeros((length, HD), single)
         d_values = jnp.zeros((length, HD), single)
         query_bias = jnp.zeros((1, HD), single)
-        for half in range(2):
-            rows = pl.ds(half * half_rows, half_rows)
-            low = chances[head, rows]
+        for place in range(2):
+            spot = pl.ds(place * half_rows, half_rows)
+            low = chances[head, spot]
             chance = low.astype(single)
-            d_chance = contract_last(d_heads[rows, lanes], heads[2, :, lanes])
+            d_chance = contract_last(wide[spot, d_lanes], heads[2, :, lanes])
             centre = jnp.sum(d_chance * chance, axis=-1, keepdims=True)
             d_score = (chance * (d_chance - centre)).astype(bfloat)
-            d_query = (
-                jnp.dot(d_score, heads[1, :, lanes], preferred_element_type=single) * scale
-            )
-            d_query = turn_back(d_query, rows).astype(bfloat)
-            d_pre[0, rows, lanes] = d_query
+            d_query = jnp.dot(d_score, heads[1, :, lanes], preferred_element_type=single) * scale
+            d_query = turn_back(d_query, place * size // 2, size // 2).astype(bfloat)
+            d_pre[0, spot, lanes] = d_query
             query_bias = query_bias + jnp.sum(d_query.astype(single), axis=0, keepdims=True)
-            d_keys = d_keys + contract_first(d_score, heads[0, rows, lanes])
-            d_values = d_values + contract_first(low, d_heads[rows, lanes])
-        whole = pl.ds(0, length)
-        d_key = turn_back(d_keys * scale, whole).astype(bfloat)
+            d_keys = d_keys + contract_first(d_score, heads[0, spot, lanes])
+            d_values = d_values + contract_first(low, wide[spot, d_lanes])
+        d_key = turn_back(d_keys * scale, 0, size).astype(bfloat)
         d_value = d_values.astype(bfloat)
         d_pre[1, :, lanes] = d_key
         d_pre[2, :, lanes] = d_value
-        bias_grads[0:1, lanes] = query_bias
-        bias_grads[1:2, lanes] = jnp.sum(d_key.astype(single), axis=0, keepdims=True)
-        bias_grads[2:3, lanes] = jnp.sum(d_value.astype(single), axis=0, keepdims=True)
-    saves[2].start()
-    for step in range(1, size - 1):
-        pl.when(jnp.logical_not(ending))(lambda: stage(step))
-    for which in range(3):
-
-        def one(index, carry):
-            first = pl.multiple_of(index * tile, tile)
-            d_normed[which, :, pl.ds(first, tile)] = contract_last(
-                d_pre[which],
-                jnp.concatenate(
-                    [
-                        w_in_low[pl.ds(first, tile), pl.ds((head * 3 + which) * HD, HD)]
-                        for head in range(group_heads)
-                    ],
-                    axis=1,
-                ),
-            ).astype(bfloat)
-            return carry
-
-        lax.fori_loop(0, D // tile, one, 0)
-        saves.append(
-            pltpu.make_async_copy(
-                d_normed.at[which], all_normed.at[which], save_sem.at[3 + which]
-            )
-        )
-        saves[-1].start()
-    push(here)
-    def unit_sum(index, carry):
-        lanes = pl.ds(pl.multiple_of(index * 256, 256), 256)
-        bias_grads[3:4, lanes] = jnp.sum(d_up[:, lanes].astype(single), axis=0, keepdims=True)
-        return carry
-
-    lax.fori_loop(0, units // 256, unit_sum, 0)
-    pl.when(jnp.logical_not(ending))(lambda: stage(size - 1))
-    for place in range(CUT):
-        chain.collect(place, d_residual)
-    for step in range(size):
-        for side, way in sides:
-
-            @pl.when(jnp.logical_and(has_next(way), has_origin(way, step)))
-            def _():
-                line_hop(side, way, step).wait_send()
-
-    chain.drain()
-    for copy in saves:
-        copy.wait()
-
-
-def backward(d_branch, rope, all_in, all_out, slope, heads, chances, size, identity):
-    own = d_branch.shape[0]
-    length = own * size
-    head_width = heads.shape[2]
-    units = slope.shape[1]
-    low = lambda *shape: jax.ShapeDtypeStruct(shape, bfloat)
-    wide = lambda *shape: jax.ShapeDtypeStruct(shape, single)
-    hbm = pl.BlockSpec(memory_space=pl.ANY)
-    vmem = pl.BlockSpec(memory_space=pltpu.VMEM)
-    return pl.pallas_call(
-        lambda *refs: backward_kernel(size, *refs),
-        out_shape=[
-            low(length, D),
-            low(length, units),
-            low(3, length, head_width),
-            low(3, length, D),
-            wide(own, D),
-            wide(8, D),
-        ],
-        in_specs=[vmem] * 2 + [hbm] * 5,
-        out_specs=[hbm] * 4 + [vmem] * 2,
-        scratch_shapes=[
-            pltpu.VMEM(all_in.shape, bfloat),
-            pltpu.VMEM(all_out.shape, bfloat),
-            pltpu.VMEM(slope.shape, bfloat),
-            pltpu.VMEM(heads.shape, bfloat),
-            pltpu.VMEM(chances.shape, bfloat),
-            pltpu.VMEM((length, D), bfloat),
-            pltpu.VMEM((length, head_width), bfloat),
-            pltpu.VMEM((length, units), bfloat),
-            pltpu.VMEM((3, length, head_width), bfloat),
-            pltpu.VMEM((length, D), bfloat),
-            pltpu.VMEM((size + 1, own, D), bfloat),
-            pltpu.VMEM((3, length, D), bfloat),
-            pltpu.SemaphoreType.DMA((5,)),
-            pltpu.SemaphoreType.DMA((2, size)),
-            pltpu.SemaphoreType.DMA((2, size)),
-            pltpu.SemaphoreType.DMA((2, size, CUT)),
-            pltpu.SemaphoreType.DMA((2, size, CUT)),
-            pltpu.SemaphoreType.DMA((6,)),
-        ],
-        compiler_params=pltpu.CompilerParams(
-            collective_id=identity, has_side_effects=True, vmem_limit_bytes=60 * 2**20
-        ),
-        name="backward_%d" % identity,
-    )(d_branch, rope, all_in, all_out, slope, heads, chances)
-
-
-def scatter_kernel(
-    size,
-    count,
-    all_normed,
-    d_normed,
-    back_in,
-    joined_in,
-    up_in,
-    pre_in,
-    flows_in,
-    small,
-    d_residual,
-    d_newest,
-    grad_in,
-    grad_out,
-    d_flows,
-    norm_grads,
-    squares,
-    back,
-    joined,
-    d_up,
-    d_pre,
-    tiles,
-    kept_in,
-    kept_out,
-    pair_in,
-    pair_out,
-    give_in,
-    give_out,
-    land_in,
-    land_out,
-    parts,
-    terms,
-    flows,
-    total,
-    sums,
-    work,
-    load_sem,
-    tile_sem,
-    flow_sem,
-    give_sem,
-    pair_sem,
-    credit,
-    cube_send,
-    cube_recv,
-    line_send,
-    line_recv,
-    save_sem,
-):
-    here = lax.axis_index("tensor")
-    me = lax.axis_index("dp")
-    bits = count.bit_length() - 1
-    routes = cube_routes(bits)
-    pieces = len(routes)
-    subsets = sorted(routes[0][0], key=lambda held: -len(held))
-    own = flows.shape[1]
-    length = own * size
-    rows = pair_in.shape[0]
-    piece_rows = rows // pieces
-    lane_rows = tiles.shape[3]
-    head_width = d_pre.shape[2]
-    group_heads = head_width // HD
-    attn_width = 3 * head_width
-    units = d_up.shape[1]
-    tile = 512
-    kept, pair, give, land = (
-        (kept_out, kept_in),
-        (pair_out, pair_in),
-        (give_out, give_in),
-        (land_out, land_in),
-    )
-    widths = (kept_out.shape[1], kept_in.shape[1])
-
-    loads = [
-        pltpu.make_async_copy(source, target, load_sem.at[place])
-        for place, (source, target) in enumerate(
-            [(d_normed.at[which], parts.at[which]) for which in range(3)]
-            + [(back_in, back), (joined_in, joined), (up_in, d_up), (pre_in, d_pre)]
-        )
-    ]
+        bias_lanes = pl.ds(pl.multiple_of(here * head_width + head * HD, HD), HD)
+        late[4:5, bias_lanes] = query_bias
+        late[5:6, bias_lanes] = jnp.sum(d_key.astype(single), axis=0, keepdims=True)
+        late[6:7, bias_lanes] = jnp.sum(d_value.astype(single), axis=0, keepdims=True)
 
     def first_lane(held):
         return pl.multiple_of(plus_flips(me, held) * rows // lane_rows * lane_rows, HD)
+
+    def normal_lanes(slot):
+        return pl.ds(slot * lane_rows, lane_rows)
 
     def load_tile(slot, held):
         return pltpu.make_async_copy(
             all_normed.at[:, :, pl.ds(first_lane(held), lane_rows)],
-            tiles.at[slot],
+            chances.at[:, :, normal_lanes(slot)],
             tile_sem.at[slot],
         )
 
-    def load_flow(flow):
-        return pltpu.make_async_copy(
-            flows_in.at[flow], flows.at[flow % 2], flow_sem.at[flow % 2]
-        )
-
-    for copy in loads:
-        copy.start()
+    load_joined.start()
     load_tile(0, (0,) + subsets[0]).start()
     load_tile(1, subsets[0]).start()
-    load_flow(3).start()
-    load_flow(0).start()
-    enter(
-        [(here < size - 1, {"tensor": here + 1}), (here > 0, {"tensor": here - 1})]
-        + [(jnp.bool_(True), {"dp": plus_flips(me, (bit,))}) for bit in range(bits)]
-    )
-    ending = jnp.logical_or(here == 0, here == size - 1)
-    chains = [
-        LineSum(size, parts.at[which], terms.at[which], line_send.at[which], line_recv.at[which], 1)
-        for which in range(3)
-    ]
-
-    def relay(rank):
-        for sign in (1, -1):
-            for chain in chains:
-                chain.relay(sign * chain.near, chain.far(rank, sign * chain.near))
-
-    for which in range(3):
-        loads[which].wait()
-    for rank in range(size - 1):
-        pl.when(ending)(lambda: relay(rank))
+    for step in range(1, size - 1):
+        middle(lambda: relay(3, size - 1 - step))
+
+    def spread(flow):
+        def one(index, carry):
+            lanes = pl.ds(pl.multiple_of(index * tile, tile), tile)
+            columns = []
+            for head in range(group_heads):
+                place, lane = divmod((head * 3 + flow) * HD, tile)
+                columns.append(arena[tiles_out + place, lanes, pl.ds(lane, HD)])
+            parts[flow, :, lanes] = contract_last(
+                d_pre[flow], jnp.concatenate(columns, axis=1)
+            ).astype(bfloat)
+            return carry
+
+        lax.fori_loop(0, D // tile, one, 0)
+
+        @pl.when(ending)
+        def _():
+            for rank in range(size - 1):
+                relay(flow, rank)
+
+    for index in range(tiles_out, first_up):
+        load_arena(index).wait()
+    spread(0)
 
     def own_rows(value, held):
         if lane_rows == rows:
             return value
-        work[:, 0 : value.shape[1]] = value
+        work[...] = value
         first = lax.rem(plus_flips(me, held) * rows, lane_rows)
-        return work[pl.ds(pl.multiple_of(first, 16), rows), 0 : value.shape[1]]
+        return work[pl.ds(pl.multiple_of(first, 16), rows)]
 
     def products(which, held, slot, emit):
         if which == 0:
             source = back[:, pl.ds(first_lane(held), lane_rows)]
 
             def one(index, carry):
-                first = pl.multiple_of(index * tile, tile)
-                emit(own_rows(contract_first(source, joined[:, pl.ds(first, tile)]), held), first)
+                lanes = pl.ds(pl.multiple_of(index * tile, tile), tile)
+                emit(own_rows(contract_first(source, wide[:, lanes]), held), index, 0)
                 return carry
 
-            lax.fori_loop(0, widths[0] // tile, one, 0)
+            lax.fori_loop(0, tiles_out, one, 0)
             return
-        for part in range(3):
-            value = own_rows(contract_first(tiles[slot, part], d_pre[part]), held)
-            for head in range(group_heads):
-                emit(value[:, head * HD : (head + 1) * HD], (head * 3 + part) * HD)
+        if which == 1:
+            for part in range(3):
+                value = own_rows(
+                    contract_first(chances[part, :, normal_lanes(slot)], d_pre[part]), held
+                )
+                for head in range(group_heads):
+                    place, lane = divmod((head * 3 + part) * HD, tile)
+                    emit(value[:, head * HD : (head + 1) * HD], place, lane)
+            return
 
         def one(index, carry):
-            first = pl.multiple_of(index * tile, tile)
-            value = contract_first(tiles[slot, 3], d_up[:, pl.ds(first, tile)])
-            emit(own_rows(value, held), attn_width + first)
+            lanes = pl.ds(pl.multiple_of(index * tile, tile), tile)
+            value = contract_first(chances[3, :, normal_lanes(slot)], d_up[:, lanes])
+            emit(own_rows(value, held), index, 0)
             return carry
 
         lax.fori_loop(0, units // tile, one, 0)
@@ -1375,26 +1371,27 @@
         return sum(2 ** (bit - 1) for bit in held)
 
     def pass_pair(which):
+        first, span = groups[which]
         return pltpu.make_async_remote_copy(
-            src_ref=give[which],
-            dst_ref=pair[which],
+            src_ref=give.at[pl.ds(give_first[which], span)],
+            dst_ref=arena.at[pl.ds(first, span), pl.ds(pair_first, rows)],
             send_sem=give_sem.at[which],
             recv_sem=pair_sem.at[which],
             device_id={"dp": plus_flips(me, (0,))},
             device_id_type=MESH,
         )
 
-    def kept_rows(piece, held):
-        return pl.ds(place_of(held) * rows + piece * piece_rows, piece_rows)
-
-    def land_rows(piece, landed):
-        slot = piece * (len(subsets) - 1) + place_of(landed) - 1
-        return pl.ds(slot * piece_rows, piece_rows)
+    def kept_row(piece, held):
+        return kept_first + place_of(held) * rows + piece * piece_rows
+
+    def land_row(piece, landed):
+        return land_first + (piece * last + place_of(landed) - 1) * piece_rows
 
     def cube_hop(which, piece, bit, landed):
+        tiles = pl.ds(*groups[which])
         return pltpu.make_async_remote_copy(
-            src_ref=kept[which].at[kept_rows(piece, landed)],
-            dst_ref=land[which].at[land_rows(piece, landed)],
+            src_ref=arena.at[tiles, pl.ds(kept_row(piece, landed), piece_rows)],
+            dst_ref=arena.at[tiles, pl.ds(land_row(piece, landed), piece_rows)],
             send_sem=cube_send.at[which, piece, place_of(landed)],
             recv_sem=cube_recv.at[which, piece, place_of(landed)],
             device_id={"dp": plus_flips(me, (bit,))},
@@ -1412,20 +1409,16 @@
     def add_landed(which, piece, held):
         for bit, landed in needs(piece, held):
             cube_hop(which, piece, bit, landed).wait_recv()
+        first, span = groups[which]
 
         def one(index, carry):
             def column(at, inner):
-                lanes = pl.ds(pl.multiple_of(at * tile, tile), tile)
-                spot = pl.ds(
-                    pl.multiple_of(kept_rows(piece, held).start + index * 16, 16), 16
-                )
-                value = kept[which][spot, lanes].astype(single)
+                spot = pl.ds(pl.multiple_of(kept_row(piece, held) + index * 16, 16), 16)
+                value = arena[first + at, spot].astype(single)
                 for _, landed in needs(piece, held):
-                    arrived = pl.ds(
-                        pl.multiple_of(land_rows(piece, landed).start + index * 16, 16), 16
-                    )
-                    value = value + land[which][arrived, lanes].astype(single)
-                kept[which][spot, lanes] = value.astype(bfloat)
+                    arrived = pl.ds(pl.multiple_of(land_row(piece, landed) + index * 16, 16), 16)
+                    value = value + arena[first + at, arrived].astype(single)
+                arena[first + at, spot] = value.astype(bfloat)
                 if not held:
                     value = value * value
                     value = value[0:8] + value[8:16]
@@ -1433,245 +1426,302 @@
                         inner = inner + value[:, group * HD : (group + 1) * HD]
                 return inner
 
-            return lax.fori_loop(0, widths[which] // tile, column, carry)
+            return lax.fori_loop(0, span, column, carry)
 
         found = lax.fori_loop(0, piece_rows // 16, one, jnp.zeros((8, HD), single))
         if not held:
             squares[...] += found
 
-    for copy in loads[3:]:
-        copy.wait()
-    last = len(subsets) - 1
-    for index, held in enumerate(subsets):
-        load_tile(0, (0,) + held).wait()
-        for which in range(2):
-            if index > 0:
-                pass_pair(which).wait_send()
-
-            def emit(value, first):
-                give[which][:, pl.ds(first, value.shape[1])] = value.astype(bfloat)
-
-            products(which, (0,) + held, 0, emit)
-            if index > 0:
-                pl.semaphore_wait(credit.at[which], 1)
-            pass_pair(which).start()
+    def offer(which, index):
+        held = subsets[index]
+        if index > 0:
+            pass_pair(which).wait_send()
+        else:
+            for bit in range(bits):
+                pl.semaphore_wait(ready.at[which, bit], 1)
+        if which == 1:
+            load_tile(0, (0,) + held).wait()
+
+        def emit(value, place, lane):
+            give[give_first[which] + place, :, pl.ds(lane, value.shape[1])] = value.astype(bfloat)
+
+        products(which, (0,) + held, 0, emit)
+        if index > 0:
+            pl.semaphore_wait(credit.at[which], 1)
+        pass_pair(which).start()
+        if which == 2 and index < last:
+            load_tile(0, (0,) + subsets[index + 1]).start()
+
+    def keep(which, index):
+        held = subsets[index]
+        first, _ = groups[which]
+        if which == 1:
+            load_tile(1, held).wait()
+        pass_pair(which).wait_recv()
+
+        def emit(value, place, lane):
+            lanes = pl.ds(lane, value.shape[1])
+            arena[first + place, pl.ds(kept_first + place_of(held) * rows, rows), lanes] = (
+                value + arena[first + place, pl.ds(pair_first, rows), lanes].astype(single)
+            ).astype(bfloat)
+
+        products(which, held, 1, emit)
         if index < last:
-            load_tile(0, (0,) + subsets[index + 1]).start()
-        load_tile(1, held).wait()
-        for which in range(2):
-            pass_pair(which).wait_recv()
-
-            def emit(value, first):
-                lanes = pl.ds(first, value.shape[1])
-                kept[which][pl.ds(place_of(held) * rows, rows), lanes] = (
-                    value + pair[which][:, lanes].astype(single)
-                ).astype(bfloat)
-
-            products(which, held, 1, emit)
-            if index < last:
-                pl.semaphore_signal(
-                    credit.at[which],
-                    inc=1,
-                    device_id={"dp": plus_flips(me, (0,))},
-                    device_id_type=MESH,
-                )
+            pl.semaphore_signal(
+                credit.at[which],
+                inc=1,
+                device_id={"dp": plus_flips(me, (0,))},
+                device_id_type=MESH,
+            )
+        else:
+            pass_pair(which).wait_send()
+        for piece, (_, steps) in enumerate(routes):
+            for bit, _, landed in steps[-1]:
+                if landed == held:
+                    cube_hop(which, piece, bit, landed).start()
+        if which == 2 and index < last:
+            load_tile(1, subsets[index + 1]).start()
+
+    def pass_on(which):
+        for step in range(pieces - 2, -1, -1):
             for piece, (_, steps) in enumerate(routes):
-                for bit, _, landed in steps[-1]:
-                    if landed == held:
-                        cube_hop(which, piece, bit, landed).start()
-        if index < last:
-            load_tile(1, subsets[index + 1]).start()
-
-    sums[...] = jnp.zeros_like(sums)
-
-    def descend(flow, gradient):
+                for bit, _, landed in steps[step]:
+                    add_landed(which, piece, landed)
+                    cube_hop(which, piece, bit, landed).start()
+
+    def descend(flow):
+        for place in range(chains[flow].cut):
+            chains[flow].collect(place, total)
         load_flow(flow).wait()
         gain = 2 if flow == 3 else 0
+        slot = flow % 2
 
         def one(index, carry):
             spot = pl.ds(pl.multiple_of(index * 16, 16), 16)
-            values = flows[flow % 2, spot].astype(single)
+            values = flows[slot, spot].astype(single)
             centred = values - jnp.mean(values, axis=-1, keepdims=True)
             inverse = lax.rsqrt(jnp.mean(centred * centred, axis=-1, keepdims=True) + norm_eps)
             unit = centred * inverse
-            incoming = gradient[spot]
+            incoming = total[spot]
             scaled = incoming * small[gain : gain + 1, :]
             result = inverse * (
                 scaled
                 - jnp.mean(scaled, axis=-1, keepdims=True)
                 - unit * jnp.mean(scaled * unit, axis=-1, keepdims=True)
             )
-            if flow == 3:
-                result = result + d_newest[spot]
-            d_flows[flow, spot] = result.astype(bfloat)
+            flows[slot, spot] = result.astype(bfloat)
             unit = unit * incoming
             sums[gain] += unit[0:8] + unit[8:16]
             sums[gain + 1] += incoming[0:8] + incoming[8:16]
             return carry
 
         lax.fori_loop(0, own // 16, one, 0)
-
-    descend(3, d_residual)
+        keep_flow(flow).start()
+
+    def near(flow, rank):
+        way = chains[flow].near
+        middle(lambda: chains[flow].relay(way, chains[flow].far(rank, way)))
+
+    def beyond(flow, rank):
+        way = -chains[flow].near
+        middle(lambda: chains[flow].relay(way, chains[flow].far(rank, way)))
+
+    def unit_sum(index, carry):
+        lanes = pl.ds(pl.multiple_of(index * 256, 256), 256)
+        late[pl.ds(8 + here, 1), lanes] = jnp.sum(
+            d_up[:, lanes].astype(single), axis=0, keepdims=True
+        )
+        return carry
+
+    def release():
+        push(here)
+        tell(2)
+        middle(lambda: relay(3, 0))
+
+    def closing():
+        spread(2)
+        tell(1)
+
+    between = [lambda: spread(1), closing, release]
+    load_joined.wait()
+    for index in range(last + 1):
+        offer(0, index)
+        if between:
+            between.pop(0)()
+        if index == last:
+            for action in between:
+                action()
+            offer(1, 0)
+        keep(0, index)
+        if index == 2:
+            near(0, 0)
+    offer(2, 0)
+    lax.fori_loop(0, units // 256, unit_sum, 0)
+    between = [lambda: near(0, 1), lambda: beyond(0, 0), lambda: pass_on(0)]
+    for index in range(last + 1):
+        keep(1, index)
+        if index < last:
+            offer(1, index + 1)
+        keep(2, index)
+        if index < last:
+            offer(2, index + 1)
+        if between:
+            between.pop(0)()
+    for action in between:
+        action()
+    sums[...] = jnp.zeros_like(sums)
+    for rank in range(1, size - 1):
+        if rank > 1:
+            near(0, rank)
+        beyond(0, rank)
+    near(1, 0)
+    descend(3)
+    descend(0)
+    keep_flow(3).wait()
     load_flow(1).start()
-    pl.when(jnp.logical_not(ending))(lambda: relay(0))
-    for step in range(pieces - 2, -1, -1):
-        for which in range(2):
-            for piece, (_, steps) in enumerate(routes):
-                for bit, _, landed in steps[step]:
-                    add_landed(which, piece, landed)
-                    cube_hop(which, piece, bit, landed).start()
+    near(1, 1)
+    beyond(1, 0)
+    pass_on(1)
+    pass_on(2)
     for rank in range(1, size - 1):
-        pl.when(jnp.logical_not(ending))(lambda: relay(rank))
-    for which in range(3):
-        chains[which].collect(0, total)
-        descend(which, total)
-        if which == 0:
-            load_flow(2).start()
-    norm_grads[...] = jnp.zeros_like(norm_grads)
-    for row in range(4):
-        norm_grads[row : row + 1] = jnp.sum(sums[row], axis=0, keepdims=True)
+        if rank > 1:
+            near(1, rank)
+        beyond(1, rank)
+    keep_flow(0).wait()
+    load_flow(2).start()
+    descend(1)
+    near(2, 0)
+    near(2, 1)
+    beyond(2, 0)
+    for rank in range(1, size - 1):
+        if rank > 1:
+            near(2, rank)
+        beyond(2, rank)
+    descend(2)
     squares[...] = jnp.zeros_like(squares)
     saves = []
-    for which, target in enumerate((grad_out, grad_in)):
+    for which in range(3):
         for piece in range(pieces):
             add_landed(which, piece, ())
-        saves.append(
-            pltpu.make_async_copy(kept[which].at[pl.ds(0, rows)], target, save_sem.at[which])
-        )
-        saves[-1].start()
-    for which in range(2):
-        pass_pair(which).wait_send()
+        first, span = groups[which]
+        target, offset = (grad_out, 0) if which == 0 else (grad_in, first - tiles_out)
+        for place in range(span):
+            saves.append(
+                pltpu.make_async_copy(
+                    arena.at[first + place, pl.ds(kept_first, rows)],
+                    target.at[:, pl.ds((offset + place) * tile, tile)],
+                    save_sem.at[first + place],
+                )
+            )
+            saves[-1].start()
+    for row in range(4):
+        late[row : row + 1] = jnp.sum(sums[row], axis=0, keepdims=True)
+    late[7:8, 0:HD] = jnp.sum(squares[...], axis=0, keepdims=True)
+    final.first()
+    final.second()
+    final.third()
+    final.last()
+    early.last()
+    for step in range(size):
+        for side, way in sides:
+
+            @pl.when(jnp.logical_and(has_next(way), has_origin(way, step)))
+            def _():
+                line_hop(side, way, step).wait_send()
+
+    for which in range(3):
         for piece, (_, steps) in enumerate(routes):
             for step in steps:
                 for bit, _, landed in step:
                     cube_hop(which, piece, bit, landed).wait_send()
     for chain in chains:
         chain.drain()
+    keep_flow(1).wait()
+    keep_flow(2).wait()
     for copy in saves:
         copy.wait()
 
 
-def scatter(
-    all_normed, d_normed, back, joined, d_up, d_pre, flows, small, d_residual, d_newest,
-    size, count, identity,
+def backward(
+    d_branch, early_grads, rope, all_in, all_out, slope, heads, chances, joined, all_normed,
+    flows, small, size, count, identity,
 ):
-    own = flows.shape[1]
+    own = d_branch.shape[0]
     length = own * size
     rows = D // count
     lane_rows = max(rows, HD)
-    head_width = d_pre.shape[2]
-    width_out = joined.shape[1]
-    width_in = 3 * head_width + d_up.shape[1]
+    tile = 512
+    head_width, units = heads.shape[2], slope.shape[1]
+    width_in, width_out = all_in.shape[1], all_out.shape[1]
+    tiles = (width_in + width_out) // tile
     pieces = count.bit_length() - 2
     held = 2**pieces
+    bits = pieces + 1
+    late_rows = 16
     low = lambda *shape: jax.ShapeDtypeStruct(shape, bfloat)
     wide = lambda *shape: jax.ShapeDtypeStruct(shape, single)
     hbm = pl.BlockSpec(memory_space=pl.ANY)
     vmem = pl.BlockSpec(memory_space=pltpu.VMEM)
-    landed = pieces * (held - 1) * (rows // pieces)
+    dma = pltpu.SemaphoreType.DMA
+    rope = rope.reshape(3, size, own, HD).transpose(2, 0, 1, 3).reshape(own, -1)
     return pl.pallas_call(
-        lambda *refs: scatter_kernel(size, count, *refs),
+        lambda *refs: backward_kernel(size, count, *refs),
         out_shape=[
             low(rows, width_in),
             low(rows, width_out),
             low(STREAMS, own, D),
-            wide(8, D),
-            wide(8, HD),
+            wide(*early_grads.shape),
+            wide(late_rows, D),
         ],
-        in_specs=[hbm] * 7 + [vmem] * 3,
-        out_specs=[hbm] * 2 + [vmem] * 3,
+        in_specs=[hbm, vmem] + [hbm] * 9 + [vmem],
+        out_specs=[hbm] * 3 + [vmem] * 2,
         scratch_shapes=[
-            pltpu.VMEM(back.shape, bfloat),
-            pltpu.VMEM(joined.shape, bfloat),
-            pltpu.VMEM(d_up.shape, bfloat),
-            pltpu.VMEM(d_pre.shape, bfloat),
-            pltpu.VMEM((2, STREAMS, length, lane_rows), bfloat),
-            pltpu.VMEM((held * rows, width_in), bfloat),
-            pltpu.VMEM((held * rows, width_out), bfloat),
-            pltpu.VMEM((rows, width_in), bfloat),
-            pltpu.VMEM((rows, width_out), bfloat),
-            pltpu.VMEM((rows, width_in), bfloat),
-            pltpu.VMEM((rows, width_out), bfloat),
-            pltpu.VMEM((landed, width_in), bfloat),
-            pltpu.VMEM((landed, width_out), bfloat),
-            pltpu.VMEM((3, length, D), bfloat),
-            pltpu.VMEM((3, size + 1, own, D), bfloat),
+            pltpu.VMEM((tiles, D, tile), bfloat),
+            pltpu.VMEM(((width_out + 3 * head_width) // tile, rows, tile), bfloat),
+            pltpu.VMEM((length, width_out), bfloat),
+            pltpu.VMEM(heads.shape, bfloat),
+            pltpu.VMEM(chances.shape, bfloat),
+            pltpu.VMEM((length, D), bfloat),
+            pltpu.VMEM((length, units), bfloat),
+            pltpu.VMEM((3, length, head_width), bfloat),
+            pltpu.VMEM((STREAMS, length, D), bfloat),
+            pltpu.VMEM((STREAMS, size + 1, own, D), bfloat),
             pltpu.VMEM((2, own, D), bfloat),
             pltpu.VMEM((own, D), single),
             pltpu.VMEM((4, 8, D), single),
-            pltpu.VMEM((lane_rows if lane_rows > rows else 8, 512), single),
-            pltpu.SemaphoreType.DMA((7,)),
-            pltpu.SemaphoreType.DMA((2,)),
-            pltpu.SemaphoreType.DMA((2,)),
-            pltpu.SemaphoreType.DMA((2,)),
-            pltpu.SemaphoreType.DMA((2,)),
-            pltpu.SemaphoreType.REGULAR((2,)),
-            pltpu.SemaphoreType.DMA((2, pieces, held)),
-            pltpu.SemaphoreType.DMA((2, pieces, held)),
-            pltpu.SemaphoreType.DMA((3, 2, size, 1)),
-            pltpu.SemaphoreType.DMA((3, 2, size, 1)),
-            pltpu.SemaphoreType.DMA((2,)),
-        ],
+            pltpu.VMEM((lane_rows, tile) if lane_rows > rows else (8, HD), single),
+            pltpu.VMEM((late_rows, D), single),
+            pltpu.VMEM((8, HD), single),
+            dma((tiles,)),
+            dma((6,)),
+            dma((2,)),
+            dma((2,)),
+            dma((2,)),
+            dma((tiles,)),
+            dma((2, size)),
+            dma((2, size)),
+            dma((STREAMS, 2, size, CUT)),
+            dma((STREAMS, 2, size, CUT)),
+            dma((3,)),
+            dma((3,)),
+            pltpu.SemaphoreType.REGULAR((3,)),
+            pltpu.SemaphoreType.REGULAR((3, bits)),
+            dma((3, pieces, held)),
+            dma((3, pieces, held)),
+        ]
+        + flat_scratch(early_grads.shape[0], count, size)
+        + flat_scratch(late_rows, count, size),
         compiler_params=pltpu.CompilerParams(
-            collective_id=identity, has_side_effects=True, vmem_limit_bytes=63 * 2**20
+            collective_id=identity, has_side_effects=True, vmem_limit_bytes=64 * 2**20 - 2**19
         ),
-        name="scatter_%d" % identity,
-    )(all_normed, d_normed, back, joined, d_up, d_pre, flows, small, d_residual, d_newest)
-
-
-def small_sum_kernel(
-    bits,
-    norm_grads,
-    row_grads,
-    bias_grads,
-    mix_in_grad,
-    mix_out_grad,
-    squares,
-    out,
-    value,
-    total,
-    landing,
-    send_a,
-    recv_a,
-    send_b,
-    recv_b,
-):
-    here = lax.axis_index("tensor")
-    value[...] = jnp.zeros_like(value)
-    width = HEADS // lax.axis_size("tensor") * HD
-    value[0:4] = norm_grads[0:4]
-    value[4:5] = row_grads[0:1]
-    lanes = pl.ds(pl.multiple_of(here * width, HD), width)
-    value[5:8, lanes] = bias_grads[0:3, 0:width]
-    value[8:9] = row_grads[1:2]
-    value[9:10] = row_grads[1:2]
-    value[pl.ds(10 + here, 1), :] = bias_grads[3:4]
-    value[SMALL_MIX : SMALL_MIX + MIXH] = mix_in_grad[0:MIXH]
-    for place in range(5):
-        value[56:64, place * HD : (place + 1) * HD] = mix_out_grad[place * 8 : place * 8 + 8]
-    value[56:64, 5 * HD : 6 * HD] = squares[...]
-    cube_sum_steps(bits, value, out, total, landing, send_a, recv_a, send_b, recv_b)
-
-
-def small_sum(parts, bits, identity):
-    steps = len(bits)
-    vmem = pl.BlockSpec(memory_space=pltpu.VMEM)
-    return pl.pallas_call(
-        lambda *refs: small_sum_kernel(bits, *refs),
-        out_shape=jax.ShapeDtypeStruct((64, D), single),
-        in_specs=[vmem] * 6,
-        out_specs=vmem,
-        scratch_shapes=[pltpu.VMEM((64, D), single)] * 2
-        + [pltpu.VMEM((steps, 32, D), single)]
-        + [pltpu.SemaphoreType.DMA((steps,))] * 4,
-        compiler_params=pltpu.CompilerParams(
-            collective_id=identity, has_side_effects=True, vmem_limit_bytes=8 * 2**20
-        ),
-        name="small_sum_%d" % identity,
-    )(*parts)
-
-
-def finish_kernel(grad_in, grad_out, sums, weights, newest, stored, cotangent, d_flows, *refs):
+        name="backward_%d" % identity,
+    )(
+        d_branch, early_grads, jnp.asarray(rope), all_in, all_out, slope, heads, chances, joined,
+        all_normed, flows, small,
+    )
+
+
+def finish_kernel(grad_in, grad_out, sums, early_sums, weights, newest, d_newest, stored, cotangent, d_flows, *refs):
     states, refs = (refs[0:4], refs[4:8]), refs[8:]
     small, mix, refs = refs[0:4], refs[4:8], refs[8:]
     norm_out, refs = refs[0], refs[1:]
@@ -1679,7 +1729,7 @@
     new_small, new_mix, refs = refs[0:4], refs[4:8], refs[8:]
     out_streams, grad_streams, grad_stored, refs = refs[0], refs[1], refs[2], refs[3:]
     held, refs = (refs[0:2], refs[2:4], refs[4:6]), refs[6:]
-    tiles_in, tiles_out, spread, passed, grad_sem, load_sem, save_sem, tile_load, tile_save, pass_sem = refs
+    tiles_in, tiles_out, spread, passed, small_sums, grad_sem, load_sem, save_sem, tile_load, tile_save, pass_sem = refs
     grads = (grad_in, grad_out)
     parts = load_sem.shape[2]
     rows = grad_in.shape[0]
@@ -1770,16 +1820,23 @@
     take_flows = pltpu.make_async_copy(d_flows, passed, pass_sem.at[0])
     give_flows = pltpu.make_async_copy(passed, grad_streams, pass_sem.at[1])
     take_flows.start()
-    small_total = sums[0 : small[0].shape[0]]
+    small_sums[0:4] = sums[0:4]
+    small_sums[4:5] = early_sums[MIXH : MIXH + 1]
+    small_sums[5:8] = sums[4:7]
+    small_sums[8:9] = early_sums[MIXH + 1 : MIXH + 2]
+    small_sums[9:10] = early_sums[MIXH + 1 : MIXH + 2]
+    small_sums[10:SMALL_MIX] = sums[8 : 8 + SMALL_MIX - 10]
+    small_sums[SMALL_MIX : SMALL_MIX + MIXH] = early_sums[0:MIXH]
+    small_total = small_sums[...]
     mix_total = jnp.concatenate(
-        [sums[56:64, place * HD : (place + 1) * HD] for place in range(5)], axis=0
+        [early_sums[40:48, place * HD : (place + 1) * HD] for place in range(5)], axis=0
     )[0 : mix[0].shape[0], 0 : mix[0].shape[1]]
 
     def whole_sum(values):
         return jnp.sum(jnp.sum(values, axis=1, keepdims=True), axis=0, keepdims=True)
 
     norm = jnp.sqrt(
-        whole_sum(sums[56:64, 5 * HD : 6 * HD])
+        whole_sum(sums[7:8, 0:HD])
         + whole_sum(small_total * small_total)
         + whole_sum(mix_total * mix_total)
     )
@@ -1794,6 +1851,13 @@
     ):
         target[...] = result
     take_flows.wait()
+
+    def add_residual(index, carry):
+        spot = pl.ds(pl.multiple_of(index * 16, 16), 16)
+        passed[3, spot] = (passed[3, spot].astype(single) + d_newest[spot]).astype(bfloat)
+        return carry
+
+    lax.fori_loop(0, own // 16, add_residual, 0)
     give_flows.start()
     tiles_done = 0
     for which in range(2):
@@ -1841,7 +1905,7 @@
 
 
 def finish(
-    grads, sums, weights, newest, stored, cotangent, d_flows, in_states, out_states, small, mix
+    grads, sums, early_sums, weights, newest, d_newest, stored, cotangent, d_flows, in_states, out_states, small, mix
 ):
     wide = lambda shape: jax.ShapeDtypeStruct(shape, single)
     low = lambda shape: jax.ShapeDtypeStruct(shape, bfloat)
@@ -1857,13 +1921,14 @@
         + [wide(small[0].shape)] * 4
         + [wide(mix[0].shape)] * 4
         + [low(cotangent.shape), low(d_flows.shape), low(stored.shape)],
-        in_specs=[hbm] * 2 + [vmem] * 3 + [hbm] * 3 + [hbm] * 8 + [vmem] * 8,
+        in_specs=[hbm] * 2 + [vmem] * 5 + [hbm] * 3 + [hbm] * 8 + [vmem] * 8,
         out_specs=[vmem] + [hbm] * 10 + [vmem] * 8 + [hbm] * 3,
         scratch_shapes=[pltpu.VMEM(shape, grads[0].dtype) for shape in shapes]
         + [pltpu.VMEM((4,) + shape, single) for shape in shapes]
         + [pltpu.VMEM(shape, bfloat) for shape in shapes]
         + [pltpu.VMEM(tile, bfloat)] * 2
         + [pltpu.VMEM((MIXH, tile[2], HD), single), pltpu.VMEM(d_flows.shape, bfloat)]
+        + [pltpu.VMEM(small[0].shape, single)]
         + [
             pltpu.SemaphoreType.DMA((2,)),
             pltpu.SemaphoreType.DMA((2, 4, parts)),
@@ -1875,7 +1940,7 @@
         compiler_params=pltpu.CompilerParams(vmem_limit_bytes=60 * 2**20),
         name="finish",
     )(
-        *grads, sums, weights, newest, stored, cotangent, d_flows,
+        *grads, sums, early_sums, weights, newest, d_newest, stored, cotangent, d_flows,
         *in_states, *out_states, *small, *mix,
     )
 
@@ -1902,7 +1967,7 @@
     mix_average,
 ):
     groups, count = lax.axis_size("tensor"), lax.axis_size("dp")
-    rope = jnp.asarray(rope_lanes(in_streams.shape[1] * groups))
+    rope = rope_lanes(in_streams.shape[1] * groups)
     (
         full_in,
         full_out,
@@ -1915,9 +1980,7 @@
         d_newest,
         d_branch,
         weights,
-        row_grads,
-        mix_in_grad,
-        mix_out_grad,
+        early_grads,
     ) = forward(
         in_streams,
         in_weights,
@@ -1931,34 +1994,30 @@
         count,
         0,
     )
-    branch_grads, d_up, d_pre, d_normed, d_residual, bias_grads = backward(
-        d_branch, rope, full_in, full_out, slope, heads, chances, groups, 1
-    )
-    grad_in, grad_out, d_flows, norm_grads, squares = scatter(
+    grad_in, grad_out, d_flows, early_sums, sums = backward(
+        d_branch,
+        early_grads,
+        rope,
+        full_in,
+        full_out,
+        slope,
+        heads,
+        chances,
+        joined,
         normed,
-        d_normed,
-        branch_grads,
-        joined,
-        d_up,
-        d_pre,
         in_streams,
         small_params,
-        d_residual,
-        d_newest,
         groups,
         count,
-        2,
-    )
-    sums = small_sum(
-        (norm_grads, row_grads, bias_grads, mix_in_grad, mix_out_grad, squares),
-        axis_bits("dp") + axis_bits("tensor"),
-        3,
+        1,
     )
     results = finish(
         (grad_in, grad_out),
         sums,
+        early_sums,
         weights,
         newest,
+        d_newest,
         stored,
         cotangent,
         d_flows,

time: 460 us -> 409 us (0.89)
  Pallas kernels: 448 us -> 404 us
    pallas_call x3 -> x1, Pallas kernels: 238 us -> 206 us  [backward(): pl.pallas_call(lambda *refs: backward_kernel(size, count, *refs), out_sha...]
    pallas_call x1, Pallas kernels: 178 us -> 166 us  [forward(): pl.pallas_call(lambda *refs: forward_kernel(size, count, *refs), out_shap...]
where the time goes in v4:
time: 409 us; the launch traced here: 405 us
  Pallas kernels  404 us (99%)
    pallas_call x1, Pallas kernels, backward(): pl.pallas_call(lambda *refs: backward_kernel(size, count, *refs), out_sha...  206 us
    pallas_call x1, Pallas kernels, forward(): pl.pallas_call(lambda *refs: forward_kernel(size, count, *refs), out_shap...  166 us
    pallas_call x1, Pallas kernels, finish(): pl.pallas_call(finish_kernel, out_shape=[wide((1, 1))] + [entry for shape...  32.4 us

profile of v4, /device:TPU:0, one launch (start us, length us, event | category | flops | bytes accessed | tf_op | source)
XLA Modules:
  0.0 404.6 jit_solution(11547682519986351151)
XLA Ops:
  0.7 165.8 %forward_0.1 = (bf16[2048,3584]{1,0:T(8,128)(2,1)}, bf16[2048,2560]{1,0:T(8,128)(2,1)}, bf16[4,512,2048]{2,1,0:T(8,128)(2,1)}, bf16[512,2560]{1,0:T(8,128)(2,1)}...) custom-call(bf16[4,128,2048]{2,1,0:T(8,128)(2,1)} %refs_10_.2, ...), custom_call_target="tpu_custom_call" | custom-call | tf_op jit(solution)/shard_map/forward_0/pallas_call | solution.py:928
  166.5 205.5 %backward_1.1 = (bf16[256,3584]{1,0:T(8,128)(2,1)}, bf16[256,2560]{1,0:T(8,128)(2,1)}, bf16[4,128,2048]{2,1,0:T(8,128)(2,1)}, f32[48,2048]{1,0:T(8,128)}, f32[16,2048]{1,0:T(8,128)}) custom-call(bf16[128,2048]{1,0:T(8,128)(2,1)} %get-tuple-element.61.refs_0_, f32[48,2048]{1,0:T(8,128)} %get-tuple-element.62.refs_1_, f32[128,1536]{1,0:T(8,128)} %constant.5.clone.refs_2_, ...), custom_call_target="tpu_custom_call" | custom-call | tf_op jit(solution)/shard_map/backward_1/pallas_call | solution.py:1667
  372.0 32.4 %finish.1 = (f32[1,1]{1,0:T(1,128)}, f32[256,3584]{1,0:T(8,128)}, f32[256,3584]{1,0:T(8,128)}, f32[256,3584]{1,0:T(8,128)}, f32[256,3584]{1,0:T(8,128)}, /*index...) custom-call(bf16[256,3584]{1,0:T(8,128)(2,1)} %get-tuple-element.70., ...), custom_call_target="tpu_custom_call" | custom-call | tf_op jit(solution)/shard_map/finish/pallas_call | solution.py:1917
